TPU v7x, 256 devices: a whole 4x4x8 slice. The times are simulated.
256 devices in a mesh: gz: 32 (over y, z_hi, core), ch: 8 (over x, z_lo).
Axes of the slice: x: 4, y: 4, z: 8 (z_hi: 4, z_lo: 2; z = z_hi * 2 + z_lo), core: 2. Of those that a mesh axis runs over, the one named last changes fastest.
Arguments:
- volume: bfloat16 [16, 256, 64, 128], P(None, 'gz', 'ch'), may hold values from -6 to 6
- filters_two: bfloat16 [32, 16, 3, 3, 3], replicated, may hold values from -0.3125 to 0.3125
- filters_three: bfloat16 [64, 32, 3, 3, 3], P(None, 'ch'), may hold values from -0.21875 to 0.21875
- filters_four: bfloat16 [128, 64, 3, 3, 3], P(None, 'ch'), may hold values from -0.15625 to 0.15625
- cotangent: bfloat16 [128, 32, 8, 16], P('ch', 'gz'), may hold values from -6 to 6
Outputs:
- pooled_four: bfloat16 [128, 32, 8, 16], P('ch', 'gz')
- grad_two: float32 [32, 16, 3, 3, 3], replicated
- grad_three: float32 [64, 32, 3, 3, 3], P(None, 'ch')
- grad_four: float32 [128, 64, 3, 3, 3], P(None, 'ch')
All inputs are finite; a program needn't handle non-finite values.
Results may differ from a plain program's by a relative error of at most 0.025.
Values may be sent and summed in bfloat16 or wider, within the bound.
No kernel may reach another device: no remote copies, remote signals or barrier semaphores. Data moves between devices by JAX's collectives and lax.ppermute only.
A program may use at most 128 MiB of HBM per device.

v0:
```python
import jax
import jax.numpy as jnp
from jax import lax
from jax.sharding import PartitionSpec as P


def extended(block, sides, width):
    for axis, dim in sides:
        count = lax.axis_size(axis)
        forward = [(i, i + 1) for i in range(count - 1)]
        backward = [(target, source) for source, target in forward]
        low = lax.ppermute(
            lax.slice_in_dim(block, block.shape[dim] - width, None, axis=dim), axis, forward
        )
        high = lax.ppermute(lax.slice_in_dim(block, 0, width, axis=dim), axis, backward)
        block = jnp.concatenate([low, block, high], axis=dim)
    return block


def activate(values):
    return 0.3 * values + 0.7 * values * jax.nn.sigmoid(values)


def slope_at(values):
    logistic = jax.nn.sigmoid(values)
    return 0.3 + 0.7 * (logistic + values * logistic * (1.0 - logistic))


def average_pool(values):
    c, z, y, x = values.shape
    return values.reshape(c, z // 2, 2, y // 2, 2, x // 2, 2).sum(axis=(2, 4, 6)) * 0.125


def spread_back(values):
    c, z, y, x = values.shape
    wide = jnp.broadcast_to(values[:, :, None, :, None, :, None], (c, z, 2, y, 2, x, 2))
    return wide.reshape(c, 2 * z, 2 * y, 2 * x) * 0.125


def conv_apply(field, filters, margins):
    return lax.conv_general_dilated(
        field[None],
        filters,
        (1, 1, 1),
        margins,
        dimension_numbers=("NCDHW", "OIDHW", "NCDHW"),
        preferred_element_type=jnp.float32,
    )[0]


def filter_grad(field, delta, margins):
    return lax.conv_general_dilated(
        field[None],
        delta[None],
        (1, 1, 1),
        margins,
        dimension_numbers=("CNDHW", "IODHW", "CNDHW"),
        preferred_element_type=jnp.float32,
    )


def flip_filter(filters):
    return jnp.flip(filters, (2, 3, 4)).transpose(1, 0, 2, 3, 4)


def channel_back(delta, held, filters, margins):
    rimmed = extended(delta, (("gz", 1),), 1)
    turned = flip_filter(filters)
    start_back = jnp.zeros((filters.shape[1],) + delta.shape[1:], jnp.float32)
    start_grad = jnp.zeros(filters.shape, jnp.float32)
    shard_piece = lax.all_gather(rimmed, "ch", axis=0, tiled=True)
    first_row = jnp.int32(0)
    back_sum = start_back
    grad_sum = start_grad
    piece_rows = shard_piece.shape[0]
    part_filters = lax.dynamic_slice_in_dim(turned, first_row, piece_rows, 1)
    back_sum = back_sum + conv_apply(shard_piece, part_filters, margins)
    piece_grad = filter_grad(held, shard_piece[:, 1:-1], margins)
    grad_sum = lax.dynamic_update_slice_in_dim(grad_sum, piece_grad, first_row, 0)
    return (back_sum, grad_sum)


def body(volume, filters_two, filters_three, filters_four, cotangent):
    x_margin = ((0, 0), (0, 0), (1, 1))
    yx_margin = ((0, 0), (1, 1), (1, 1))
    held_two = extended(volume, (("gz", 1), ("ch", 2)), 1)
    pre_two = conv_apply(held_two, filters_two, x_margin)
    pooled_two = average_pool(activate(pre_two)).astype(jnp.bfloat16)
    local_three = lax.all_to_all(pooled_two, "ch", split_axis=0, concat_axis=2, tiled=True)
    held_three = extended(local_three, (("gz", 1),), 1)
    part_filters = filters_three
    pre_three = lax.psum_scatter(
        conv_apply(held_three, part_filters, yx_margin).astype(jnp.bfloat16),
        "ch",
        scatter_dimension=0,
        tiled=True,
    ).astype(jnp.float32)
    pooled_three = average_pool(activate(pre_three)).astype(jnp.bfloat16)
    held_four = extended(pooled_three, (("gz", 1),), 1)
    part_filters = filters_four
    pre_four = lax.psum_scatter(
        conv_apply(held_four, part_filters, yx_margin).astype(jnp.bfloat16),
        "ch",
        scatter_dimension=0,
        tiled=True,
    ).astype(jnp.float32)
    pooled_four = average_pool(activate(pre_four)).astype(jnp.bfloat16)
    delta_four = (spread_back(cotangent.astype(jnp.float32)) * slope_at(pre_four)).astype(
        jnp.bfloat16
    )
    back_four, grads_four = channel_back(delta_four, held_four, filters_four, yx_margin)
    grads_four = lax.psum(grads_four.astype(jnp.bfloat16), "gz").astype(jnp.float32)
    back_four = back_four.astype(jnp.bfloat16)
    delta_three = (spread_back(back_four.astype(jnp.float32)) * slope_at(pre_three)).astype(
        jnp.bfloat16
    )
    back_local, grads_three = channel_back(delta_three, held_three, filters_three, yx_margin)
    back_three = lax.all_to_all(
        back_local.astype(jnp.bfloat16), "ch", split_axis=2, concat_axis=0, tiled=True
    )
    grads_three = lax.psum(grads_three, "gz")
    delta_two = (spread_back(back_three.astype(jnp.float32)) * slope_at(pre_two)).astype(
        jnp.bfloat16
    )
    grads_two = lax.psum(filter_grad(held_two, delta_two, x_margin), ("gz", "ch"))
    return (pooled_four, grads_two, grads_three, grads_four)


def solution(mesh):
    in_specs = (
        P(None, "gz", "ch", None),
        P(),
        P(None, "ch", None, None, None),
        P(None, "ch", None, None, None),
        P("ch", "gz", None, None),
    )
    out_specs = (
        P("ch", "gz", None, None),
        P(),
        P(None, "ch", None, None, None),
        P(None, "ch", None, None, None),
    )
    return jax.shard_map(body, mesh=mesh, in_specs=in_specs, out_specs=out_specs, check_vma=False)
```

profile of v0, /device:TPU:1, one launch (start us, length us, event | category | flops | bytes accessed | tf_op | source)
XLA Modules:
  0.0 985.4 jit_solution(13116458150061177906)
XLA Ops:
  8.0 6.3 collective-permute-start
  14.3 1.9 collective-permute-start.1
  17.4 3.0 collective-permute-done.1
  20.5 3.5 collective-permute-start.2
  25.3 3.4 collective-permute-done.3
  30.8 3.8 reshape.93
  34.6 6.5 copy.302
  42.3 11.0 %multiply_add_fusion = (f32[8,8,8,17,32]{4,2,3,1,0:T(8,128)}, f32[8,8,8,17,32]{4,2,3,1,0:T(8,128)S(1)}, f32[8,8,8,17,32]{4,2,3,1,0:T(8,128)S(1)}, f32[8,8,8,17,32]{4,2,3,1,0:T(8,128)S(1)}) fusion(pred[8,17]{0,1:T(8,128)(4,1)S(1)} %copy-done.9, bf16[32,16,3,3,3]{0,1,4,3,2:T(8,128)(2,1)S(1)} %copy-done, bf16[16,10,10,1,7,2]{0,4,5,2,1,3:T(8,128)(2,1)S(1)} %slice.73, ...), kind=kOutput, calls=%fused_computation.5 | convolution fusion | flops 245449728 | bytes 4964232 | tf_op jit(solution)/shard_map/conv_general_dilated | solution.py:41
  55.7 2.6 fusion.12
  58.3 5.2 reduce_sum.34
  64.0 10.1 %all_to_all.27 = bf16[8,2,2048]{2,1,0:T(2,128)(2,1)S(1)} all-to-all(bf16[8,2,2048]{2,1,0:T(2,128)(2,1)S(1)} %reshape.162), channel_id=1, replica_groups=mesh['gz'=32,'ch'=8] {'ch'}, dimensions={0} | all-to-all | bytes 131072 | tf_op jit(solution)/shard_map/all_to_all | solution.py:89
  74.4 6.2 collective-permute-start.4
  80.6 1.9 collective-permute-start.5
  82.6 4.5 collective-permute-done.5
  89.0 10.2 %select_convert_fusion = bf16[4,32,8,9,64]{4,2,3,1,0:T(8,128)(2,1)S(1)} fusion(pred[8,9]{0,1:T(8,128)(4,1)S(1)} %copy-done.5, bf16[64,4,3,3,3]{0,1,4,3,2:T(4,128)(2,1)S(1)} %copy-done.8, bf16[4,6,32,1,7,2]{4,0,5,2,1,3:T(4,128)(2,1)S(1)} %slice.79, bf16[4,6,32,1,8,9]{4,0,5,2,1,3:T(4,128)(2,1)S(1)} %copy.312), kind=kOutput, calls=%fused_computation.4 | convolution fusion | flops 126332928 | bytes 1325640 | tf_op jit(solution)/shard_map/conv_general_dilated | solution.py:41
  100.1 5.0 copy.314
  105.1 53.9 %reduce-scatter.3.cloned.1.call-done = bf16[8,4,32,64]{3,2,1,0:T(8,128)(2,1)} async-done(((bf16[64,4,32,64]{3,2,1,0:T(8,128)(2,1)}), bf16[8,4,32,64]{3,2,1,0:T(8,128)(2,1)}) %reduce-scatter.3.cloned.1.call-update) | async-done | bytes 131088 | tf_op jit(solution)/shard_map/reduce_scatter | solution.py:92
  160.2 3.1 copy.315
  163.3 4.9 reduce_sum.35
  168.6 4.9 collective-permute-start.6
  173.5 1.9 collective-permute-start.7
  176.7 4.5 collective-permute-done.7
  184.1 2.4 copy.321
  187.0 37.1 %reduce-scatter.5.cloned.1.call-done = bf16[16,2,16,32]{3,2,1,0:T(8,128)(2,1)} async-done(((bf16[128,2,16,32]{3,2,1,0:T(8,128)(2,1)}), bf16[16,2,16,32]{3,2,1,0:T(8,128)(2,1)}) %reduce-scatter.5.cloned.1.call-update) | async-done | bytes 32784 | tf_op jit(solution)/shard_map/reduce_scatter | solution.py:101
  225.2 9.6 collective-permute-start.8
  236.8 4.5 collective-permute-done.9
  241.4 41.3 %all_gather.6 = bf16[128,4,16,32]{3,2,1,0:T(8,128)(2,1)S(1)} all-gather(bf16[16,4,16,32]{3,2,1,0:T(8,128)(2,1)S(1)} %pad_maximum_fusion.3), channel_id=1, replica_groups=mesh['gz'=32,'ch'=8] {'ch'}, dimensions={0}, use_global_device_ids=true | all-gather | bytes 589824 | tf_op jit(solution)/shard_map/all_gather | solution.py:71
  282.7 2.6 copy.326
  285.7 2.4 fusion.40
  289.1 4.1 broadcast_in_dim.51
  293.2 2.9 copy.331
  296.3 3.3 collective-permute-start.10
  301.6 5.2 collective-permute-done.11
  307.6 5.1 copy.341
  312.7 10.1 %copy.342 = bf16[1,16,10,10,128]{1,0,4,3,2:T(2,128)(2,1)} copy(bf16[1,16,10,10,128]{4,1,3,2,0:T(8,128)(2,1)S(1)} %copy-done.2) | data formatting | bytes 819200 | tf_op jit(solution)/shard_map/broadcast_in_dim | solution.py:42
  322.9 11.1 %copy.344 = bf16[1,4,6,32,64]{1,0,4,3,2:T(2,128)(2,1)} copy(bf16[1,4,6,32,64]{4,3,2,1,0:T(8,128)(2,1)S(1)} %get-tuple-element.40) | data formatting | bytes 196608 | tf_op jit(solution)/shard_map/broadcast_in_dim | solution.py:42
  336.3 7.0 convolution_convert_fusion
  343.3 132.9 %psum.23 = bf16[128,8,3,3,3]{0,1,4,3,2:T(8,128)(2,1)S(1)} all-reduce(bf16[128,8,3,3,3]{0,1,4,3,2:T(8,128)(2,1)S(1)} %convolution_convert_fusion), channel_id=1, replica_groups=mesh['gz'=32,'ch'=8] {'gz'}, use_global_device_ids=true, to_apply=%region_8.9 | all-reduce | flops 27648 | bytes 110592 | tf_op jit(solution)/shard_map/psum | solution.py:112
  476.9 2.0 slice_bitcast_fusion.1
  478.8 7.6 copy.345
  486.5 5.7 copy.332
  494.4 145.3 %fusion.4 = bf16[4,32,8,9,4]{2,4,3,1,0:T(4,128)(2,1)S(1)} fusion(bf16[64,4,3,3,3]{0,1,4,3,2:T(4,128)(2,1)S(1)} %copy-done.8, bf16[64,6,32,1,7,2]{0,4,5,2,1,3:T(8,128)(2,1)S(1)} %slice.91, bf16[64,6,32,1,8,9]{0,4,5,2,1,3:T(8,128)(2,1)S(1)} %copy.334), kind=kOutput, calls=%fused_computation.9 | convolution fusion | flops 131235840 | bytes 2201088 | tf_op jit(solution)/shard_map/conv_general_dilated | solution.py:41
  641.7 3.6 all-to-all-start.1
  645.3 56.3 %fusion.106 = f32[64,4,3,3,3]{0,1,4,3,2:T(4,128)S(1)} fusion(bf16[1,4,6,32,64]{1,0,4,3,2:T(2,128)(2,1)} %copy.344, bf16[1,64,4,32,64]{1,0,4,3,2:T(2,128)(2,1)} %copy.345), kind=kOutput, calls=%fused_computation.142 | convolution fusion | flops 109731840 | bytes 1174528 | tf_op jit(solution)/shard_map/conv_general_dilated | solution.py:52
  701.6 138.7 %psum.22 = f32[64,4,3,3,3]{0,1,4,3,2:T(4,128)} all-reduce(f32[64,4,3,3,3]{0,1,4,3,2:T(4,128)S(1)} %fusion.106), channel_id=1, replica_groups=mesh['gz'=32,'ch'=8] {'gz'}, use_global_device_ids=true, to_apply=%region_7.8 | all-reduce | flops 6912 | bytes 55296 | tf_op jit(solution)/shard_map/psum | solution.py:121
  842.0 3.1 fusion.11
  845.5 50.9 %fusion.13 = f32[32,16,3,3,3]{0,1,4,3,2:T(8,128)S(1)} fusion(bf16[1,16,10,10,128]{1,0,4,3,2:T(2,128)(2,1)S(1)} %bitcast.116, bf16[1,32,8,8,128]{1,3,4,2,0:T(8,128)(2,1)S(1)} %fusion.11), kind=kOutput, calls=%fused_computation.20 | convolution fusion | flops 225312768 | bytes 989184 | tf_op jit(solution)/shard_map/conv_general_dilated | solution.py:52
  896.5 82.1 %psum.21 = f32[32,16,3,3,3]{0,1,4,3,2:T(8,128)} all-reduce(f32[32,16,3,3,3]{0,1,4,3,2:T(8,128)S(1)} %fusion.13), channel_id=1, replica_groups=mesh['gz'=32,'ch'=8] {'gz','ch'}, use_global_device_ids=true, to_apply=%region_6.7 | all-reduce | flops 13824 | bytes 110592 | tf_op jit(solution)/shard_map/psum | solution.py:125
  (120 shorter events, 35.0 us)
Async XLA Ops:
  7.2 35.1 %copy-start = (bf16[32,16,3,3,3]{0,1,4,3,2:T(8,128)(2,1)S(1)}, bf16[32,16,3,3,3]{0,1,4,3,2:T(8,128)(2,1)}, u32[]{:S(2)}) copy-start(bf16[32,16,3,3,3]{0,1,4,3,2:T(8,128)(2,1)} %param.6) | copy-start | bytes 82948
  7.2 151.9 %reduce-scatter.3.cloned.1.call-start = ((), (), s32[]{:S(2)}) async-start(), calls=%async_computation.4 | async-start | bytes 2359296 | tf_op jit(solution)/shard_map/reduce_scatter | solution.py:92
  8.0 8.2 collective-permute-start
  14.3 6.1 collective-permute-start.1
  20.5 4.9 collective-permute-start.2
  24.0 4.7 collective-permute-start.3
  34.6 7.7 copy-start.9
  63.6 25.5 %copy-start.5 = (pred[8,9]{0,1:T(8,128)(4,1)S(1)}, pred[8,9]{0,1:T(8,128)(4,1)}, u32[]{:S(2)}) copy-start(pred[8,9]{0,1:T(8,128)(4,1)} %constant.45) | copy-start | bytes 220
  63.6 25.5 %copy-start.8 = (bf16[64,4,3,3,3]{0,1,4,3,2:T(4,128)(2,1)S(1)}, bf16[64,4,3,3,3]{0,1,4,3,2:T(4,128)(2,1)}, u32[]{:S(2)}) copy-start(bf16[64,4,3,3,3]{0,1,4,3,2:T(4,128)(2,1)} %param.7) | copy-start | bytes 41476
  74.4 8.2 collective-permute-start.4
  80.6 6.5 collective-permute-start.5
  105.1 119.0 %reduce-scatter.5.cloned.1.call-start = ((), (), s32[]{:S(2)}) async-start(), calls=%async_computation.5 | async-start | bytes 1179648 | tf_op jit(solution)/shard_map/reduce_scatter | solution.py:101
  163.3 19.2 %copy-start.7 = (bf16[128,8,3,3,3]{0,1,4,3,2:T(8,128)(2,1)S(1)}, bf16[128,8,3,3,3]{0,1,4,3,2:T(8,128)(2,1)}, u32[]{:S(2)}) copy-start(bf16[128,8,3,3,3]{0,1,4,3,2:T(8,128)(2,1)} %param.8) | copy-start | bytes 165892
  163.3 19.2 %copy-start.10 = (pred[8,5]{0,1:T(8,128)(4,1)S(1)}, pred[8,5]{0,1:T(8,128)(4,1)}, u32[]{:S(2)}) copy-start(pred[8,5]{0,1:T(8,128)(4,1)} %constant.49) | copy-start | bytes 124
  168.6 8.2 collective-permute-start.6
  173.5 7.8 collective-permute-start.7
  182.5 4.1 copy-start.4
  186.5 290.3 %all-gather.2.cloned.1.call-start = ((), (), s32[]{:S(2)}) async-start(), calls=%async_computation.6 | async-start | bytes 3538944 | tf_op jit(solution)/shard_map/all_gather | solution.py:71
  225.2 11.6 %collective-permute-start.8 = (bf16[16,1,16,32]{3,2,1,0:T(8,128)(2,1)S(1)}, bf16[16,1,16,32]{3,2,1,0:T(8,128)(2,1)S(1)}, u32[]{:S(2)}, u32[]{:S(2)}) collective-permute-start(bf16[16,1,16,32]{3,2,1,0:T(8,128)(2,1)S(1)} %get-tuple-element.42), channel_id=1, source_target_pairs={{0,8},{8,16},{16,24},{24,32},{32,40},{40,48},{48,56},{56,64},{64,7... | collective-permute-start | bytes 49160 | tf_op jit(solution)/shard_map/ppermute | solution.py:12
  234.8 6.5 collective-permute-start.9
  285.6 2.8 copy-start.6
  289.0 7.0 copy-start.3
  296.3 5.2 collective-permute-start.10
  299.6 7.1 collective-permute-start.11
  307.6 5.1 copy-start.2
  641.7 198.6 %all-to-all-start.1 = ((bf16[8,2,2048]{2,1,0:T(2,128)(2,1)}), bf16[8,2,2048]{2,1,0:T(2,128)(2,1)S(1)}, u32[]{:S(2)}, u32[]{:S(2)}) async-start(bf16[8,2,2048]{2,1,0:T(2,128)(2,1)} %reshape.164), calls=%async_computation.3 | async-start | bytes 131072 | tf_op jit(solution)/shard_map/all_to_all | solution.py:118
  840.6 4.4 slice-start
  842.0 3.5 slice-start.1
  845.5 133.1 %copy-start.1 = (bf16[32,16,3,3,3]{0,1,4,3,2:T(8,128)(2,1)S(1)}, bf16[32,16,3,3,3]{0,1,4,3,2:T(8,128)(2,1)}, u32[]{:S(2)}) copy-start(bf16[32,16,3,3,3]{0,1,4,3,2:T(8,128)(2,1)} %param.6) | copy-start | bytes 82948
Sparse Core Ops, SparseCore 0:
  105.2 53.7 reduce-scatter.2
  186.7 37.3 reduce-scatter.4
  307.7 76.2 all-gather.1
where the time goes:
time: 989 us; the launch traced here: 985 us
  blocking collectives  405 us (41%)
  matrix products  285 us (29%)
  waiting for transfers between devices  118 us (12%)
  local copies, waits for them, and re-layouts  92.2 us (9%)
  starting transfers between devices  48.5 us (5%)
  other arithmetic  22.4 us (2%)
  between operations  14.8 us (1%)
    conv_general_dilated x5, matrix products, conv_apply(): lax.conv_general_dilated(field[None], filters, (1, 1, 1), margins, dimens...  170 us
    psum x1, blocking collectives, body(): grads_three = lax.psum(grads_three, 'gz')  139 us
    psum x1, blocking collectives, body(): lax.psum(grads_four.astype(jnp.bfloat16), 'gz').astype(jnp.float32)  133 us
    conv_general_dilated x3, matrix products, filter_grad(): lax.conv_general_dilated(field[None], delta[None], (1, 1, 1), margins, di...  114 us
    psum x1, blocking collectives, body(): lax.psum(filter_grad(held_two, delta_two, x_margin), ('gz', 'ch'))  82.1 us
    reduce_scatter x1, waiting for transfers between devices, body(): lax.psum_scatter(conv_apply(held_three, part_filters, yx_margin).astype(j...  53.9 us
    all_gather x1, blocking collectives, channel_back(): shard_piece = lax.all_gather(rimmed, 'ch', axis=0, tiled=True)  41.3 us
    reduce_scatter x1, waiting for transfers between devices, body(): lax.psum_scatter(conv_apply(held_four, part_filters, yx_margin).astype(jn...  37.1 us
  transfers between devices with their start and end apart: 16, of which 9 were waited for; matrix products, arithmetic and copies ran while one was open for 10% of the time, Pallas kernels for 0%

commit v1 on v0

v1 whole, which is shorter than its diff:
```python
import jax
import jax.numpy as jnp
import numpy as np
from jax import lax
from jax.experimental import pallas as pl
from jax.experimental.pallas import tpu as pltpu
from jax.sharding import PartitionSpec as P

BF = jnp.bfloat16
F32 = jnp.float32
VMEM_LIMIT = 40 * 1024 * 1024


def grid(*extents):
    return np.meshgrid(*[np.arange(n) for n in extents], indexing="ij")


def shift_rows():
    out = np.zeros((128, 2, 128), np.float32)
    for x in range(128):
        if x > 0:
            out[x - 1, 0, x] = 1
        if x < 127:
            out[x + 1, 1, x] = 1
    return out.reshape(128, 256)


def shift_halves():
    out = np.zeros((2, 64, 2, 2, 64), np.float32)
    for h in range(2):
        for x in range(64):
            if x > 0:
                out[h, x - 1, 0, h, x] = 1
            if x < 63:
                out[h, x + 1, 1, h, x] = 1
    return out.reshape(128, 256)


def shift_straight():
    side = shift_halves()
    return np.concatenate([side[:, :128], np.eye(128, dtype=np.float32), side[:, 128:]], 1)


def shift_cross():
    straight = shift_straight()
    out = np.zeros((256, 384), np.float32)
    out[64:128] = straight[0:64]
    out[128:192] = straight[64:128]
    return out


def pool_two():
    out = np.zeros((2, 64, 2, 2, 64), np.float32)
    for h in range(2):
        for x in range(64):
            out[h, x, :, h, x] = 0.125
    return out.reshape(256, 128)


def pool_three():
    out = np.zeros((2, 2, 32, 2, 2, 2, 32), np.float32)
    for yc in range(2):
        for zc in range(2):
            for x in range(32):
                out[yc, zc, x, :, zc, yc, x] = 0.125
    return out.reshape(256, 128)


def gather_planes():
    out = np.zeros((5, 2, 2, 32, 2, 8, 32), np.float32)
    for b in range(5):
        for yy in range(2):
            y = 2 * b + yy - 1
            if 0 <= y < 8:
                for zz in range(2):
                    for x in range(32):
                        out[b, zz, yy, x, zz, y, x] = 1
    return out.reshape(640, 512)


def shift_planes():
    out = np.zeros((8, 32, 3, 3, 8, 32), np.float32)
    for ky in range(3):
        for kx in range(3):
            for y in range(8):
                for x in range(32):
                    sy, sx = y + ky, x + kx - 1
                    if sy < 8 and 0 <= sx < 32:
                        out[sy, sx, ky, kx, y, x] = 1
    return out.reshape(256, 2304)


def pool_four():
    out = np.zeros((8, 16, 2, 128), np.float32)
    for x in range(16):
        out[2:4, x, :, x] = 0.125
    return out.reshape(256, 128)


def spread_three():
    out = np.zeros((2, 8, 32, 6, 2, 32, 2), np.float32)
    for r in range(6):
        cell = (r - 1) // 2 + 1
        for h in range(2):
            for x in range(32):
                out[h, cell, x, r, h, x, :] = 0.125
    return out.reshape(512, 768)


def spread_two():
    out = np.zeros((2, 64, 2, 64, 2), np.float32)
    for h in range(2):
        for x in range(64):
            out[h, x, h, x, :] = 0.125
    return out.reshape(128, 256)


def const(build):
    return jnp.asarray(build(), BF)


def dot(a, b):
    return lax.dot_general(a, b, (((1,), (0,)), ((), ())), preferred_element_type=F32)


def dot_nt(a, b):
    return lax.dot_general(a, b, (((1,), (1,)), ((), ())), preferred_element_type=F32)


def sigmoid(u):
    return 0.5 * jnp.tanh(0.5 * u) + 0.5


def act_of(u, s):
    return u * (0.3 + 0.7 * s)


def slope_of(u, s):
    return 0.3 + 0.7 * (s + u * s * (1.0 - s))


def call(kernel, out_shape, scratch, flops, args):
    specs = [pl.BlockSpec(memory_space=pltpu.SMEM)] + [
        pl.BlockSpec(memory_space=pltpu.VMEM) for _ in args[1:]
    ]
    return pl.pallas_call(
        kernel,
        out_shape=out_shape,
        in_specs=specs,
        out_specs=jax.tree.map(lambda _: pl.BlockSpec(memory_space=pltpu.VMEM), out_shape),
        scratch_shapes=scratch,
        compiler_params=pltpu.CompilerParams(vmem_limit_bytes=VMEM_LIMIT),
        cost_estimate=pl.CostEstimate(flops=flops, bytes_accessed=1 << 20, transcendentals=0),
    )(*args)


def shift_volume(z, planes, shift, vx, zi):
    y = 0
    for ref, first, rows in planes:
        field = ref[z, first : first + rows].reshape(rows * 16, 128)
        sides = dot(field, shift)
        for r in range(rows):
            lanes = pl.ds((y + r) * 128, 128)
            vx[zi, 0:16, lanes] = sides[r * 16 : r * 16 + 16, :128].astype(BF)
            vx[zi, 16:32, lanes] = field[r * 16 : r * 16 + 16]
            vx[zi, 32:48, lanes] = sides[r * 16 : r * 16 + 16, 128:].astype(BF)
        y += rows


def forward_kernel(
    pos, ylo, mid, yhi, w2, w3, shift2, pool2, shift3, pool3, p3, sl3, sl2, vq, vx, sums
):
    gz, ch = pos[0], pos[1]
    shift = shift2[...]

    @pl.loop(0, 14)
    def _(z):
        shift_volume(z, ((ylo, 0, 5), (mid, 0, 8), (yhi, 0, 5)), shift, vx, z)

    filters = w2[...]

    @pl.loop(0, 6)
    def _(zc):
        zg = 4 * gz + zc - 1
        z_in = jnp.logical_and(zg >= 0, zg < 128)
        for q in range(4):
            total = [None, None]
            for dz in range(2):
                z = 2 * zc + dz
                rhs = jnp.concatenate(
                    [
                        vx[z + kz, :, (4 * q + ky) * 128 : (4 * q + ky + 4) * 128]
                        for kz in range(3)
                        for ky in range(3)
                    ],
                    axis=0,
                )
                pre = dot(filters, rhs)
                s = sigmoid(pre)
                a = act_of(pre, s)
                if q in (1, 2):
                    sl2[z, :, (q - 1) * 512 : q * 512] = slope_of(pre, s).astype(BF)
                for c in range(2):
                    part = a[:, c * 256 : c * 256 + 128] + a[:, c * 256 + 128 : c * 256 + 256]
                    total[c] = part if dz == 0 else total[c] + part
            for c in range(2):
                yc = 2 * q + c
                yg = 4 * ch + yc - 2
                inside = jnp.logical_and(z_in, jnp.logical_and(yg >= 0, yg < 32))
                sums[zc, yc * 32 : yc * 32 + 32] = jnp.where(inside, total[c], 0.0).astype(BF)

    pool = pool2[...]
    halves = shift3[...]
    for j in range(4):
        pair = jnp.concatenate([sums[j], sums[j + 2]], axis=1)
        pooled = dot(pair, pool).astype(BF)
        sides = dot(pooled, halves)
        for y in range(8):
            rows = slice(y * 32, y * 32 + 32)
            lanes = slice(y * 128, y * 128 + 128)
            vq[j, 0:32, lanes] = sides[rows, :128].astype(BF)
            vq[j, 32:64, lanes] = pooled[rows]
            vq[j, 64:96, lanes] = sides[rows, 128:].astype(BF)

    filters = w3[...]
    cells = [None, None]
    for zp in range(2):
        for n, (ya, yb) in enumerate(((1, 2), (3, 4), (0, 5))):
            blocks = []
            for kz in range(3):
                for ky in range(3):
                    if yb == ya + 1:
                        blocks.append(vq[zp + kz, :, (ya + ky) * 128 : (ya + ky + 2) * 128])
                    else:
                        blocks.append(
                            jnp.concatenate(
                                [
                                    vq[zp + kz, :, (ya + ky) * 128 : (ya + ky + 1) * 128],
                                    vq[zp + kz, :, (yb + ky) * 128 : (yb + ky + 1) * 128],
                                ],
                                axis=1,
                            )
                        )
            pre = dot(filters, jnp.concatenate(blocks, axis=0))
            s = sigmoid(pre)
            slope = slope_of(pre, s).astype(BF)
            sl3[zp, :, ya * 128 : ya * 128 + 128] = slope[:, :128]
            sl3[zp, :, yb * 128 : yb * 128 + 128] = slope[:, 128:]
            if n < 2:
                a = act_of(pre, s)
                part = a[:, :128] + a[:, 128:]
                cells[n] = part if zp == 0 else cells[n] + part
    both = jnp.concatenate(cells, axis=1).astype(BF)
    p3[...] = dot(both, pool3[...]).astype(BF)


def deep_kernel(
    pos, got, w4f, w4b, cot, sl3, planes_of, shift4, pool4, spread3, p4, d3, field, own, planes, back_in
):
    ch = pos[1]
    parts = []
    for b in range(5):
        yb = ch + (b - 2)
        inside = jnp.logical_and(yb >= 0, yb < 8)
        block = got[jnp.clip(yb, 0, 7)].reshape(192, 128)
        parts.append(jnp.where(inside, block.astype(F32), 0.0).astype(BF))
    flat = dot(jnp.concatenate(parts, axis=1), planes_of[...]).astype(BF)
    for zb in range(3):
        for zz in range(2):
            p = 2 * zb + zz
            planes[p * 64 : p * 64 + 64] = flat[zb * 64 : zb * 64 + 64, zz * 256 : zz * 256 + 256]
    for k in range(9):
        moved = dot(planes[...], shift4[:, k * 256 : k * 256 + 256]).astype(BF)
        for p in range(6):
            field[p, k * 64 : k * 64 + 64] = moved[p * 64 : p * 64 + 64]

    row = lax.broadcasted_iota(jnp.int32, (128, 256), 0)
    lane = lax.broadcasted_iota(jnp.int32, (128, 256), 1)
    source_y, source_x = row // 16, row % 16
    y, x = lane // 32, lane % 32
    match = (source_x == x // 2) & (source_y == ch - 1 + y // 2) & (y < 6)
    spread = jnp.where(match, 0.125, 0.0).astype(BF)
    mine = lax.broadcasted_iota(jnp.int32, (128, 256), 1) // 64 == 1

    filters = w4f[...]
    pooled = None
    deltas = []
    for z in range(4):
        pre = dot(filters, field[z : z + 3].reshape(1728, 256))
        s = sigmoid(pre)
        cell = (z + 1) // 2
        wide = dot(cot[:, cell].reshape(128, 128), spread)
        delta = wide * slope_of(pre, s)
        deltas.append(delta.astype(BF))
        if z in (1, 2):
            own[z - 1] = jnp.where(mine, delta, 0.0).astype(BF)
            a = act_of(pre, s)
            pooled = a if pooled is None else pooled + a
    high = pooled.astype(BF)
    low = (pooled - high.astype(F32)).astype(BF)
    p4[...] = dot(high, pool4[...]) + dot(low, pool4[...])

    stacked = jnp.concatenate(deltas, axis=0)
    for k in range(9):
        moved = dot(stacked, shift4[:, k * 256 : k * 256 + 256]).astype(BF)
        for z in range(4):
            back_in[z, k * 128 : k * 128 + 128] = moved[z * 128 : z * 128 + 128]
    filters = w4b[...]
    back = [
        dot(filters, back_in[z : z + 3].reshape(3456, 256)).astype(BF) for z in range(2)
    ]
    wide = dot(jnp.concatenate(back, axis=1), spread3[...])
    for r in range(6):
        yg = 4 * ch + r - 1
        inside = jnp.logical_and(yg >= 0, yg < 32)
        lanes = slice(r * 128, r * 128 + 128)
        value = jnp.where(inside, wide[:, lanes], 0.0)
        for zp in range(2):
            d3[zp, :, lanes] = (value * sl3[zp, :, lanes].astype(F32)).astype(BF)


def grads_kernel(pos, field, own, vq, d3, out):
    right = jnp.concatenate([own[0], own[1]], axis=1)
    for kz in range(3):
        left = jnp.concatenate([field[1 + kz], field[2 + kz]], axis=1)
        res = dot_nt(left, right)
        for k in range(9):
            for c in range(8):
                at = (kz * 9 + k) * 8
                out[c, at : at + 8] = res[k * 64 + c * 8 : k * 64 + c * 8 + 8]
    total = None
    zero = jnp.zeros((64, 512), BF)
    for j in range(4):
        rows = []
        for kz in range(3):
            zp = j - kz
            rows.append(d3[zp, :, 128:640] if 0 <= zp < 2 else zero)
        left = jnp.concatenate(
            [vq[j, :, (1 + ky) * 128 : (1 + ky) * 128 + 512] for ky in range(3)], axis=0
        )
        res = dot_nt(left, jnp.concatenate(rows, axis=0))
        total = res if total is None else total + res
    for k in range(9):
        for c in range(8):
            at = 216 + k * 4
            piece = total[k * 32 + c * 4 : k * 32 + c * 4 + 4]
            out[c, at : at + 4] = piece[:, :128]
            out[c, at + 36 : at + 40, 0:64] = piece[:, 128:]
    for c in range(8):
        out[c, 252:288, 64:128] = jnp.zeros((36, 64), F32)


def shallow_kernel(
    pos, d3, above, below, w3b, sl2, ylo, mid, yhi, shift2, straight, cross, spread2, g2, ds, vx, d2
):
    direct = straight[...]
    across = cross[...]
    for y in range(6):
        lanes = slice(y * 128, y * 128 + 128)
        first, second = d3[0, :, lanes], d3[1, :, lanes]
        moved = (
            dot(jnp.concatenate([above[:, lanes], second], axis=1), across),
            dot(first, direct),
            dot(second, direct),
            dot(jnp.concatenate([first, below[:, lanes]], axis=1), across),
        )
        for j in range(4):
            for kx in range(3):
                ds[j, kx * 64 : kx * 64 + 64, lanes] = moved[j][:, kx * 128 : kx * 128 + 128].astype(BF)

    shift = shift2[...]

    @pl.loop(0, 10)
    def _(z):
        shift_volume(z + 2, ((ylo, 4, 1), (mid, 0, 8), (yhi, 0, 1)), shift, vx, z)

    for z in (0, 1, 10, 11):
        d2[z] = jnp.zeros((32, 1024), BF)
    filters = w3b[...]
    widen = spread2[...]
    for zp in range(2):
        for q in range(2):
            rhs = jnp.concatenate(
                [
                    ds[zp + kz, :, (2 * q + ky) * 128 : (2 * q + ky + 2) * 128]
                    for kz in range(3)
                    for ky in range(3)
                ],
                axis=0,
            )
            back = dot(filters, rhs).astype(BF)
            for r in range(2):
                y = 2 * q + r
                wide = dot(back[:, r * 128 : r * 128 + 128], widen)
                for h in range(2):
                    value = wide[:, h * 128 : h * 128 + 128]
                    for dz in range(2):
                        z2 = 2 * (zp + 2 * h) + dz
                        for dy in range(2):
                            lanes = slice((2 * y + dy) * 128, (2 * y + dy) * 128 + 128)
                            slope = sl2[z2 + 2, :, lanes].astype(F32)
                            d2[z2 + 2, :, lanes] = (value * slope).astype(BF)

    def step(z, total):
        left = jnp.concatenate([vx[z, :, ky * 128 : ky * 128 + 1024] for ky in range(3)], axis=0)
        right = jnp.concatenate([d2[z + 2 - kz] for kz in range(3)], axis=0)
        return total + dot_nt(left, right)

    total = lax.fori_loop(0, 10, step, jnp.zeros((144, 96), F32))
    g2[...] = jnp.zeros((160, 128), F32)
    g2[0:144, 0:96] = total


def ladder(count):
    up = [(i, i + 1) for i in range(count - 1)]
    return up, [(b, a) for a, b in up]


def to_all(piece, axis):
    count = lax.axis_size(axis)
    copies = jnp.broadcast_to(piece[None], (count,) + piece.shape)
    return lax.all_to_all(copies, axis, 0, 0, tiled=True)


def body(volume, filters_two, filters_three, filters_four, cotangent):
    gz, ch = lax.axis_index("gz"), lax.axis_index("ch")
    pos = jnp.stack([gz, ch]).astype(jnp.int32)
    z_up, z_down = ladder(lax.axis_size("gz"))
    y_up, y_down = ladder(lax.axis_size("ch"))
    shape = jax.ShapeDtypeStruct

    field = volume.transpose(1, 2, 0, 3)
    cot = cotangent.reshape(1, 16, 128)
    low = lax.ppermute(
        jnp.concatenate([field[5:].reshape(24, 16, 128), cot], axis=0), "gz", z_up
    )
    high = lax.ppermute(
        jnp.concatenate([field[:3].reshape(24, 16, 128), cot], axis=0), "gz", z_down
    )
    mid = jnp.concatenate(
        [low[:24].reshape(3, 8, 16, 128), field, high[:24].reshape(3, 8, 16, 128)], axis=0
    )
    ylo = lax.ppermute(mid[:, 3:], "ch", y_up)
    yhi = lax.ppermute(mid[:, :5], "ch", y_down)

    four = filters_four.transpose(2, 3, 4, 1, 0).reshape(216, 128)
    three = filters_three.transpose(2, 3, 4, 1, 0).reshape(108, 64)
    three = jnp.pad(three, ((0, 0), (0, 64)))
    cots = jnp.concatenate([low[24:], cot, high[24:]], axis=0).reshape(48, 128)
    all_of = to_all(jnp.concatenate([four, three, cots], axis=0), "ch")
    four = all_of[:, :216].reshape(8, 27, 8, 128)
    three = all_of[:, 216:324, :64].reshape(8, 27, 4, 64)
    cots = all_of[:, 324:].reshape(8, 3, 16, 128)

    w2 = filters_two.transpose(0, 2, 3, 4, 1).reshape(32, 432)
    w3f = three.transpose(3, 1, 0, 2).reshape(64, 864)
    w3b = three[:, ::-1].transpose(0, 2, 1, 3).reshape(32, 1728)
    w4f = four.transpose(3, 1, 0, 2).reshape(128, 1728)
    w4b = four[:, ::-1].transpose(0, 2, 1, 3).reshape(64, 3456)

    shift2 = const(shift_rows)
    p3, sl3, sl2, vq = call(
        forward_kernel,
        (
            shape((64, 128), BF),
            shape((2, 64, 768), BF),
            shape((12, 32, 1024), BF),
            shape((4, 96, 1024), BF),
        ),
        [pltpu.VMEM((14, 48, 2304), BF), pltpu.VMEM((6, 256, 128), BF)],
        1 << 32,
        (pos, ylo, mid, yhi, w2, w3f, shift2, const(pool_two), const(shift_halves), const(pool_three)),
    )
    below = lax.ppermute(p3, "gz", z_up)
    above = lax.ppermute(p3, "gz", z_down)
    got = to_all(jnp.stack([below, p3, above]), "ch")
    p4, d3, field4, own4 = call(
        deep_kernel,
        (
            shape((128, 128), F32),
            shape((2, 64, 768), BF),
            shape((6, 576, 256), BF),
            shape((2, 128, 256), BF),
        ),
        [pltpu.VMEM((384, 256), BF), pltpu.VMEM((4, 1152, 256), BF)],
        1 << 32,
        (
            pos, got, w4f, w4b, cots, sl3,
            const(gather_planes), const(shift_planes), const(pool_four), const(spread_three),
        ),
    )
    above = lax.ppermute(d3[1], "gz", z_up)
    below = lax.ppermute(d3[0], "gz", z_down)

    grads = call(
        grads_kernel, shape((8, 288, 128), F32), [], 1 << 32, (pos, field4, own4, vq, d3)
    )
    grads = lax.all_to_all(grads.astype(BF), "ch", 0, 0, tiled=True)
    grads = grads.astype(F32).sum(axis=0).astype(BF)

    pooled_four = lax.all_to_all(
        p4[:, :16].astype(BF).reshape(8, 16, 16), "ch", 0, 0, tiled=True
    ).transpose(1, 0, 2)[:, None]

    g2 = call(
        shallow_kernel,
        shape((160, 128), F32),
        [
            pltpu.VMEM((4, 192, 768), BF),
            pltpu.VMEM((10, 48, 1280), BF),
            pltpu.VMEM((12, 32, 1024), BF),
        ],
        1 << 32,
        (
            pos, d3, above, below, w3b, sl2, ylo, mid, yhi,
            shift2, const(shift_straight), const(shift_cross), const(spread_two),
        ),
    )
    pieces = jnp.concatenate(
        [grads.reshape(32, 9, 128), g2.astype(BF).reshape(32, 5, 128)], axis=1
    )
    pieces = lax.all_to_all(pieces, "gz", 0, 0, tiled=True).astype(F32).sum(axis=0)
    two = to_all(pieces[9:].astype(BF), "ch").astype(F32).sum(axis=0)
    whole = to_all(jnp.concatenate([pieces[:9], two], axis=0).astype(BF), "gz")
    deep = whole[:, :9].reshape(288, 128).astype(F32)
    grad_four = deep[:216].reshape(3, 3, 3, 8, 128).transpose(4, 3, 0, 1, 2)
    lanes = jnp.concatenate([deep[216:252], deep[252:288, :64]], axis=1)
    grad_three = lanes.reshape(3, 3, 4, 3, 64).transpose(4, 2, 3, 0, 1)
    two = whole[:, 9:].reshape(160, 128)[:144, :96].astype(F32)
    grad_two = two.reshape(3, 3, 16, 3, 32).transpose(4, 2, 3, 0, 1)
    return (pooled_four, grad_two, grad_three, grad_four)


def solution(mesh):
    in_specs = (
        P(None, "gz", "ch", None),
        P(),
        P(None, "ch", None, None, None),
        P(None, "ch", None, None, None),
        P("ch", "gz", None, None),
    )
    out_specs = (
        P("ch", "gz", None, None),
        P(),
        P(None, "ch", None, None, None),
        P(None, "ch", None, None, None),
    )
    return jax.shard_map(body, mesh=mesh, in_specs=in_specs, out_specs=out_specs, check_vma=False)
```

time: 989 us -> 173 us (0.17)
  blocking collectives: 405 us -> 26.8 us
  matrix products: 285 us -> 0 us
  waiting for transfers between devices: 118 us -> 40.2 us
  local copies, waits for them, and re-layouts: 92.2 us -> 22.3 us
  other arithmetic: 22.4 us -> 1.35 us
  Pallas kernels: 0 us -> 20.8 us
  between operations: 14.8 us -> 1.24 us
  starting transfers between devices: 48.5 us -> 59.3 us
    psum x3 -> x0, blocking collectives: 354 us -> none  [the longest x1 139 us: body(): grads_three = lax.psum(grads_three, 'gz')]
    conv_general_dilated x8 -> x0, matrix products: 285 us -> none  [the longest x5 170 us: conv_apply(): lax.conv_general_dilated(field[None], filters, (1, 1, 1), margins, dimens...]
    reduce_scatter x2 -> x0, waiting for transfers between devices: 91.1 us -> none  [the longest x1 53.9 us: body(): lax.psum_scatter(conv_apply(held_three, part_filters, yx_margin).astype(j...]
    all_gather x1 -> x0, blocking collectives: 41.3 us -> none  [channel_back(): shard_piece = lax.all_gather(rimmed, 'ch', axis=0, tiled=True)]
    broadcast_in_dim x12 -> x4, local copies, waits for them, and re-layouts: 38.4 us -> 3.13 us  [to_all(): copies = jnp.broadcast_to(piece[None], (count,) + piece.shape)]
    all_to_all x1 -> x6, waiting for transfers between devices: 0.01 us -> 30.7 us  [the longest x4 25.9 us: to_all(): return lax.all_to_all(copies, axis, 0, 0, tiled=True)]
    all_to_all x1 -> x6, starting transfers between devices: 3.64 us -> 31.3 us  [the longest x4 24.3 us: to_all(): return lax.all_to_all(copies, axis, 0, 0, tiled=True)]
    pallas_call x0 -> x4, Pallas kernels: none -> 20.8 us  [call(): pl.pallas_call(kernel, out_shape=out_shape, in_specs=specs, out_specs=jax...]
  transfers between devices with their start and end apart: 16 -> 14, of which waited for: 9 -> 8; matrix products, arithmetic and copies ran while one was open for 10% -> 5% of each run, Pallas kernels for 0% -> 4%
where the time goes in v1:
time: 173 us; the launch traced here: 172 us
  starting transfers between devices  59.3 us (34%)
  waiting for transfers between devices  40.2 us (23%)
  blocking collectives  26.8 us (15%)
  local copies, waits for them, and re-layouts  22.3 us (13%)
  Pallas kernels  20.8 us (12%)
    all_to_all x1, blocking collectives, body(): lax.all_to_all(pieces, 'gz', 0, 0, tiled=True).astype(F32).sum(axis=0)  26.8 us
    all_to_all x4, waiting for transfers between devices, to_all(): return lax.all_to_all(copies, axis, 0, 0, tiled=True)  25.9 us
    all_to_all x4, starting transfers between devices, to_all(): return lax.all_to_all(copies, axis, 0, 0, tiled=True)  24.3 us
    pallas_call x4, Pallas kernels, call(): pl.pallas_call(kernel, out_shape=out_shape, in_specs=specs, out_specs=jax...  20.8 us
    unnamed x53, local copies, waits for them, and re-layouts  9.91 us
    ppermute x1, starting transfers between devices, body(): lax.ppermute(jnp.concatenate([field[5:].reshape(24, 16, 128), cot], axis=...  6.29 us
    ppermute x1, starting transfers between devices, body(): above = lax.ppermute(d3[1], 'gz', z_up)  5.86 us
    ppermute x1, waiting for transfers between devices, body(): lax.ppermute(jnp.concatenate([field[:3].reshape(24, 16, 128), cot], axis=...  4.89 us
  transfers between devices with their start and end apart: 14, of which 8 were waited for; matrix products, arithmetic and copies ran while one was open for 5% of the time, Pallas kernels for 4%

profile of v1, /device:TPU:1, one launch (start us, length us, event | category | flops | bytes accessed | tf_op | source)
XLA Modules:
  0.0 171.9 jit_solution(5736428522817237727)
XLA Ops:
  0.7 0.9 reshape.102
  1.5 1.1 copy.85
  2.7 6.3 %collective-permute-start = (bf16[25,16,128]{2,1,0:T(8,128)(2,1)S(1)}, bf16[25,16,128]{2,1,0:T(8,128)(2,1)S(1)}, u32[]{:S(2)}, u32[]{:S(2)}) collective-permute-start(bf16[25,16,128]{2,1,0:T(8,128)(2,1)S(1)} %get-tuple-element.48), channel_id=1, source_target_pairs={{0,8},{8,16},{16,24},{24,32},{32,40},{40,48},{48,56},{56,64},{64,7... | collective-permute-start | bytes 307208 | tf_op jit(solution)/shard_map/ppermute | solution.py:434
  9.0 1.9 %collective-permute-start.1 = (bf16[25,16,128]{2,1,0:T(8,128)(2,1)S(1)}, bf16[25,16,128]{2,1,0:T(8,128)(2,1)S(1)}, u32[]{:S(2)}, u32[]{:S(2)}) collective-permute-start(bf16[25,16,128]{2,1,0:T(8,128)(2,1)S(1)} %get-tuple-element.49), channel_id=1, source_target_pairs={{8,0},{16,8},{24,16},{32,24},{40,32},{48,40},{56,48},{64,56},{72,6... | collective-permute-start | bytes 307208 | tf_op jit(solution)/shard_map/ppermute | solution.py:437
  11.0 4.9 %collective-permute-done.1 = bf16[25,16,128]{2,1,0:T(8,128)(2,1)S(1)} collective-permute-done((bf16[25,16,128]{2,1,0:T(8,128)(2,1)S(1)}, bf16[25,16,128]{2,1,0:T(8,128)(2,1)S(1)}, u32[]{:S(2)}, u32[]{:S(2)}) %collective-permute-start.1) | collective-permute-done | bytes 102432 | tf_op jit(solution)/shard_map/ppermute | solution.py:437
  15.9 1.0 broadcast_in_dim.10
  16.9 5.4 %all-to-all-start = ((bf16[8,372,128]{2,1,0:T(8,128)(2,1)}), bf16[8,372,128]{2,1,0:T(8,128)(2,1)S(1)}, u32[]{:S(2)}, u32[]{:S(2)}) async-start(bf16[8,372,128]{2,1,0:T(8,128)(2,1)} %broadcast_in_dim.10), calls=%async_computation | async-start | bytes 1540096 | tf_op jit(solution)/shard_map/all_to_all | solution.py:422
  22.5 1.4 collective-permute-start.3
  23.9 4.0 %collective-permute-start.2 = (bf16[14,5,16,128]{3,2,1,0:T(8,128)(2,1)S(1)}, bf16[14,5,16,128]{3,2,1,0:T(8,128)(2,1)S(1)}, u32[]{:S(2)}, u32[]{:S(2)}) collective-permute-start(bf16[14,5,16,128]{3,2,1,0:T(8,128)(2,1)S(1)} %get-tuple-element.43), channel_id=1, source_target_pairs={{0,1},{1,2},{2,3},{3,4},{4,5},{5,6},{6,7},{8,9},{9,10},{10,11},{11... | collective-permute-start | bytes 860168 | tf_op jit(solution)/shard_map/ppermute | solution.py:443
  28.1 7.2 %all-to-all-done = bf16[8,372,128]{2,1,0:T(8,128)(2,1)S(1)} async-done(((bf16[8,372,128]{2,1,0:T(8,128)(2,1)}), bf16[8,372,128]{2,1,0:T(8,128)(2,1)S(1)}, u32[]{:S(2)}, u32[]{:S(2)}) %all-to-all-start) | async-done | bytes 761888 | tf_op jit(solution)/shard_map/all_to_all | solution.py:422
  35.7 3.7 %collective-permute-done.3.yhi = bf16[14,5,16,128]{3,2,1,0:T(8,128)(2,1)S(1)} collective-permute-done((bf16[14,5,16,128]{3,2,1,0:T(8,128)(2,1)S(1)}, bf16[14,5,16,128]{3,2,1,0:T(8,128)(2,1)S(1)}, u32[]{:S(2)}, u32[]{:S(2)}) %collective-permute-start.3) | collective-permute-done | bytes 286752 | tf_op jit(solution)/shard_map/ppermute | solution.py:444
  39.4 8.8 %shard_map.183 = (bf16[64,128]{1,0:T(8,128)(2,1)S(1)}, bf16[2,64,768]{2,1,0:T(8,128)(2,1)S(1)}, bf16[12,32,1024]{2,1,0:T(8,128)(2,1)S(1)}, bf16[4,96,1024]{2,1,0:T(8,128)(2,1)S(1)}) custom-call(s32[2]{0:T(128)S(1)} %pad_add_fusion.pos, bf16[14,5,16,128]{3,2,1,0:T(8,128)(2,1)S(1)} %collective-permute-done.2.ylo, ...), custom_call_target="tpu_custom_call" | custom-call | flops 4294967296 | bytes 1048576 | tf_op jit(solution)/shard_map/pallas_call | solution.py:146
  48.2 0.9 copy-done.11
  49.1 0.9 copy-done.13
  50.0 2.0 %collective-permute-start.5 = (bf16[64,128]{1,0:T(8,128)(2,1)S(1)}, bf16[64,128]{1,0:T(8,128)(2,1)S(1)}, u32[]{:S(2)}, u32[]{:S(2)}) collective-permute-start(bf16[64,128]{1,0:T(8,128)(2,1)S(1)} %get-tuple-element.12), channel_id=1, source_target_pairs={{8,0},{16,8},{24,16},{32,24},{40,32},{48,40},{56,48},{64,56},{72,6... | collective-permute-start | bytes 49160 | tf_op jit(solution)/shard_map/ppermute | solution.py:475
  52.1 4.5 %collective-permute-start.4 = (bf16[64,128]{1,0:T(8,128)(2,1)S(1)}, bf16[64,128]{1,0:T(8,128)(2,1)S(1)}, u32[]{:S(2)}, u32[]{:S(2)}) collective-permute-start(bf16[64,128]{1,0:T(8,128)(2,1)S(1)} %get-tuple-element.12), channel_id=1, source_target_pairs={{0,8},{8,16},{16,24},{24,32},{32,40},{40,48},{48,56},{56,64},{64,7... | collective-permute-start | bytes 49160 | tf_op jit(solution)/shard_map/ppermute | solution.py:474
  56.6 0.8 collective-permute-done.4
  57.5 0.9 broadcast_in_dim.11
  58.3 7.1 %all-to-all-start.1 = ((bf16[8,3,64,128]{3,2,1,0:T(8,128)(2,1)}), bf16[8,3,64,128]{3,2,1,0:T(8,128)(2,1)S(1)}, u32[]{:S(2)}, u32[]{:S(2)}) async-start(bf16[8,3,64,128]{3,2,1,0:T(8,128)(2,1)} %broadcast_in_dim.11), calls=%async_computation.1 | async-start | bytes 786432 | tf_op jit(solution)/shard_map/all_to_all | solution.py:422
  65.5 0.9 slice_bitcast_fusion.1
  66.7 1.0 slice.106
  67.7 1.0 reverse_bitcast_fusion.w4b
  68.7 4.3 %all-to-all-done.1.got = bf16[8,3,64,128]{3,2,1,0:T(8,128)(2,1)S(1)} async-done(((bf16[8,3,64,128]{3,2,1,0:T(8,128)(2,1)}), bf16[8,3,64,128]{3,2,1,0:T(8,128)(2,1)S(1)}, u32[]{:S(2)}, u32[]{:S(2)}) %all-to-all-start.1) | async-done | bytes 393248 | tf_op jit(solution)/shard_map/all_to_all | solution.py:422
  73.0 1.3 copy-done
  74.3 1.1 copy-done.2
  75.4 0.8 copy-done.7
  76.2 0.9 copy-done.16
  77.1 3.6 %shard_map.184 = (f32[128,128]{1,0:T(8,128)S(1)}, bf16[2,64,768]{2,1,0:T(8,128)(2,1)S(1)}, bf16[6,576,256]{2,1,0:T(8,128)(2,1)S(1)}, bf16[2,128,256]{2,1,0:T(8,128)(2,1)S(1)}) custom-call(s32[2]{0:T(128)S(1)} %pad_add_fusion.pos, bf16[8,3,64,128]{3,2,1,0:T(8,128)(2,1)S(1)} %all-to-all-done.1.got, bf16[128,1728]{1,0:T(8,128)(2,1)S(1)} %copy.76.w4f, ...), custom_call_target="tpu_custom_call" | custom-call | flops 4294967296 | bytes 1048576 | tf_op jit(solution)/shard_map/pallas_call | solution.py:146
  80.8 1.5 shard_map.185
  82.3 0.9 convert_element_type.30
  83.2 3.7 %all-to-all-start.3 = ((bf16[8,288,128]{2,1,0:T(8,128)(2,1)}), bf16[8,288,128]{2,1,0:T(8,128)(2,1)S(1)}, u32[]{:S(2)}, u32[]{:S(2)}) async-start(bf16[8,288,128]{2,1,0:T(8,128)(2,1)} %convert_element_type.30), calls=%async_computation.3 | async-start | bytes 1179648 | tf_op jit(solution)/shard_map/all_to_all | solution.py:498
  87.6 1.9 %collective-permute-start.7 = (bf16[64,768]{1,0:T(8,128)(2,1)}, bf16[64,768]{1,0:T(8,128)(2,1)S(1)}, u32[]{:S(2)}, u32[]{:S(2)}) collective-permute-start(bf16[64,768]{1,0:T(8,128)(2,1)} %get-tuple-element.46), channel_id=1, source_target_pairs={{8,0},{16,8},{24,16},{32,24},{40,32},{48,40},{56,48},{64,56},{72,6... | collective-permute-start | bytes 294920 | tf_op jit(solution)/shard_map/ppermute | solution.py:493
  89.5 5.9 %collective-permute-start.6 = (bf16[64,768]{1,0:T(8,128)(2,1)S(1)}, bf16[64,768]{1,0:T(8,128)(2,1)S(1)}, u32[]{:S(2)}, u32[]{:S(2)}) collective-permute-start(bf16[64,768]{1,0:T(8,128)(2,1)S(1)} %get-tuple-element.47), channel_id=1, source_target_pairs={{0,8},{8,16},{16,24},{24,32},{32,40},{40,48},{48,56},{56,64},{64,7... | collective-permute-start | bytes 294920 | tf_op jit(solution)/shard_map/ppermute | solution.py:492
  95.3 1.0 reverse_bitcast_fusion.1
  96.3 0.8 copy.77
  97.1 1.2 reshape.118.w3b
  98.4 6.9 %shard_map.186 = f32[160,128]{1,0:T(8,128)S(1)} custom-call(s32[2]{0:T(128)S(1)} %pad_add_fusion.pos, bf16[2,64,768]{2,1,0:T(8,128)(2,1)S(1)} %get-tuple-element.18.d3, bf16[64,768]{1,0:T(8,128)(2,1)S(1)} %collective-permute-done.6.above, bf16[64,768]{1,0:T(8,128)(2,1)S(1)} %collective-permute-done.7.below, bf16[32,1728]{1,0:T(8,128)(2,1)S(1)} %reshape.118.w3b, ...), custom_call_target="tpu_custom_call" | custom-call | flops 4294967296 | bytes 1048576 | tf_op jit(solution)/shard_map/pallas_call | solution.py:146
  105.5 26.8 %all_to_all.35 = bf16[32,14,128]{2,1,0:T(8,128)(2,1)S(1)} all-to-all(bf16[32,14,128]{2,1,0:T(8,128)(2,1)S(1)} %pad_maximum_fusion.3), channel_id=1, replica_groups=mesh['gz'=32,'ch'=8] {'gz'}, dimensions={0} | all-to-all | bytes 229376 | tf_op jit(solution)/shard_map/all_to_all | solution.py:522
  133.0 5.7 %all-to-all-start.5 = ((bf16[8,5,128]{2,1,0:T(8,128)(2,1)}), bf16[8,5,128]{2,1,0:T(8,128)(2,1)S(1)}, u32[]{:S(2)}, u32[]{:S(2)}) async-start(bf16[8,5,128]{2,1,0:T(8,128)(2,1)} %broadcast_in_dim.13), calls=%async_computation.5 | async-start | bytes 32768 | tf_op jit(solution)/shard_map/all_to_all | solution.py:422
  138.6 0.7 reshape.125
  139.3 4.4 %all-to-all-done.5 = bf16[8,5,128]{2,1,0:T(8,128)(2,1)S(1)} async-done(((bf16[8,5,128]{2,1,0:T(8,128)(2,1)}), bf16[8,5,128]{2,1,0:T(8,128)(2,1)S(1)}, u32[]{:S(2)}, u32[]{:S(2)}) %all-to-all-start.5) | async-done | bytes 10272 | tf_op jit(solution)/shard_map/all_to_all | solution.py:422
  143.7 3.3 %all-to-all-start.2 = ((bf16[8,2,128]{2,1,0:T(2,128)(2,1)}), bf16[8,2,128]{2,1,0:T(2,128)(2,1)S(1)}, u32[]{:S(2)}, u32[]{:S(2)}) async-start(bf16[8,2,128]{2,1,0:T(2,128)(2,1)} %reshape.125), calls=%async_computation.2 | async-start | bytes 8192 | tf_op jit(solution)/shard_map/all_to_all | solution.py:501
  147.0 4.8 %all-to-all-done.2 = bf16[8,2,128]{2,1,0:T(2,128)(2,1)S(1)} async-done(((bf16[8,2,128]{2,1,0:T(2,128)(2,1)}), bf16[8,2,128]{2,1,0:T(2,128)(2,1)S(1)}, u32[]{:S(2)}, u32[]{:S(2)}) %all-to-all-start.2) | async-done | bytes 4128 | tf_op jit(solution)/shard_map/all_to_all | solution.py:501
  151.9 0.7 broadcast_in_dim.14
  152.5 6.2 %all-to-all-start.6 = ((bf16[32,14,128]{2,1,0:T(8,128)(2,1)}), bf16[32,14,128]{2,1,0:T(8,128)(2,1)S(1)}, u32[]{:S(2)}, u32[]{:S(2)}) async-start(bf16[32,14,128]{2,1,0:T(8,128)(2,1)} %broadcast_in_dim.14), calls=%async_computation.6 | async-start | bytes 262144 | tf_op jit(solution)/shard_map/all_to_all | solution.py:422
  159.4 10.0 %all-to-all-done.6 = bf16[32,14,128]{2,1,0:T(8,128)(2,1)S(1)} async-done(((bf16[32,14,128]{2,1,0:T(8,128)(2,1)}), bf16[32,14,128]{2,1,0:T(8,128)(2,1)S(1)}, u32[]{:S(2)}, u32[]{:S(2)}) %all-to-all-start.6) | async-done | bytes 114720 | tf_op jit(solution)/shard_map/all_to_all | solution.py:422
  169.6 0.7 reshape.123
  171.2 0.7 copy.80
  (93 shorter events, 4.4 us)
Async XLA Ops:
  0.6 10.3 %copy-start.22 = (bf16[64,4,3,3,3]{0,1,4,3,2:T(4,128)(2,1)S(1)}, bf16[64,4,3,3,3]{0,1,4,3,2:T(4,128)(2,1)}, u32[]{:S(2)}) copy-start(bf16[64,4,3,3,3]{0,1,4,3,2:T(4,128)(2,1)} %param.18) | copy-start | bytes 41476
  0.6 15.3 %copy-start.21 = (bf16[128,8,3,3,3]{0,1,4,3,2:T(8,128)(2,1)S(1)}, bf16[128,8,3,3,3]{0,1,4,3,2:T(8,128)(2,1)}, u32[]{:S(2)}) copy-start(bf16[128,8,3,3,3]{0,1,4,3,2:T(8,128)(2,1)} %param.19) | copy-start | bytes 165892
  2.7 8.3 %collective-permute-start = (bf16[25,16,128]{2,1,0:T(8,128)(2,1)S(1)}, bf16[25,16,128]{2,1,0:T(8,128)(2,1)S(1)}, u32[]{:S(2)}, u32[]{:S(2)}) collective-permute-start(bf16[25,16,128]{2,1,0:T(8,128)(2,1)S(1)} %get-tuple-element.48), channel_id=1, source_target_pairs={{0,8},{8,16},{16,24},{24,32},{32,40},{40,48},{48,56},{56,64},{64,7... | collective-permute-start | bytes 307208 | tf_op jit(solution)/shard_map/ppermute | solution.py:434
  9.0 6.9 %collective-permute-start.1 = (bf16[25,16,128]{2,1,0:T(8,128)(2,1)S(1)}, bf16[25,16,128]{2,1,0:T(8,128)(2,1)S(1)}, u32[]{:S(2)}, u32[]{:S(2)}) collective-permute-start(bf16[25,16,128]{2,1,0:T(8,128)(2,1)S(1)} %get-tuple-element.49), channel_id=1, source_target_pairs={{8,0},{16,8},{24,16},{32,24},{40,32},{48,40},{56,48},{64,56},{72,6... | collective-permute-start | bytes 307208 | tf_op jit(solution)/shard_map/ppermute | solution.py:437
  16.9 18.4 %all-to-all-start = ((bf16[8,372,128]{2,1,0:T(8,128)(2,1)}), bf16[8,372,128]{2,1,0:T(8,128)(2,1)S(1)}, u32[]{:S(2)}, u32[]{:S(2)}) async-start(bf16[8,372,128]{2,1,0:T(8,128)(2,1)} %broadcast_in_dim.10), calls=%async_computation | async-start | bytes 1540096 | tf_op jit(solution)/shard_map/all_to_all | solution.py:422
  22.3 5.7 %copy-start.20 = (bf16[32,16,3,3,3]{0,1,4,3,2:T(8,128)(2,1)S(1)}, bf16[32,16,3,3,3]{0,1,4,3,2:T(8,128)(2,1)}, u32[]{:S(2)}) copy-start(bf16[32,16,3,3,3]{0,1,4,3,2:T(8,128)(2,1)} %param.17) | copy-start | bytes 82948
  22.4 16.9 %copy-start.5 = (bf16[128,256]{1,0:T(8,128)(2,1)S(1)}, bf16[128,256]{1,0:T(8,128)(2,1)}, u32[]{:S(2)}) copy-start(bf16[128,256]{1,0:T(8,128)(2,1)} %constant.37.clone.shift2) | copy-start | bytes 196612
  22.5 16.9 %copy-start.8 = (bf16[256,128]{1,0:T(8,128)(2,1)S(1)}, bf16[256,128]{1,0:T(8,128)(2,1)}, u32[]{:S(2)}) copy-start(bf16[256,128]{1,0:T(8,128)(2,1)} %constant.40.clone.pool3) | copy-start | bytes 196612
  22.5 16.9 %copy-start.9 = (bf16[128,256]{1,0:T(8,128)(2,1)S(1)}, bf16[128,256]{1,0:T(8,128)(2,1)}, u32[]{:S(2)}) copy-start(bf16[128,256]{1,0:T(8,128)(2,1)} %constant.39.clone.shift3) | copy-start | bytes 196612
  22.5 16.9 %copy-start.10 = (bf16[256,128]{1,0:T(8,128)(2,1)S(1)}, bf16[256,128]{1,0:T(8,128)(2,1)}, u32[]{:S(2)}) copy-start(bf16[256,128]{1,0:T(8,128)(2,1)} %constant.38.clone.pool2) | copy-start | bytes 196612
  22.5 16.9 %collective-permute-start.3 = (bf16[14,5,16,128]{3,2,1,0:T(8,128)(2,1)S(1)}, bf16[14,5,16,128]{3,2,1,0:T(8,128)(2,1)S(1)}, u32[]{:S(2)}, u32[]{:S(2)}) collective-permute-start(bf16[14,5,16,128]{3,2,1,0:T(8,128)(2,1)S(1)} %get-tuple-element.42), channel_id=1, source_target_pairs={{1,0},{2,1},{3,2},{4,3},{5,4},{6,5},{7,6},{9,8},{10,9},{11,10},{12... | collective-permute-start | bytes 860168 | tf_op jit(solution)/shard_map/ppermute | solution.py:444
  23.9 15.5 %collective-permute-start.2 = (bf16[14,5,16,128]{3,2,1,0:T(8,128)(2,1)S(1)}, bf16[14,5,16,128]{3,2,1,0:T(8,128)(2,1)S(1)}, u32[]{:S(2)}, u32[]{:S(2)}) collective-permute-start(bf16[14,5,16,128]{3,2,1,0:T(8,128)(2,1)S(1)} %get-tuple-element.43), channel_id=1, source_target_pairs={{0,1},{1,2},{2,3},{3,4},{4,5},{5,6},{6,7},{8,9},{9,10},{10,11},{11... | collective-permute-start | bytes 860168 | tf_op jit(solution)/shard_map/ppermute | solution.py:443
  35.3 4.1 %copy-start.17 = (bf16[8,372,128]{2,1,0:T(8,128)(2,1)}, bf16[8,372,128]{2,1,0:T(8,128)(2,1)S(1)}, u32[]{:S(2)}) copy-start(bf16[8,372,128]{2,1,0:T(8,128)(2,1)S(1)} %all-to-all-done) | copy-start | bytes 2285572
  35.4 4.0 %copy-start.19 = (bf16[8,108,64]{2,0,1:T(8,128)(2,1)}, bf16[8,108,64]{2,0,1:T(8,128)(2,1)S(1)}, u32[]{:S(2)}) copy-start(bf16[8,108,64]{2,0,1:T(8,128)(2,1)S(1)} %copy.83) | copy-start | bytes 331780
  48.2 0.9 copy-start.11
  49.1 0.9 copy-start.13
  50.0 16.3 %copy-start.15 = (bf16[2,64,768]{2,1,0:T(8,128)(2,1)}, bf16[2,64,768]{2,1,0:T(8,128)(2,1)S(1)}, u32[]{:S(2)}) copy-start(bf16[2,64,768]{2,1,0:T(8,128)(2,1)S(1)} %get-tuple-element.13.sl3) | copy-start | bytes 589828
  50.0 15.4 %copy-start.18 = (bf16[8,372,128]{2,1,0:T(8,128)(2,1)S(1)}, bf16[8,372,128]{2,1,0:T(8,128)(2,1)}, u32[]{:S(2)}) copy-start(bf16[8,372,128]{2,1,0:T(8,128)(2,1)} %copy-done.17) | copy-start | bytes 2285572
  50.0 6.6 %collective-permute-start.5 = (bf16[64,128]{1,0:T(8,128)(2,1)S(1)}, bf16[64,128]{1,0:T(8,128)(2,1)S(1)}, u32[]{:S(2)}, u32[]{:S(2)}) collective-permute-start(bf16[64,128]{1,0:T(8,128)(2,1)S(1)} %get-tuple-element.12), channel_id=1, source_target_pairs={{8,0},{16,8},{24,16},{32,24},{40,32},{48,40},{56,48},{64,56},{72,6... | collective-permute-start | bytes 49160 | tf_op jit(solution)/shard_map/ppermute | solution.py:475
  52.1 5.4 %collective-permute-start.4 = (bf16[64,128]{1,0:T(8,128)(2,1)S(1)}, bf16[64,128]{1,0:T(8,128)(2,1)S(1)}, u32[]{:S(2)}, u32[]{:S(2)}) collective-permute-start(bf16[64,128]{1,0:T(8,128)(2,1)S(1)} %get-tuple-element.12), channel_id=1, source_target_pairs={{0,8},{8,16},{16,24},{24,32},{32,40},{40,48},{48,56},{56,64},{64,7... | collective-permute-start | bytes 49160 | tf_op jit(solution)/shard_map/ppermute | solution.py:474
  58.3 14.7 %all-to-all-start.1 = ((bf16[8,3,64,128]{3,2,1,0:T(8,128)(2,1)}), bf16[8,3,64,128]{3,2,1,0:T(8,128)(2,1)S(1)}, u32[]{:S(2)}, u32[]{:S(2)}) async-start(bf16[8,3,64,128]{3,2,1,0:T(8,128)(2,1)} %broadcast_in_dim.11), calls=%async_computation.1 | async-start | bytes 786432 | tf_op jit(solution)/shard_map/all_to_all | solution.py:422
  66.5 6.5 %copy-start.1 = (bf16[512,768]{1,0:T(8,128)(2,1)S(1)}, bf16[512,768]{1,0:T(8,128)(2,1)}, u32[]{:S(2)}) copy-start(bf16[512,768]{1,0:T(8,128)(2,1)} %constant.44.clone.spread3) | copy-start | bytes 2359300
  73.0 1.3 copy-start
  74.3 1.1 copy-start.2
  75.4 0.8 copy-start.7
  76.2 0.9 copy-start.16
  77.1 3.7 %copy-start.12 = (bf16[4,96,1024]{2,1,0:T(8,128)(2,1)S(1)}, bf16[4,96,1024]{2,1,0:T(8,128)(2,1)}, u32[]{:S(2)}) copy-start(bf16[4,96,1024]{2,1,0:T(8,128)(2,1)} %copy-done.11) | copy-start | bytes 2359300
  83.2 15.1 %copy-start.3 = (bf16[256,384]{1,0:T(8,128)(2,1)S(1)}, bf16[256,384]{1,0:T(8,128)(2,1)}, u32[]{:S(2)}) copy-start(bf16[256,384]{1,0:T(8,128)(2,1)} %constant.46.clone.cross) | copy-start | bytes 589828
  83.2 15.1 %copy-start.4 = (bf16[128,384]{1,0:T(8,128)(2,1)S(1)}, bf16[128,384]{1,0:T(8,128)(2,1)}, u32[]{:S(2)}) copy-start(bf16[128,384]{1,0:T(8,128)(2,1)} %constant.45.clone.straight) | copy-start | bytes 294916
  83.2 15.1 %copy-start.6 = (bf16[128,256]{1,0:T(8,128)(2,1)S(1)}, bf16[128,256]{1,0:T(8,128)(2,1)}, u32[]{:S(2)}) copy-start(bf16[128,256]{1,0:T(8,128)(2,1)} %constant.47.clone.spread2) | copy-start | bytes 196612
  83.2 15.2 %copy-start.14 = (bf16[12,32,1024]{2,1,0:T(8,128)(2,1)S(1)}, bf16[12,32,1024]{2,1,0:T(8,128)(2,1)}, u32[]{:S(2)}) copy-start(bf16[12,32,1024]{2,1,0:T(8,128)(2,1)} %copy-done.13) | copy-start | bytes 2359300
  83.2 22.1 %all-to-all-start.3 = ((bf16[8,288,128]{2,1,0:T(8,128)(2,1)}), bf16[8,288,128]{2,1,0:T(8,128)(2,1)S(1)}, u32[]{:S(2)}, u32[]{:S(2)}) async-start(bf16[8,288,128]{2,1,0:T(8,128)(2,1)} %convert_element_type.30), calls=%async_computation.3 | async-start | bytes 1179648 | tf_op jit(solution)/shard_map/all_to_all | solution.py:498
  87.6 10.8 %collective-permute-start.7 = (bf16[64,768]{1,0:T(8,128)(2,1)}, bf16[64,768]{1,0:T(8,128)(2,1)S(1)}, u32[]{:S(2)}, u32[]{:S(2)}) collective-permute-start(bf16[64,768]{1,0:T(8,128)(2,1)} %get-tuple-element.46), channel_id=1, source_target_pairs={{8,0},{16,8},{24,16},{32,24},{40,32},{48,40},{56,48},{64,56},{72,6... | collective-permute-start | bytes 294920 | tf_op jit(solution)/shard_map/ppermute | solution.py:493
  89.5 8.8 %collective-permute-start.6 = (bf16[64,768]{1,0:T(8,128)(2,1)S(1)}, bf16[64,768]{1,0:T(8,128)(2,1)S(1)}, u32[]{:S(2)}, u32[]{:S(2)}) collective-permute-start(bf16[64,768]{1,0:T(8,128)(2,1)S(1)} %get-tuple-element.47), channel_id=1, source_target_pairs={{0,8},{8,16},{16,24},{24,32},{32,40},{40,48},{48,56},{56,64},{64,7... | collective-permute-start | bytes 294920 | tf_op jit(solution)/shard_map/ppermute | solution.py:492
  133.0 10.7 %all-to-all-start.5 = ((bf16[8,5,128]{2,1,0:T(8,128)(2,1)}), bf16[8,5,128]{2,1,0:T(8,128)(2,1)S(1)}, u32[]{:S(2)}, u32[]{:S(2)}) async-start(bf16[8,5,128]{2,1,0:T(8,128)(2,1)} %broadcast_in_dim.13), calls=%async_computation.5 | async-start | bytes 32768 | tf_op jit(solution)/shard_map/all_to_all | solution.py:422
  143.7 8.2 %all-to-all-start.2 = ((bf16[8,2,128]{2,1,0:T(2,128)(2,1)}), bf16[8,2,128]{2,1,0:T(2,128)(2,1)S(1)}, u32[]{:S(2)}, u32[]{:S(2)}) async-start(bf16[8,2,128]{2,1,0:T(2,128)(2,1)} %reshape.125), calls=%async_computation.2 | async-start | bytes 8192 | tf_op jit(solution)/shard_map/all_to_all | solution.py:501
  152.5 16.9 %all-to-all-start.6 = ((bf16[32,14,128]{2,1,0:T(8,128)(2,1)}), bf16[32,14,128]{2,1,0:T(8,128)(2,1)S(1)}, u32[]{:S(2)}, u32[]{:S(2)}) async-start(bf16[32,14,128]{2,1,0:T(8,128)(2,1)} %broadcast_in_dim.14), calls=%async_computation.6 | async-start | bytes 262144 | tf_op jit(solution)/shard_map/all_to_all | solution.py:422

commit v2 on v1

v2 whole, which is shorter than its diff:
```python
import jax
import jax.numpy as jnp
import numpy as np
from jax import lax
from jax.experimental import pallas as pl
from jax.experimental.pallas import tpu as pltpu
from jax.sharding import PartitionSpec as P

BF = jnp.bfloat16
F32 = jnp.float32
VMEM_LIMIT = 12 * 1024 * 1024


def grid(*extents):
    return np.meshgrid(*[np.arange(n) for n in extents], indexing="ij")


def shift_rows():
    out = np.zeros((128, 2, 128), np.float32)
    for x in range(128):
        if x > 0:
            out[x - 1, 0, x] = 1
        if x < 127:
            out[x + 1, 1, x] = 1
    return out.reshape(128, 256)


def shift_halves():
    out = np.zeros((2, 64, 2, 2, 64), np.float32)
    for h in range(2):
        for x in range(64):
            if x > 0:
                out[h, x - 1, 0, h, x] = 1
            if x < 63:
                out[h, x + 1, 1, h, x] = 1
    return out.reshape(128, 256)


def shift_straight():
    side = shift_halves()
    return np.concatenate([side[:, :128], np.eye(128, dtype=np.float32), side[:, 128:]], 1)


def shift_cross():
    straight = shift_straight()
    out = np.zeros((256, 384), np.float32)
    out[64:128] = straight[0:64]
    out[128:192] = straight[64:128]
    return out


def pool_two():
    out = np.zeros((2, 64, 2, 2, 64), np.float32)
    for h in range(2):
        for x in range(64):
            out[h, x, :, h, x] = 0.125
    return out.reshape(256, 128)


def pool_three():
    out = np.zeros((2, 2, 32, 2, 2, 2, 32), np.float32)
    for yc in range(2):
        for zc in range(2):
            for x in range(32):
                out[yc, zc, x, :, zc, yc, x] = 0.125
    return out.reshape(256, 128)


def gather_planes():
    out = np.zeros((5, 2, 2, 32, 2, 8, 32), np.float32)
    for b in range(5):
        for yy in range(2):
            y = 2 * b + yy - 1
            if 0 <= y < 8:
                for zz in range(2):
                    for x in range(32):
                        out[b, zz, yy, x, zz, y, x] = 1
    return out.reshape(640, 512)


def shift_planes():
    out = np.zeros((8, 32, 3, 3, 8, 32), np.float32)
    for ky in range(3):
        for kx in range(3):
            for y in range(8):
                for x in range(32):
                    sy, sx = y + ky, x + kx - 1
                    if sy < 8 and 0 <= sx < 32:
                        out[sy, sx, ky, kx, y, x] = 1
    return out.reshape(256, 2304)


def pool_four():
    out = np.zeros((8, 16, 2, 128), np.float32)
    for x in range(16):
        out[2:4, x, :, x] = 0.125
    return out.reshape(256, 128)


def spread_three():
    out = np.zeros((2, 8, 32, 6, 2, 32, 2), np.float32)
    for r in range(6):
        cell = (r - 1) // 2 + 1
        for h in range(2):
            for x in range(32):
                out[h, cell, x, r, h, x, :] = 0.125
    return out.reshape(512, 768)


def spread_two():
    out = np.zeros((2, 64, 2, 64, 2), np.float32)
    for h in range(2):
        for x in range(64):
            out[h, x, h, x, :] = 0.125
    return out.reshape(128, 256)


def deep_matrices():
    out = np.zeros((896, 2304), np.float32)
    out[:256] = shift_planes()
    out[256:896, :512] = gather_planes()
    out[256:768, 512:1280] = spread_three()
    return out


def const(build):
    return jnp.asarray(build(), BF)


def dot(a, b):
    return lax.dot_general(a, b, (((1,), (0,)), ((), ())), preferred_element_type=F32)


def dot_nt(a, b):
    return lax.dot_general(a, b, (((1,), (1,)), ((), ())), preferred_element_type=F32)


def sigmoid(u):
    return 0.5 * jnp.tanh(0.5 * u) + 0.5


def act_of(u, s):
    return u * (0.3 + 0.7 * s)


def slope_of(u, s):
    return 0.3 + 0.7 * (s + u * s * (1.0 - s))


def call(kernel, out_shape, scratch, flops, args, far_in=(), far_out=()):
    def place(far):
        return pl.BlockSpec(memory_space=pltpu.HBM if far else pltpu.VMEM)

    specs = [pl.BlockSpec(memory_space=pltpu.SMEM)] + [
        place(n in far_in) for n in range(1, len(args))
    ]
    args = [
        pltpu.with_memory_space_constraint(a, pltpu.HBM) if n in far_in else a
        for n, a in enumerate(args)
    ]
    return pl.pallas_call(
        kernel,
        out_shape=tuple(
            pltpu.HBM(o.shape, o.dtype) if n in far_out else o for n, o in enumerate(out_shape)
        ),
        in_specs=specs,
        out_specs=tuple(place(n in far_out) for n in range(len(out_shape))),
        scratch_shapes=scratch,
        compiler_params=pltpu.CompilerParams(vmem_limit_bytes=VMEM_LIMIT),
        cost_estimate=pl.CostEstimate(flops=flops, bytes_accessed=1 << 20, transcendentals=0),
    )(*args)


def copies(pairs, sems):
    out = [pltpu.make_async_copy(a, b, sems.at[n]) for n, (a, b) in enumerate(pairs)]
    for copy in out:
        copy.start()
    return out


def shallow_forward_kernel(
    pos, near, mid, far, w2, shift2, pool2, shift3, vq, sl2_far, vx_far, sums, sl2, vx, sems
):
    gz, ch = pos[0], pos[1]
    shift = shift2[...]

    odd = gz % 2 == 1
    for which, first, count in ((0, 0, 3), (1, 3, 8), (2, 11, 3)):

        @pl.loop(0, count, unroll=2 if count == 8 else 3)
        def _(z):
            if which == 1:
                field = mid[z].reshape(288, 128)
            else:
                one, two = near[z].reshape(288, 128), far[z].reshape(288, 128)
                if which == 2:
                    one, two = two, one
                field = jnp.where(odd, one.astype(F32), two.astype(F32)).astype(BF)
            sides = dot(field, shift)
            for y in range(18):
                lanes = slice(y * 128, y * 128 + 128)
                rows = slice(y * 16, y * 16 + 16)
                vx[z + first, 0:16, lanes] = sides[rows, :128].astype(BF)
                vx[z + first, 16:32, lanes] = field[rows]
                vx[z + first, 32:48, lanes] = sides[rows, 128:].astype(BF)

    vx_copy = pltpu.make_async_copy(
        vx.at[2:12, :, 512:1792], vx_far, sems.at[0]
    )
    vx_copy.start()
    filters = w2[...]

    @pl.loop(0, 6, unroll=2)
    def _(zc):
        zg = 4 * gz + zc - 1
        z_in = jnp.logical_and(zg >= 0, zg < 128)
        for q in range(4):
            rhs = jnp.concatenate(
                [
                    jnp.concatenate(
                        [
                            vx[2 * zc + zz, :, (4 * q + yy) * 128 : (4 * q + yy + 1) * 128],
                            vx[2 * zc + zz, :, (4 * q + yy + 2) * 128 : (4 * q + yy + 3) * 128],
                        ],
                        axis=1,
                    )
                    for zz in range(4)
                    for yy in range(4)
                ],
                axis=0,
            )
            pre = dot(filters, rhs)
            s = sigmoid(pre)
            a = act_of(pre, s)
            if q in (1, 2):
                sl2[zc, :, (q - 1) * 256 : q * 256] = slope_of(pre, s).astype(BF)
            total = (a[0:32] + a[32:64]) + (a[64:96] + a[96:128])
            for c in range(2):
                yc = 2 * q + c
                yg = 4 * ch + yc - 2
                inside = jnp.logical_and(z_in, jnp.logical_and(yg >= 0, yg < 32))
                cell = jnp.where(inside, total[:, c * 128 : c * 128 + 128], 0.0)
                sums[zc, yc * 32 : yc * 32 + 32] = cell.astype(BF)

    sl2_copy = pltpu.make_async_copy(sl2.at[1:5], sl2_far, sems.at[1])
    sl2_copy.start()
    pool = pool2[...]
    halves = shift3[...]
    for j in range(4):
        pair = jnp.concatenate([sums[j], sums[j + 2]], axis=1)
        pooled = dot(pair, pool).astype(BF)
        sides = dot(pooled, halves)
        for y in range(8):
            rows = slice(y * 32, y * 32 + 32)
            lanes = slice(y * 128, y * 128 + 128)
            vq[j, 0:32, lanes] = sides[rows, :128].astype(BF)
            vq[j, 32:64, lanes] = pooled[rows]
            vq[j, 64:96, lanes] = sides[rows, 128:].astype(BF)
    vx_copy.wait()
    sl2_copy.wait()


def middle_forward_kernel(pos, vq, w3, pool3, p3, sl3_far, vq_far, sl3, sems):
    vq_copy = pltpu.make_async_copy(vq, vq_far, sems.at[0])
    vq_copy.start()
    filters = w3[...]
    cells = [None, None]
    for zp in range(2):
        for n, (ya, yb) in enumerate(((1, 2), (3, 4), (0, 5))):
            blocks = []
            for kz in range(3):
                for ky in range(3):
                    if yb == ya + 1:
                        blocks.append(vq[zp + kz, :, (ya + ky) * 128 : (ya + ky + 2) * 128])
                    else:
                        blocks.append(
                            jnp.concatenate(
                                [
                                    vq[zp + kz, :, (ya + ky) * 128 : (ya + ky + 1) * 128],
                                    vq[zp + kz, :, (yb + ky) * 128 : (yb + ky + 1) * 128],
                                ],
                                axis=1,
                            )
                        )
            pre = dot(filters, jnp.concatenate(blocks, axis=0))
            s = sigmoid(pre)
            slope = slope_of(pre, s).astype(BF)
            sl3[zp, :, ya * 128 : ya * 128 + 128] = slope[:, :128]
            sl3[zp, :, yb * 128 : yb * 128 + 128] = slope[:, 128:]
            if n < 2:
                a = act_of(pre, s)
                part = a[:, :128] + a[:, 128:]
                cells[n] = part if zp == 0 else cells[n] + part
    sl3_copy = pltpu.make_async_copy(sl3, sl3_far, sems.at[1])
    sl3_copy.start()
    both = jnp.concatenate(cells, axis=1).astype(BF)
    p3[...] = dot(both, pool3[...]).astype(BF)
    vq_copy.wait()
    sl3_copy.wait()


def deep_kernel(
    pos, got, w4f, w4b, pool4, w3b, sl3_far, matrices,
    p4, d3, near_out, far_out, field, own,
    planes, back_in, sl3, planes_of, shift4, spread3, sems,
):
    planes_copy, shift_copy, spread_copy, sl3_copy = copies(
        (
            (matrices.at[256:896, 0:512], planes_of),
            (matrices.at[0:256], shift4),
            (matrices.at[256:768, 512:1280], spread3),
            (sl3_far, sl3),
        ),
        sems,
    )
    odd, ch = pos[0] % 2, pos[1]
    low = 2 - 2 * odd
    parts = []
    for b in range(5):
        yb = ch + (b - 2)
        inside = jnp.logical_and(yb >= 0, yb < 8)
        source = jnp.clip(yb, 0, 7)
        block = jnp.concatenate(
            [got[source, zb, 0:64] for zb in (low, 1, 2 - low)], axis=0
        )
        parts.append(jnp.where(inside, block.astype(F32), 0.0).astype(BF))
    planes_copy.wait()
    flat = dot(jnp.concatenate(parts, axis=1), planes_of[...]).astype(BF)
    for zb in range(3):
        for zz in range(2):
            p = 2 * zb + zz
            planes[p * 64 : p * 64 + 64] = flat[zb * 64 : zb * 64 + 64, zz * 256 : zz * 256 + 256]
    shift_copy.wait()
    for k in range(9):
        moved = dot(planes[...], shift4[:, k * 256 : k * 256 + 256]).astype(BF)
        for p in range(6):
            field[p, k * 64 : k * 64 + 64] = moved[p * 64 : p * 64 + 64]

    row = lax.broadcasted_iota(jnp.int32, (128, 256), 0)
    lane = lax.broadcasted_iota(jnp.int32, (128, 256), 1)
    source_y, source_x = row // 16, row % 16
    y, x = lane // 32, lane % 32
    match = (source_x == x // 2) & (source_y == ch - 1 + y // 2) & (y < 6)
    spread = jnp.where(match, 0.125, 0.0).astype(BF)
    mine = lax.broadcasted_iota(jnp.int32, (128, 256), 1) // 64 == 1

    filters = w4f[...]
    pooled = None
    deltas = []
    for z in range(4):
        pre = dot(filters, field[z : z + 3].reshape(1728, 256))
        s = sigmoid(pre)
        cell = (low, 1, 2 - low)[(z + 1) // 2]
        wide = dot(got[:, cell, 64:80].reshape(128, 128), spread)
        delta = wide * slope_of(pre, s)
        deltas.append(delta.astype(BF))
        if z in (1, 2):
            own[z - 1] = jnp.where(mine, delta, 0.0).astype(BF)
            a = act_of(pre, s)
            pooled = a if pooled is None else pooled + a
    high = pooled.astype(BF)
    low = (pooled - high.astype(F32)).astype(BF)
    p4[...] = dot(high, pool4[...]) + dot(low, pool4[...])

    stacked = jnp.concatenate(deltas, axis=0)
    for k in range(9):
        moved = dot(stacked, shift4[:, k * 256 : k * 256 + 256]).astype(BF)
        for z in range(4):
            back_in[z, k * 128 : k * 128 + 128] = moved[z * 128 : z * 128 + 128]
    filters = w4b[...]
    back = [
        dot(filters, back_in[z : z + 3].reshape(3456, 256)).astype(BF) for z in range(2)
    ]
    spread_copy.wait()
    sl3_copy.wait()
    wide = dot(jnp.concatenate(back, axis=1), spread3[...])
    for r in range(6):
        yg = 4 * ch + r - 1
        inside = jnp.logical_and(yg >= 0, yg < 32)
        lanes = slice(r * 128, r * 128 + 128)
        value = jnp.where(inside, wide[:, lanes], 0.0)
        for zp in range(2):
            d3[zp, :, lanes] = (value * sl3[zp, :, lanes].astype(F32)).astype(BF)
    near_out[...] = d3[1 - odd]
    far_out[...] = d3[odd]


def grads_kernel(pos, field, own, d3, p4, vq_far, sent, out, vq, sems):
    vq_copy = pltpu.make_async_copy(vq_far, vq, sems.at[0])
    vq_copy.start()
    right = jnp.concatenate([own[0], own[1]], axis=1)
    for kz in range(3):
        left = jnp.concatenate([field[1 + kz], field[2 + kz]], axis=1)
        res = dot_nt(left, right)
        for k in range(9):
            for c in range(8):
                at = (kz * 9 + k) * 8
                out[c, at : at + 8] = res[k * 64 + c * 8 : k * 64 + c * 8 + 8]
    vq_copy.wait()
    total = None
    zero = jnp.zeros((64, 512), BF)
    for j in range(4):
        rows = []
        for kz in range(3):
            zp = j - kz
            rows.append(d3[zp, :, 128:640] if 0 <= zp < 2 else zero)
        left = jnp.concatenate(
            [vq[j, :, (1 + ky) * 128 : (1 + ky) * 128 + 512] for ky in range(3)], axis=0
        )
        res = dot_nt(left, jnp.concatenate(rows, axis=0))
        total = res if total is None else total + res
    for k in range(9):
        for c in range(8):
            at = 216 + k * 4
            piece = total[k * 32 + c * 4 : k * 32 + c * 4 + 4]
            out[c, at : at + 4] = piece[:, :128]
            out[c, at + 36 : at + 40, 0:64] = piece[:, 128:]
    for c in range(8):
        out[c, 252:288, 64:128] = jnp.zeros((36, 64), F32)
        out[c, 288:304] = p4[c * 16 : c * 16 + 16]
        sent[c] = out[c].astype(BF)


def shallow_back_kernel(
    pos, d3, near, far, w3b, straight, cross, spread2, sl2_far, vx_far,
    g2, ds, d2, sl2, vx, sems,
):
    sl2_copy, vx_copy = copies(
        ((sl2_far, sl2), (vx_far, vx)), sems
    )

    def rows_of(ref, lead=None):
        parts = []
        for y in range(6):
            lanes = slice(y * 128, y * 128 + 128)
            parts.append(ref[:, lanes] if lead is None else ref[lead, :, lanes])
        return jnp.concatenate(parts, axis=0)

    odd = pos[0] % 2 == 1
    one, two = rows_of(near).astype(F32), rows_of(far).astype(F32)
    above = jnp.where(odd, one, two).astype(BF)
    below = jnp.where(odd, two, one).astype(BF)
    first, second = rows_of(d3, 0), rows_of(d3, 1)
    direct, across = straight[...], cross[...]
    sources = (
        (jnp.concatenate([above, second], axis=1), across),
        (first, direct),
        (second, direct),
        (jnp.concatenate([first, below], axis=1), across),
    )
    for j, (source, matrix) in enumerate(sources):
        moved = dot(source, matrix).astype(BF)
        for y in range(6):
            for kx in range(3):
                piece = moved[y * 64 : y * 64 + 64, kx * 128 : kx * 128 + 128]
                ds[j, kx * 64 : kx * 64 + 64, y * 128 : y * 128 + 128] = piece

    for z in (0, 1, 10, 11):
        d2[z] = jnp.zeros((32, 1024), BF)
    filters = w3b[...]
    backs = []
    for zp in range(2):
        for q in range(2):
            rhs = jnp.concatenate(
                [
                    ds[zp + kz, :, (2 * q + ky) * 128 : (2 * q + ky + 2) * 128]
                    for kz in range(3)
                    for ky in range(3)
                ],
                axis=0,
            )
            back = dot(filters, rhs).astype(BF)
            backs += [back[:, :128], back[:, 128:]]
    wide = dot(jnp.concatenate(backs, axis=0), spread2[...])
    sl2_copy.wait()
    for zp in range(2):
        for y in range(4):
            at = (zp * 4 + y) * 32
            for h in range(2):
                value = wide[at : at + 32, h * 128 : h * 128 + 128]
                z = zp + 2 * h
                for dz in range(2):
                    for dy in range(2):
                        rows = slice((dz * 2 + dy) * 32, (dz * 2 + dy) * 32 + 32)
                        slope = sl2[z, rows, y * 128 : y * 128 + 128].astype(F32)
                        lanes = slice((2 * y + dy) * 128, (2 * y + dy) * 128 + 128)
                        d2[2 * z + dz + 2, :, lanes] = (value * slope).astype(BF)

    vx_copy.wait()
    total = None
    for z in range(10):
        left = jnp.concatenate(
            [vx[z, :, ky * 128 : ky * 128 + 1024] for ky in range(3)], axis=0
        )
        right = jnp.concatenate([d2[z + 2 - kz] for kz in range(3)], axis=0)
        part = dot_nt(left, right)
        total = part if total is None else total + part
    g2[...] = jnp.zeros((160, 128), F32)
    g2[0:144, 0:96] = total


def write_kernel(pos, whole, four, three, two):
    deep = whole[:, 0:9].astype(F32).reshape(288, 128)
    four[...] = deep[:216]
    for k in range(9):
        low = deep[216 + k * 4 : 220 + k * 4]
        high = deep[252 + k * 4 : 256 + k * 4]
        three[k] = low[:, 0:64]
        three[9 + k] = low[:, 64:128]
        three[18 + k] = high[:, 0:64]
    shallow = whole[:, 9:14].astype(F32).reshape(160, 128)
    for kz in range(3):
        two[kz] = shallow[:144, kz * 32 : kz * 32 + 32]


def swap(one, two, axis):
    count = lax.axis_size(axis)
    inside = [(i, i ^ 1) for i in range(count)]
    outside = [(i, i + 1) for i in range(1, count - 1, 2)]
    outside = outside + [(b, a) for a, b in outside]
    return lax.ppermute(one, axis, inside), lax.ppermute(two, axis, outside)


def to_all(piece, axis):
    count = lax.axis_size(axis)
    copies = jnp.broadcast_to(piece[None], (count,) + piece.shape)
    return lax.all_to_all(copies, axis, 0, 0, tiled=True)


def band(filters):
    taps = filters.transpose(0, 2, 3, 4, 1).reshape(32, 3, 3, 48)
    rows = [
        jnp.pad(taps, ((0, 0), (dz, 1 - dz), (dy, 1 - dy), (0, 0)))
        for dz in range(2)
        for dy in range(2)
    ]
    return jnp.stack(rows).reshape(128, 768)


def body(volume, filters_two, filters_three, filters_four, cotangent):
    gz, ch = lax.axis_index("gz"), lax.axis_index("ch")
    pos = jnp.stack([gz, ch]).astype(jnp.int32)
    odd_z, odd_y = gz % 2, ch % 2
    shape = jax.ShapeDtypeStruct

    field = volume.transpose(1, 2, 0, 3)
    near, far = swap(
        lax.dynamic_slice_in_dim(field, 3 * (1 - odd_y), 5, 1),
        lax.dynamic_slice_in_dim(field, 3 * odd_y, 5, 1),
        "ch",
    )
    low = jnp.where(odd_y == 1, near, far)
    high = jnp.where(odd_y == 1, far, near)
    mid = jnp.concatenate([low, field, high], axis=1)
    near, far = swap(
        lax.dynamic_slice_in_dim(mid, 5 * (1 - odd_z), 3, 0),
        lax.dynamic_slice_in_dim(mid, 5 * odd_z, 3, 0),
        "gz",
    )
    w2 = band(filters_two)

    four = filters_four.transpose(2, 3, 4, 1, 0).reshape(216, 128)
    three = filters_three.transpose(2, 3, 4, 1, 0).reshape(108, 64)
    three = jnp.pad(three, ((0, 0), (0, 64)))
    held = jnp.concatenate([four, three], axis=0)
    near, far, held, w2 = lax.optimization_barrier((near, far, held, w2))
    all_of = to_all(held, "ch")
    four = all_of[:, :216].reshape(8, 27, 8, 128)
    three = all_of[:, 216:324, :64].reshape(8, 27, 4, 64)
    w3f = three.transpose(3, 1, 0, 2).reshape(64, 864)
    w3b = three[:, ::-1].transpose(0, 2, 1, 3).reshape(32, 1728)
    w4f = four.transpose(3, 1, 0, 2).reshape(128, 1728)
    w4b = four[:, ::-1].transpose(0, 2, 1, 3).reshape(64, 3456)

    vq, sl2, vx = call(
        shallow_forward_kernel,
        (
            shape((4, 96, 1024), BF),
            shape((4, 128, 512), BF),
            shape((10, 48, 1280), BF),
        ),
        [
            pltpu.VMEM((6, 256, 128), BF),
            pltpu.VMEM((6, 128, 512), BF),
            pltpu.VMEM((14, 48, 2304), BF),
            pltpu.SemaphoreType.DMA((2,)),
        ],
        1 << 32,
        (
            pos, near, mid, far, w2,
            const(shift_rows), const(pool_two), const(shift_halves),
        ),
        far_out=(1, 2),
    )
    p3, sl3, vq = call(
        middle_forward_kernel,
        (shape((64, 128), BF), shape((2, 64, 768), BF), shape((4, 96, 1024), BF)),
        [pltpu.VMEM((2, 64, 768), BF), pltpu.SemaphoreType.DMA((2,))],
        1 << 30,
        (pos, vq, w3f, const(pool_three)),
        far_out=(1, 2),
    )
    cot = cotangent.reshape(16, 128)
    sent = jnp.concatenate([p3, cot], axis=0)
    near, far = swap(sent, sent, "gz")
    got = to_all(jnp.stack([near, sent, far]), "ch")
    p4, d3, near, far, field4, own4 = call(
        deep_kernel,
        (
            shape((128, 128), F32),
            shape((2, 64, 768), BF),
            shape((64, 768), BF),
            shape((64, 768), BF),
            shape((6, 576, 256), BF),
            shape((2, 128, 256), BF),
        ),
        [
            pltpu.VMEM((384, 256), BF),
            pltpu.VMEM((4, 1152, 256), BF),
            pltpu.VMEM((2, 64, 768), BF),
            pltpu.VMEM((640, 512), BF),
            pltpu.VMEM((256, 2304), BF),
            pltpu.VMEM((512, 768), BF),
            pltpu.SemaphoreType.DMA((4,)),
        ],
        1 << 32,
        (
            pos, got, w4f, w4b, const(pool_four), w3b, sl3, const(deep_matrices),
        ),
        far_in=(5, 6, 7),
    )
    near, far = swap(near, far, "gz")
    (sent,) = call(
        grads_kernel,
        (shape((8, 304, 128), BF),),
        [
            pltpu.VMEM((8, 304, 128), F32),
            pltpu.VMEM((4, 96, 1024), BF),
            pltpu.SemaphoreType.DMA((1,)),
        ],
        1 << 31,
        (pos, field4, own4, d3, p4, vq),
        far_in=(5,),
    )
    near, far, sent = lax.optimization_barrier((near, far, sent))
    got = lax.all_to_all(sent, "ch", 0, 0, tiled=True)
    grads = got[:, :288].astype(F32).sum(axis=0).astype(BF)
    pooled_four = got[:, 288:, :16].transpose(1, 0, 2)[:, None]

    (g2,) = call(
        shallow_back_kernel,
        (shape((160, 128), F32),),
        [
            pltpu.VMEM((4, 192, 768), BF),
            pltpu.VMEM((12, 32, 1024), BF),
            pltpu.VMEM((4, 128, 512), BF),
            pltpu.VMEM((10, 48, 1280), BF),
            pltpu.SemaphoreType.DMA((2,)),
        ],
        1 << 32,
        (
            pos, d3, near, far, w3b,
            const(shift_straight), const(shift_cross), const(spread_two), sl2, vx,
        ),
        far_in=(8, 9),
    )
    pieces = jnp.concatenate(
        [grads.reshape(32, 9, 128), g2.astype(BF).reshape(32, 5, 128)], axis=1
    )
    pieces = lax.all_to_all(pieces, "gz", 0, 0, tiled=True).astype(F32).sum(axis=0)
    two = to_all(pieces[9:].astype(BF), "ch").astype(F32).sum(axis=0)
    whole = to_all(jnp.concatenate([pieces[:9], two], axis=0).astype(BF), "gz")
    four, three, two = call(
        write_kernel,
        (shape((216, 128), F32), shape((27, 4, 64), F32), shape((3, 144, 32), F32)),
        [],
        1 << 20,
        (pos, whole),
    )
    grad_four = four.reshape(3, 3, 3, 8, 128).transpose(4, 3, 0, 1, 2)
    grad_three = three.reshape(3, 3, 3, 4, 64).transpose(4, 3, 0, 1, 2)
    grad_two = two.reshape(3, 3, 3, 16, 32).transpose(4, 3, 0, 1, 2)
    return (pooled_four, grad_two, grad_three, grad_four)


def solution(mesh):
    in_specs = (
        P(None, "gz", "ch", None),
        P(),
        P(None, "ch", None, None, None),
        P(None, "ch", None, None, None),
        P("ch", "gz", None, None),
    )
    out_specs = (
        P("ch", "gz", None, None),
        P(),
        P(None, "ch", None, None, None),
        P(None, "ch", None, None, None),
    )
    return jax.shard_map(body, mesh=mesh, in_specs=in_specs, out_specs=out_specs, check_vma=False)
```

time: 173 us -> 142 us (0.82)
  local copies, waits for them, and re-layouts: 22.3 us -> 8.86 us
  starting transfers between devices: 59.3 us -> 47.4 us
  waiting for transfers between devices: 40.2 us -> 29.8 us
  blocking collectives: 26.8 us -> 31.2 us
    unnamed x53 -> x26, local copies, waits for them, and re-layouts: 9.91 us -> 1.88 us
    all_to_all x0 -> x1, blocking collectives: none -> 7.43 us  [to_all(): return lax.all_to_all(copies, axis, 0, 0, tiled=True)]
    ppermute x8, waiting for transfers between devices: 9.45 us -> 3.86 us  [swap(): return (lax.ppermute(one, axis, inside), lax.ppermute(two, axis, outside))]
    ppermute x8, starting transfers between devices: 28 us -> 23.4 us  [swap(): return (lax.ppermute(one, axis, inside), lax.ppermute(two, axis, outside))]
    all_to_all x4 -> x3, starting transfers between devices: 24.3 us -> 20.3 us  [to_all(): return lax.all_to_all(copies, axis, 0, 0, tiled=True)]
    all_to_all x4 -> x3, waiting for transfers between devices: 25.9 us -> 22.1 us  [to_all(): return lax.all_to_all(copies, axis, 0, 0, tiled=True)]
    all_to_all x2 -> x1, starting transfers between devices: 6.99 us -> 3.73 us  [body(): got = lax.all_to_all(sent, 'ch', 0, 0, tiled=True)]
    all_to_all x1, blocking collectives: 26.8 us -> 23.8 us  [body(): lax.all_to_all(pieces, 'gz', 0, 0, tiled=True).astype(F32).sum(axis=0)]
  transfers between devices with their start and end apart: 14 -> 12, of which waited for: 8 -> 7; matrix products, arithmetic and copies ran while one was open for 5% -> 4% of each run, Pallas kernels for 4% -> 9%
where the time goes in v2:
time: 142 us; the launch traced here: 141 us
  starting transfers between devices  47.4 us (33%)
  blocking collectives  31.2 us (22%)
  waiting for transfers between devices  29.8 us (21%)
  Pallas kernels  21.8 us (15%)
  local copies, waits for them, and re-layouts  8.86 us (6%)
    all_to_all x1, blocking collectives, body(): lax.all_to_all(pieces, 'gz', 0, 0, tiled=True).astype(F32).sum(axis=0)  23.8 us
    ppermute x8, starting transfers between devices, swap(): return (lax.ppermute(one, axis, inside), lax.ppermute(two, axis, outside))  23.4 us
    all_to_all x3, waiting for transfers between devices, to_all(): return lax.all_to_all(copies, axis, 0, 0, tiled=True)  22.1 us
    pallas_call x6, Pallas kernels, call(): pl.pallas_call(kernel, out_shape=tuple((pltpu.HBM(o.shape, o.dtype) if n...  21.8 us
    all_to_all x3, starting transfers between devices, to_all(): return lax.all_to_all(copies, axis, 0, 0, tiled=True)  20.3 us
    all_to_all x1, blocking collectives, to_all(): return lax.all_to_all(copies, axis, 0, 0, tiled=True)  7.43 us
    ppermute x8, waiting for transfers between devices, swap(): return (lax.ppermute(one, axis, inside), lax.ppermute(two, axis, outside))  3.86 us
    all_to_all x1, waiting for transfers between devices, body(): got = lax.all_to_all(sent, 'ch', 0, 0, tiled=True)  3.81 us
  transfers between devices with their start and end apart: 12, of which 7 were waited for; matrix products, arithmetic and copies ran while one was open for 4% of the time, Pallas kernels for 9%

profile of v2, /device:TPU:1, one launch (start us, length us, event | category | flops | bytes accessed | tf_op | source)
XLA Modules:
  0.0 141.1 jit_solution(13005096906572070899)
XLA Ops:
  0.7 1.1 copy.103
  1.8 2.6 %collective-permute-start = (bf16[8,5,16,128]{3,2,1,0:T(8,128)(2,1)S(1)}, bf16[8,5,16,128]{3,2,1,0:T(8,128)(2,1)S(1)}, u32[]{:S(2)}, u32[]{:S(2)}) collective-permute-start(bf16[8,5,16,128]{3,2,1,0:T(8,128)(2,1)S(1)} %get-tuple-element.80), channel_id=1, source_target_pairs={{0,1},{1,0},{2,3},{3,2},{4,5},{5,4},{6,7},{7,6},{8,9},{9,8},{10,11... | collective-permute-start | bytes 491528 | tf_op jit(solution)/shard_map/ppermute | solution.py:521
  4.4 0.7 collective-permute-start.1
  5.1 0.8 reshape.75
  5.8 1.0 copy.87
  6.9 0.3 pad_bitcast_fusion.3
  7.1 0.1 collective-permute-done
  7.3 0.1 pad_maximum_fusion.mid
  7.4 7.1 %collective-permute-start.3 = (bf16[3,18,16,128]{3,2,1,0:T(8,128)(2,1)S(1)}, bf16[3,18,16,128]{3,2,1,0:T(8,128)(2,1)S(1)}, u32[]{:S(2)}, u32[]{:S(2)}) collective-permute-start(bf16[3,18,16,128]{3,2,1,0:T(8,128)(2,1)S(1)} %get-tuple-element.74), channel_id=1, source_target_pairs={{8,16},{24,32},{40,48},{56,64},{72,80},{88,96},{104,112},{120,128}... | collective-permute-start | bytes 663560 | tf_op jit(solution)/shard_map/ppermute | solution.py:521
  14.5 0.1 collective-permute-start.2
  14.6 0.5 pad_maximum_fusion.1
  15.2 0.5 reshape.77.w2
  15.7 2.4 %collective-permute-done.3.far = bf16[3,18,16,128]{3,2,1,0:T(8,128)(2,1)S(1)} collective-permute-done((bf16[3,18,16,128]{3,2,1,0:T(8,128)(2,1)S(1)}, bf16[3,18,16,128]{3,2,1,0:T(8,128)(2,1)S(1)}, u32[]{:S(2)}, u32[]{:S(2)}) %collective-permute-start.3) | collective-permute-done | bytes 221216 | tf_op jit(solution)/shard_map/ppermute | solution.py:521
  18.1 0.9 broadcast_in_dim.10
  19.1 11.8 %all-to-all-start = ((bf16[8,324,128]{2,1,0:T(8,128)(2,1)}), bf16[8,324,128]{2,1,0:T(8,128)(2,1)S(1)}, u32[]{:S(2)}, u32[]{:S(2)}) async-start(bf16[8,324,128]{2,1,0:T(8,128)(2,1)} %broadcast_in_dim.10), calls=%async_computation | async-start | bytes 1343488 | tf_op jit(solution)/shard_map/all_to_all | solution.py:527
  30.8 0.1 reshape.80
  30.9 0.1 pad_add_fusion.pos
  31.0 4.9 %shard_map.165 = (bf16[4,96,1024]{2,1,0:T(8,128)(2,1)S(1)}, bf16[4,128,512]{2,1,0:T(8,128)(2,1)}, bf16[10,48,1280]{2,1,0:T(8,128)(2,1)}) custom-call(s32[2]{0:T(128)S(1)} %pad_add_fusion.pos, bf16[3,18,16,128]{3,2,1,0:T(8,128)(2,1)S(1)} %collective-permute-done.2.near, bf16[8,18,16,128]{3,2,1,0:T(8,128)(2,1)S(1)} %pad_maximum_fusion.mid, ...), custom_call_target="tpu_custom_call" | custom-call | flops 4294967296 | bytes 1048576 | tf_op jit(solution)/shard_map/pallas_call | solution.py:161
  35.9 3.5 %all-to-all-done = bf16[8,324,128]{2,1,0:T(8,128)(2,1)S(1)} async-done(((bf16[8,324,128]{2,1,0:T(8,128)(2,1)}), bf16[8,324,128]{2,1,0:T(8,128)(2,1)S(1)}, u32[]{:S(2)}, u32[]{:S(2)}) %all-to-all-start) | async-done | bytes 663584 | tf_op jit(solution)/shard_map/all_to_all | solution.py:527
  39.5 0.1 copy.92
  39.6 0.1 copy.93.w3
  39.8 1.9 %shard_map.166 = (bf16[64,128]{1,0:T(8,128)(2,1)S(1)}, bf16[2,64,768]{2,1,0:T(8,128)(2,1)}, bf16[4,96,1024]{2,1,0:T(8,128)(2,1)}) custom-call(s32[2]{0:T(128)S(1)} %pad_add_fusion.pos, bf16[4,96,1024]{2,1,0:T(8,128)(2,1)S(1)} %get-tuple-element.29.vq, bf16[64,864]{1,0:T(8,128)(2,1)S(1)} %copy.93.w3, bf16[256,128]{1,0:T(8,128)(2,1)S(1)} %copy-done.5), custom_call_target="tpu_custom_call" | custom-call | flops 1073741824 | bytes 1048576 | tf_op jit(solution)/shard_map/pallas_call | solution.py:161
  41.7 8.0 %collective-permute-start.5 = (bf16[80,128]{1,0:T(8,128)(2,1)S(1)}, bf16[80,128]{1,0:T(8,128)(2,1)S(1)}, u32[]{:S(2)}, u32[]{:S(2)}) collective-permute-start(bf16[80,128]{1,0:T(8,128)(2,1)S(1)} %constant_dynamic-update-slice_fusion), channel_id=1, source_target_pairs={{8,16},{24,32},{40,48},{56,64},{72,80},{88,96},{104,112},{120,128}... | collective-permute-start | bytes 61448 | tf_op jit(solution)/shard_map/ppermute | solution.py:521
  49.7 0.1 collective-permute-start.4
  49.8 1.4 collective-permute-done.5
  51.2 0.8 broadcast_in_dim.11
  52.0 3.5 %all-to-all-start.1 = ((bf16[8,3,80,128]{3,2,1,0:T(8,128)(2,1)}), bf16[8,3,80,128]{3,2,1,0:T(8,128)(2,1)S(1)}, u32[]{:S(2)}, u32[]{:S(2)}) async-start(bf16[8,3,80,128]{3,2,1,0:T(8,128)(2,1)} %broadcast_in_dim.11), calls=%async_computation.1 | async-start | bytes 983040 | tf_op jit(solution)/shard_map/all_to_all | solution.py:527
  55.6 0.1 copy.95
  55.7 0.9 reshape.84.w3b
  56.5 0.1 slice_bitcast_fusion.1
  56.7 0.1 copy.94
  56.8 0.2 copy.96.w4f
  57.0 8.4 %all-to-all-done.1.got = bf16[8,3,80,128]{3,2,1,0:T(8,128)(2,1)S(1)} async-done(((bf16[8,3,80,128]{3,2,1,0:T(8,128)(2,1)}), bf16[8,3,80,128]{3,2,1,0:T(8,128)(2,1)S(1)}, u32[]{:S(2)}, u32[]{:S(2)}) %all-to-all-start.1) | async-done | bytes 491552 | tf_op jit(solution)/shard_map/all_to_all | solution.py:527
  65.4 5.0 %shard_map.167 = (f32[128,128]{1,0:T(8,128)S(1)}, bf16[2,64,768]{2,1,0:T(8,128)(2,1)S(1)}, bf16[64,768]{1,0:T(8,128)(2,1)S(1)}, bf16[64,768]{1,0:T(8,128)(2,1)S(...) custom-call(s32[2]{0:T(128)S(1)} %pad_add_fusion.pos, ...), custom_call_target="tpu_custom_call" | custom-call | flops 4294967296 | bytes 1048576 | tf_op jit(solution)/shard_map/pallas_call | solution.py:161
  70.5 0.8 collective-permute-start.6
  71.3 4.1 %collective-permute-start.7 = (bf16[64,768]{1,0:T(8,128)(2,1)S(1)}, bf16[64,768]{1,0:T(8,128)(2,1)S(1)}, u32[]{:S(2)}, u32[]{:S(2)}) collective-permute-start(bf16[64,768]{1,0:T(8,128)(2,1)S(1)} %get-tuple-element.34), channel_id=1, source_target_pairs={{8,16},{24,32},{40,48},{56,64},{72,80},{88,96},{104,112},{120,128}... | collective-permute-start | bytes 294920 | tf_op jit(solution)/shard_map/ppermute | solution.py:521
  75.5 4.0 %shard_map.168 = bf16[8,304,128]{2,1,0:T(8,128)(2,1)} custom-call(s32[2]{0:T(128)S(1)} %pad_add_fusion.pos, bf16[6,576,256]{2,1,0:T(8,128)(2,1)S(1)} %get-tuple-element.35.field, bf16[2,128,256]{2,1,0:T(8,128)(2,1)S(1)} %get-tuple-element.36.own, bf16[2,64,768]{2,1,0:T(8,128)(2,1)S(1)} %get-tuple-element.37.d3, f32[128,128]{1,0:T(8,128)S(1)} %get-tuple-element.38.p4, ...), custom_call_target="tpu_custom_call" | custom-call | flops 2147483648 | bytes 1048576 | tf_op jit(solution)/shard_map/pallas_call | solution.py:161
  79.6 3.7 %all-to-all-start.2 = ((bf16[8,304,128]{2,1,0:T(8,128)(2,1)}), bf16[8,304,128]{2,1,0:T(8,128)(2,1)S(1)}, u32[]{:S(2)}, u32[]{:S(2)}) async-start(bf16[8,304,128]{2,1,0:T(8,128)(2,1)} %shard_map.168), calls=%async_computation.2 | async-start | bytes 1245184 | tf_op jit(solution)/shard_map/all_to_all | solution.py:646
  83.3 4.5 %shard_map.169 = f32[160,128]{1,0:T(8,128)S(1)} custom-call(s32[2]{0:T(128)S(1)} %pad_add_fusion.pos, bf16[2,64,768]{2,1,0:T(8,128)(2,1)S(1)} %get-tuple-element.37.d3, bf16[64,768]{1,0:T(8,128)(2,1)S(1)} %collective-permute-done.6.near, bf16[64,768]{1,0:T(8,128)(2,1)S(1)} %collective-permute-done.7.far, bf16[32,1728]{1,0:T(8,128)(2,1)S(1)} %copy-done, ...), custom_call_target="tpu_custom_call" | custom-call | flops 4294967296 | bytes 1048576 | tf_op jit(solution)/shard_map/pallas_call | solution.py:161
  87.9 3.8 %all-to-all-done.2 = bf16[8,304,128]{2,1,0:T(8,128)(2,1)S(1)} async-done(((bf16[8,304,128]{2,1,0:T(8,128)(2,1)}), bf16[8,304,128]{2,1,0:T(8,128)(2,1)S(1)}, u32[]{:S(2)}, u32[]{:S(2)}) %all-to-all-start.2) | async-done | bytes 622624 | tf_op jit(solution)/shard_map/all_to_all | solution.py:646
  91.7 0.1 slice_reduce_fusion
  91.9 23.8 %all_to_all.30 = bf16[32,14,128]{2,1,0:T(8,128)(2,1)S(1)} all-to-all(bf16[32,14,128]{2,1,0:T(8,128)(2,1)S(1)} %pad_maximum_fusion.2), channel_id=1, replica_groups=mesh['gz'=32,'ch'=8] {'gz'}, dimensions={0} | all-to-all | bytes 229376 | tf_op jit(solution)/shard_map/all_to_all | solution.py:670
  115.7 7.4 %all_to_all.31 = bf16[8,5,128]{2,1,0:T(8,128)(2,1)S(1)} all-to-all(bf16[8,5,128]{2,1,0:T(8,128)(2,1)S(1)} %broadcast_in_dim.13), channel_id=1, replica_groups=mesh['gz'=32,'ch'=8] {'ch'}, dimensions={0} | all-to-all | bytes 20480 | tf_op jit(solution)/shard_map/all_to_all | solution.py:527
  123.2 0.7 broadcast_in_dim.14
  123.9 5.0 %all-to-all-start.5 = ((bf16[32,14,128]{2,1,0:T(8,128)(2,1)}), bf16[32,14,128]{2,1,0:T(8,128)(2,1)S(1)}, u32[]{:S(2)}, u32[]{:S(2)}) async-start(bf16[32,14,128]{2,1,0:T(8,128)(2,1)} %broadcast_in_dim.14), calls=%async_computation.5 | async-start | bytes 262144 | tf_op jit(solution)/shard_map/all_to_all | solution.py:527
  128.9 0.6 copy.98
  129.5 10.2 %all-to-all-done.5.whole = bf16[32,14,128]{2,1,0:T(8,128)(2,1)S(1)} async-done(((bf16[32,14,128]{2,1,0:T(8,128)(2,1)}), bf16[32,14,128]{2,1,0:T(8,128)(2,1)S(1)}, u32[]{:S(2)}, u32[]{:S(2)}) %all-to-all-start.5) | async-done | bytes 114720 | tf_op jit(solution)/shard_map/all_to_all | solution.py:527
  139.7 1.4 %shard_map.170 = (f32[216,128]{1,0:T(8,128)}, f32[27,4,64]{2,1,0:T(4,128)}, f32[3,144,32]{2,1,0:T(8,128)}) custom-call(s32[2]{0:T(128)S(1)} %pad_add_fusion.pos, bf16[32,14,128]{2,1,0:T(8,128)(2,1)S(1)} %all-to-all-done.5.whole), custom_call_target="tpu_custom_call" | custom-call | flops 1048576 | bytes 1048576 | tf_op jit(solution)/shard_map/pallas_call | solution.py:161
  (48 shorter events, 0.6 us)
Async XLA Ops:
  1.8 5.4 %collective-permute-start = (bf16[8,5,16,128]{3,2,1,0:T(8,128)(2,1)S(1)}, bf16[8,5,16,128]{3,2,1,0:T(8,128)(2,1)S(1)}, u32[]{:S(2)}, u32[]{:S(2)}) collective-permute-start(bf16[8,5,16,128]{3,2,1,0:T(8,128)(2,1)S(1)} %get-tuple-element.80), channel_id=1, source_target_pairs={{0,1},{1,0},{2,3},{3,2},{4,5},{5,4},{6,7},{7,6},{8,9},{9,8},{10,11... | collective-permute-start | bytes 491528 | tf_op jit(solution)/shard_map/ppermute | solution.py:521
  4.4 2.9 %collective-permute-start.1 = (bf16[8,5,16,128]{3,2,1,0:T(8,128)(2,1)S(1)}, bf16[8,5,16,128]{3,2,1,0:T(8,128)(2,1)S(1)}, u32[]{:S(2)}, u32[]{:S(2)}) collective-permute-start(bf16[8,5,16,128]{3,2,1,0:T(8,128)(2,1)S(1)} %get-tuple-element.81), channel_id=1, source_target_pairs={{1,2},{3,4},{5,6},{2,1},{4,3},{6,5},{9,10},{11,12},{13,14},{10,9},... | collective-permute-start | bytes 491528 | tf_op jit(solution)/shard_map/ppermute | solution.py:521
  7.3 8.4 %copy-start.9 = (bf16[128,8,3,3,3]{0,1,4,3,2:T(8,128)(2,1)S(1)}, bf16[128,8,3,3,3]{0,1,4,3,2:T(8,128)(2,1)}, u32[]{:S(2)}) copy-start(bf16[128,8,3,3,3]{0,1,4,3,2:T(8,128)(2,1)} %param.17) | copy-start | bytes 165892
  7.4 10.7 %collective-permute-start.3 = (bf16[3,18,16,128]{3,2,1,0:T(8,128)(2,1)S(1)}, bf16[3,18,16,128]{3,2,1,0:T(8,128)(2,1)S(1)}, u32[]{:S(2)}, u32[]{:S(2)}) collective-permute-start(bf16[3,18,16,128]{3,2,1,0:T(8,128)(2,1)S(1)} %get-tuple-element.74), channel_id=1, source_target_pairs={{8,16},{24,32},{40,48},{56,64},{72,80},{88,96},{104,112},{120,128}... | collective-permute-start | bytes 663560 | tf_op jit(solution)/shard_map/ppermute | solution.py:521
  14.5 3.6 %collective-permute-start.2 = (bf16[3,18,16,128]{3,2,1,0:T(8,128)(2,1)S(1)}, bf16[3,18,16,128]{3,2,1,0:T(8,128)(2,1)S(1)}, u32[]{:S(2)}, u32[]{:S(2)}) collective-permute-start(bf16[3,18,16,128]{3,2,1,0:T(8,128)(2,1)S(1)} %get-tuple-element.75), channel_id=1, source_target_pairs={{0,8},{8,0},{16,24},{24,16},{32,40},{40,32},{48,56},{56,48},{64,72... | collective-permute-start | bytes 663560 | tf_op jit(solution)/shard_map/ppermute | solution.py:521
  14.6 16.2 %copy-start.10 = (bf16[16,1,8,16]{3,2,1,0:T(8,128)(2,1)S(1)}, bf16[16,1,8,16]{3,2,1,0:T(8,128)(2,1)}, u32[]{:S(2)}) copy-start(bf16[16,1,8,16]{3,2,1,0:T(8,128)(2,1)} %param.18) | copy-start | bytes 12292
  15.2 15.8 %copy-start.6 = (bf16[128,256]{1,0:T(8,128)(2,1)S(1)}, bf16[128,256]{1,0:T(8,128)(2,1)}, u32[]{:S(2)}) copy-start(bf16[128,256]{1,0:T(8,128)(2,1)} %constant.59.clone.shift3) | copy-start | bytes 196612
  15.2 15.8 %copy-start.7 = (bf16[256,128]{1,0:T(8,128)(2,1)S(1)}, bf16[256,128]{1,0:T(8,128)(2,1)}, u32[]{:S(2)}) copy-start(bf16[256,128]{1,0:T(8,128)(2,1)} %constant.58.clone.pool2) | copy-start | bytes 196612
  15.2 15.8 %copy-start.8 = (bf16[128,256]{1,0:T(8,128)(2,1)S(1)}, bf16[128,256]{1,0:T(8,128)(2,1)}, u32[]{:S(2)}) copy-start(bf16[128,256]{1,0:T(8,128)(2,1)} %constant.57.clone.shift2) | copy-start | bytes 196612
  19.1 20.4 %all-to-all-start = ((bf16[8,324,128]{2,1,0:T(8,128)(2,1)}), bf16[8,324,128]{2,1,0:T(8,128)(2,1)S(1)}, u32[]{:S(2)}, u32[]{:S(2)}) async-start(bf16[8,324,128]{2,1,0:T(8,128)(2,1)} %broadcast_in_dim.10), calls=%async_computation | async-start | bytes 1343488 | tf_op jit(solution)/shard_map/all_to_all | solution.py:527
  31.0 8.8 %copy-start.5 = (bf16[256,128]{1,0:T(8,128)(2,1)S(1)}, bf16[256,128]{1,0:T(8,128)(2,1)}, u32[]{:S(2)}) copy-start(bf16[256,128]{1,0:T(8,128)(2,1)} %constant.60.clone.pool3) | copy-start | bytes 196612
  41.7 9.5 %collective-permute-start.5 = (bf16[80,128]{1,0:T(8,128)(2,1)S(1)}, bf16[80,128]{1,0:T(8,128)(2,1)S(1)}, u32[]{:S(2)}, u32[]{:S(2)}) collective-permute-start(bf16[80,128]{1,0:T(8,128)(2,1)S(1)} %constant_dynamic-update-slice_fusion), channel_id=1, source_target_pairs={{8,16},{24,32},{40,48},{56,64},{72,80},{88,96},{104,112},{120,128}... | collective-permute-start | bytes 61448 | tf_op jit(solution)/shard_map/ppermute | solution.py:521
  49.7 1.5 %collective-permute-start.4 = (bf16[80,128]{1,0:T(8,128)(2,1)S(1)}, bf16[80,128]{1,0:T(8,128)(2,1)S(1)}, u32[]{:S(2)}, u32[]{:S(2)}) collective-permute-start(bf16[80,128]{1,0:T(8,128)(2,1)S(1)} %constant_dynamic-update-slice_fusion), channel_id=1, source_target_pairs={{0,8},{8,0},{16,24},{24,16},{32,40},{40,32},{48,56},{56,48},{64,72... | collective-permute-start | bytes 61448 | tf_op jit(solution)/shard_map/ppermute | solution.py:521
  52.0 13.4 %all-to-all-start.1 = ((bf16[8,3,80,128]{3,2,1,0:T(8,128)(2,1)}), bf16[8,3,80,128]{3,2,1,0:T(8,128)(2,1)S(1)}, u32[]{:S(2)}, u32[]{:S(2)}) async-start(bf16[8,3,80,128]{3,2,1,0:T(8,128)(2,1)} %broadcast_in_dim.11), calls=%async_computation.1 | async-start | bytes 983040 | tf_op jit(solution)/shard_map/all_to_all | solution.py:527
  56.5 8.9 %copy-start.4 = (bf16[256,128]{1,0:T(8,128)(2,1)S(1)}, bf16[256,128]{1,0:T(8,128)(2,1)}, u32[]{:S(2)}) copy-start(bf16[256,128]{1,0:T(8,128)(2,1)} %constant.61.clone.pool4) | copy-start | bytes 196612
  70.5 9.1 %collective-permute-start.6 = (bf16[64,768]{1,0:T(8,128)(2,1)S(1)}, bf16[64,768]{1,0:T(8,128)(2,1)S(1)}, u32[]{:S(2)}, u32[]{:S(2)}) collective-permute-start(bf16[64,768]{1,0:T(8,128)(2,1)S(1)} %get-tuple-element.33), channel_id=1, source_target_pairs={{0,8},{8,0},{16,24},{24,16},{32,40},{40,32},{48,56},{56,48},{64,72... | collective-permute-start | bytes 294920 | tf_op jit(solution)/shard_map/ppermute | solution.py:521
  71.3 8.2 %collective-permute-start.7 = (bf16[64,768]{1,0:T(8,128)(2,1)S(1)}, bf16[64,768]{1,0:T(8,128)(2,1)S(1)}, u32[]{:S(2)}, u32[]{:S(2)}) collective-permute-start(bf16[64,768]{1,0:T(8,128)(2,1)S(1)} %get-tuple-element.34), channel_id=1, source_target_pairs={{8,16},{24,32},{40,48},{56,64},{72,80},{88,96},{104,112},{120,128}... | collective-permute-start | bytes 294920 | tf_op jit(solution)/shard_map/ppermute | solution.py:521
  75.4 7.9 %copy-start = (bf16[32,1728]{1,0:T(8,128)(2,1)S(1)}, bf16[32,1728]{1,0:T(8,128)(2,1)}, u32[]{:S(2)}) copy-start(bf16[32,1728]{1,0:T(8,128)(2,1)} %reshape.84.w3b) | copy-start | bytes 331780
  75.5 7.9 %copy-start.1 = (bf16[256,384]{1,0:T(8,128)(2,1)S(1)}, bf16[256,384]{1,0:T(8,128)(2,1)}, u32[]{:S(2)}) copy-start(bf16[256,384]{1,0:T(8,128)(2,1)} %constant.64.clone.cross) | copy-start | bytes 589828
  75.5 7.9 %copy-start.2 = (bf16[128,384]{1,0:T(8,128)(2,1)S(1)}, bf16[128,384]{1,0:T(8,128)(2,1)}, u32[]{:S(2)}) copy-start(bf16[128,384]{1,0:T(8,128)(2,1)} %constant.63.clone.straight) | copy-start | bytes 294916
  75.5 7.9 %copy-start.3 = (bf16[128,256]{1,0:T(8,128)(2,1)S(1)}, bf16[128,256]{1,0:T(8,128)(2,1)}, u32[]{:S(2)}) copy-start(bf16[128,256]{1,0:T(8,128)(2,1)} %constant.65.clone.spread2) | copy-start | bytes 196612
  79.6 12.1 %all-to-all-start.2 = ((bf16[8,304,128]{2,1,0:T(8,128)(2,1)}), bf16[8,304,128]{2,1,0:T(8,128)(2,1)S(1)}, u32[]{:S(2)}, u32[]{:S(2)}) async-start(bf16[8,304,128]{2,1,0:T(8,128)(2,1)} %shard_map.168), calls=%async_computation.2 | async-start | bytes 1245184 | tf_op jit(solution)/shard_map/all_to_all | solution.py:646
  123.9 15.8 %all-to-all-start.5 = ((bf16[32,14,128]{2,1,0:T(8,128)(2,1)}), bf16[32,14,128]{2,1,0:T(8,128)(2,1)S(1)}, u32[]{:S(2)}, u32[]{:S(2)}) async-start(bf16[32,14,128]{2,1,0:T(8,128)(2,1)} %broadcast_in_dim.14), calls=%async_computation.5 | async-start | bytes 262144 | tf_op jit(solution)/shard_map/all_to_all | solution.py:527

commit v3 on v2

--- a/solution.py
+++ b/solution.py
@@ -116,10 +116,9 @@
 
 
 def deep_matrices():
-    out = np.zeros((896, 2304), np.float32)
+    out = np.zeros((768, 2304), np.float32)
     out[:256] = shift_planes()
-    out[256:896, :512] = gather_planes()
-    out[256:768, 512:1280] = spread_three()
+    out[256:768, :768] = spread_three()
     return out
 
 
@@ -190,14 +189,14 @@
         @pl.loop(0, count, unroll=2 if count == 8 else 3)
         def _(z):
             if which == 1:
-                field = mid[z].reshape(288, 128)
+                field = mid[z].reshape(224, 128)
             else:
-                one, two = near[z].reshape(288, 128), far[z].reshape(288, 128)
+                one, two = near[z].reshape(224, 128), far[z].reshape(224, 128)
                 if which == 2:
                     one, two = two, one
                 field = jnp.where(odd, one.astype(F32), two.astype(F32)).astype(BF)
             sides = dot(field, shift)
-            for y in range(18):
+            for y in range(14):
                 lanes = slice(y * 128, y * 128 + 128)
                 rows = slice(y * 16, y * 16 + 16)
                 vx[z + first, 0:16, lanes] = sides[rows, :128].astype(BF)
@@ -205,7 +204,7 @@
                 vx[z + first, 32:48, lanes] = sides[rows, 128:].astype(BF)
 
     vx_copy = pltpu.make_async_copy(
-        vx.at[2:12, :, 512:1792], vx_far, sems.at[0]
+        vx.at[2:12, :, 256:1536], vx_far, sems.at[0]
     )
     vx_copy.start()
     filters = w2[...]
@@ -214,13 +213,13 @@
     def _(zc):
         zg = 4 * gz + zc - 1
         z_in = jnp.logical_and(zg >= 0, zg < 128)
-        for q in range(4):
+        for q, (ya, yb) in enumerate(((1, 2), (3, 4), (0, 5))):
             rhs = jnp.concatenate(
                 [
                     jnp.concatenate(
                         [
-                            vx[2 * zc + zz, :, (4 * q + yy) * 128 : (4 * q + yy + 1) * 128],
-                            vx[2 * zc + zz, :, (4 * q + yy + 2) * 128 : (4 * q + yy + 3) * 128],
+                            vx[2 * zc + zz, :, (2 * ya + yy) * 128 : (2 * ya + yy + 1) * 128],
+                            vx[2 * zc + zz, :, (2 * yb + yy) * 128 : (2 * yb + yy + 1) * 128],
                         ],
                         axis=1,
                     )
@@ -232,12 +231,11 @@
             pre = dot(filters, rhs)
             s = sigmoid(pre)
             a = act_of(pre, s)
-            if q in (1, 2):
-                sl2[zc, :, (q - 1) * 256 : q * 256] = slope_of(pre, s).astype(BF)
+            if q < 2:
+                sl2[zc, :, q * 256 : q * 256 + 256] = slope_of(pre, s).astype(BF)
             total = (a[0:32] + a[32:64]) + (a[64:96] + a[96:128])
-            for c in range(2):
-                yc = 2 * q + c
-                yg = 4 * ch + yc - 2
+            for c, yc in enumerate((ya, yb)):
+                yg = 4 * ch + yc - 1
                 inside = jnp.logical_and(z_in, jnp.logical_and(yg >= 0, yg < 32))
                 cell = jnp.where(inside, total[:, c * 128 : c * 128 + 128], 0.0)
                 sums[zc, yc * 32 : yc * 32 + 32] = cell.astype(BF)
@@ -250,7 +248,7 @@
         pair = jnp.concatenate([sums[j], sums[j + 2]], axis=1)
         pooled = dot(pair, pool).astype(BF)
         sides = dot(pooled, halves)
-        for y in range(8):
+        for y in range(6):
             rows = slice(y * 32, y * 32 + 32)
             lanes = slice(y * 128, y * 128 + 128)
             vq[j, 0:32, lanes] = sides[rows, :128].astype(BF)
@@ -260,71 +258,63 @@
     sl2_copy.wait()
 
 
-def middle_forward_kernel(pos, vq, w3, pool3, p3, sl3_far, vq_far, sl3, sems):
-    vq_copy = pltpu.make_async_copy(vq, vq_far, sems.at[0])
-    vq_copy.start()
+def middle_forward_kernel(pos, vq, w3, pool3, cot, sent, edges, sl3):
+    sent[64:192] = cot[...]
     filters = w3[...]
     cells = [None, None]
     for zp in range(2):
-        for n, (ya, yb) in enumerate(((1, 2), (3, 4), (0, 5))):
-            blocks = []
-            for kz in range(3):
-                for ky in range(3):
-                    if yb == ya + 1:
-                        blocks.append(vq[zp + kz, :, (ya + ky) * 128 : (ya + ky + 2) * 128])
-                    else:
-                        blocks.append(
-                            jnp.concatenate(
-                                [
-                                    vq[zp + kz, :, (ya + ky) * 128 : (ya + ky + 1) * 128],
-                                    vq[zp + kz, :, (yb + ky) * 128 : (yb + ky + 1) * 128],
-                                ],
-                                axis=1,
-                            )
-                        )
+        for n in range(2):
+            blocks = [
+                vq[zp + kz, :, (2 * n + ky) * 128 : (2 * n + ky + 2) * 128]
+                for kz in range(3)
+                for ky in range(3)
+            ]
             pre = dot(filters, jnp.concatenate(blocks, axis=0))
             s = sigmoid(pre)
-            slope = slope_of(pre, s).astype(BF)
-            sl3[zp, :, ya * 128 : ya * 128 + 128] = slope[:, :128]
-            sl3[zp, :, yb * 128 : yb * 128 + 128] = slope[:, 128:]
-            if n < 2:
-                a = act_of(pre, s)
-                part = a[:, :128] + a[:, 128:]
-                cells[n] = part if zp == 0 else cells[n] + part
-    sl3_copy = pltpu.make_async_copy(sl3, sl3_far, sems.at[1])
-    sl3_copy.start()
+            sl3[zp, :, n * 256 : n * 256 + 256] = slope_of(pre, s).astype(BF)
+            a = act_of(pre, s)
+            part = a[:, :128] + a[:, 128:]
+            cells[n] = part if zp == 0 else cells[n] + part
     both = jnp.concatenate(cells, axis=1).astype(BF)
-    p3[...] = dot(both, pool3[...]).astype(BF)
-    vq_copy.wait()
-    sl3_copy.wait()
+    sent[0:64] = dot(both, pool3[...]).astype(BF)
+    odd = pos[1] % 2
+    for zp in range(2):
+        top, bottom = sl3[zp, :, 384:512], sl3[zp, :, 0:128]
+        edges[odd, zp * 64 : zp * 64 + 64] = top
+        edges[1 - odd, zp * 64 : zp * 64 + 64] = bottom
 
 
 def deep_kernel(
-    pos, got, w4f, w4b, pool4, w3b, sl3_far, matrices,
+    pos, own3, near, far, in1, out1, in2, out2, w4f, w4b, pool4, sl3, planes_of, w3b, matrices,
     p4, d3, near_out, far_out, field, own,
-    planes, back_in, sl3, planes_of, shift4, spread3, sems,
+    planes, back_in, shift4, spread3, sems,
 ):
-    planes_copy, shift_copy, spread_copy, sl3_copy = copies(
-        (
-            (matrices.at[256:896, 0:512], planes_of),
-            (matrices.at[0:256], shift4),
-            (matrices.at[256:768, 512:1280], spread3),
-            (sl3_far, sl3),
-        ),
-        sems,
+    shift_copy, spread_copy = copies(
+        ((matrices.at[0:256], shift4), (matrices.at[256:768, 0:768], spread3)), sems
     )
     odd, ch = pos[0] % 2, pos[1]
-    low = 2 - 2 * odd
-    parts = []
-    for b in range(5):
-        yb = ch + (b - 2)
-        inside = jnp.logical_and(yb >= 0, yb < 8)
-        source = jnp.clip(yb, 0, 7)
-        block = jnp.concatenate(
-            [got[source, zb, 0:64] for zb in (low, 1, 2 - low)], axis=0
-        )
-        parts.append(jnp.where(inside, block.astype(F32), 0.0).astype(BF))
-    planes_copy.wait()
+
+    def pick(cond, one, two):
+        return jnp.where(cond, one.astype(F32), two.astype(F32)).astype(BF)
+
+    def in_order(blocks):
+        first, second, third = blocks
+        return [pick(odd == 1, first, third), second, pick(odd == 1, third, first)]
+
+    def neighbour(inside, outside, upper, rows):
+        one, two = inside[rows], outside[rows]
+        return pick(upper, one, two), pick(upper, two, one)
+
+    odd_y, odd_pair = ch % 2 == 1, ch % 4 >= 2
+    mine = jnp.concatenate([near[0:64], own3[0:64], far[0:64]], axis=0)
+    below1, above1 = neighbour(in1, out1, odd_y, slice(0, 192))
+    below2, above2 = neighbour(in2, out2, odd_pair, slice(0, 192))
+    parts = [
+        jnp.concatenate(in_order([p[0:64], p[64:128], p[128:192]]), axis=0)
+        for p in (below2, below1, mine, above1, above2)
+    ]
+    cots = in_order([near[64:192], own3[64:192], far[64:192]])
+    edge_low, edge_high = neighbour(in1, out1, odd_y, slice(192, 320))
     flat = dot(jnp.concatenate(parts, axis=1), planes_of[...]).astype(BF)
     for zb in range(3):
         for zz in range(2):
@@ -342,7 +332,7 @@
     y, x = lane // 32, lane % 32
     match = (source_x == x // 2) & (source_y == ch - 1 + y // 2) & (y < 6)
     spread = jnp.where(match, 0.125, 0.0).astype(BF)
-    mine = lax.broadcasted_iota(jnp.int32, (128, 256), 1) // 64 == 1
+    inner = lax.broadcasted_iota(jnp.int32, (128, 256), 1) // 64 == 1
 
     filters = w4f[...]
     pooled = None
@@ -350,12 +340,11 @@
     for z in range(4):
         pre = dot(filters, field[z : z + 3].reshape(1728, 256))
         s = sigmoid(pre)
-        cell = (low, 1, 2 - low)[(z + 1) // 2]
-        wide = dot(got[:, cell, 64:80].reshape(128, 128), spread)
+        wide = dot(cots[(z + 1) // 2], spread)
         delta = wide * slope_of(pre, s)
         deltas.append(delta.astype(BF))
         if z in (1, 2):
-            own[z - 1] = jnp.where(mine, delta, 0.0).astype(BF)
+            own[z - 1] = jnp.where(inner, delta, 0.0).astype(BF)
             a = act_of(pre, s)
             pooled = a if pooled is None else pooled + a
     high = pooled.astype(BF)
@@ -372,7 +361,6 @@
         dot(filters, back_in[z : z + 3].reshape(3456, 256)).astype(BF) for z in range(2)
     ]
     spread_copy.wait()
-    sl3_copy.wait()
     wide = dot(jnp.concatenate(back, axis=1), spread3[...])
     for r in range(6):
         yg = 4 * ch + r - 1
@@ -380,14 +368,19 @@
         lanes = slice(r * 128, r * 128 + 128)
         value = jnp.where(inside, wide[:, lanes], 0.0)
         for zp in range(2):
-            d3[zp, :, lanes] = (value * sl3[zp, :, lanes].astype(F32)).astype(BF)
+            rows = slice(zp * 64, zp * 64 + 64)
+            if r == 0:
+                slope = edge_low[rows]
+            elif r == 5:
+                slope = edge_high[rows]
+            else:
+                slope = sl3[zp, :, (r - 1) * 128 : r * 128]
+            d3[zp, :, lanes] = (value * slope.astype(F32)).astype(BF)
     near_out[...] = d3[1 - odd]
     far_out[...] = d3[odd]
 
 
-def grads_kernel(pos, field, own, d3, p4, vq_far, sent, out, vq, sems):
-    vq_copy = pltpu.make_async_copy(vq_far, vq, sems.at[0])
-    vq_copy.start()
+def grads_kernel(pos, field, own, d3, p4, vq, sent, out):
     right = jnp.concatenate([own[0], own[1]], axis=1)
     for kz in range(3):
         left = jnp.concatenate([field[1 + kz], field[2 + kz]], axis=1)
@@ -396,7 +389,6 @@
             for c in range(8):
                 at = (kz * 9 + k) * 8
                 out[c, at : at + 8] = res[k * 64 + c * 8 : k * 64 + c * 8 + 8]
-    vq_copy.wait()
     total = None
     zero = jnp.zeros((64, 512), BF)
     for j in range(4):
@@ -405,7 +397,7 @@
             zp = j - kz
             rows.append(d3[zp, :, 128:640] if 0 <= zp < 2 else zero)
         left = jnp.concatenate(
-            [vq[j, :, (1 + ky) * 128 : (1 + ky) * 128 + 512] for ky in range(3)], axis=0
+            [vq[j, :, ky * 128 : ky * 128 + 512] for ky in range(3)], axis=0
         )
         res = dot_nt(left, jnp.concatenate(rows, axis=0))
         total = res if total is None else total + res
@@ -414,20 +406,20 @@
             at = 216 + k * 4
             piece = total[k * 32 + c * 4 : k * 32 + c * 4 + 4]
             out[c, at : at + 4] = piece[:, :128]
-            out[c, at + 36 : at + 40, 0:64] = piece[:, 128:]
+            at, lanes = (252 + k * 4, slice(0, 64)) if k < 5 else (232 + k * 4, slice(64, 128))
+            out[c, at : at + 4, lanes] = piece[:, 128:]
     for c in range(8):
-        out[c, 252:288, 64:128] = jnp.zeros((36, 64), F32)
-        out[c, 288:304] = p4[c * 16 : c * 16 + 16]
+        out[c, 268:272, 64:128] = jnp.zeros((4, 64), F32)
+        out[c, 272:288] = p4[c * 16 : c * 16 + 16]
         sent[c] = out[c].astype(BF)
 
 
 def shallow_back_kernel(
-    pos, d3, near, far, w3b, straight, cross, spread2, sl2_far, vx_far,
-    g2, ds, d2, sl2, vx, sems,
+    pos, d3, near, far, w3b, straight, cross, spread2, sl2, vx_far,
+    g2, ds, d2, vx, sems,
 ):
-    sl2_copy, vx_copy = copies(
-        ((sl2_far, sl2), (vx_far, vx)), sems
-    )
+    vx_copy = pltpu.make_async_copy(vx_far, vx, sems.at[0])
+    vx_copy.start()
 
     def rows_of(ref, lead=None):
         parts = []
@@ -472,7 +464,6 @@
             back = dot(filters, rhs).astype(BF)
             backs += [back[:, :128], back[:, 128:]]
     wide = dot(jnp.concatenate(backs, axis=0), spread2[...])
-    sl2_copy.wait()
     for zp in range(2):
         for y in range(4):
             at = (zp * 4 + y) * 32
@@ -504,21 +495,26 @@
     four[...] = deep[:216]
     for k in range(9):
         low = deep[216 + k * 4 : 220 + k * 4]
-        high = deep[252 + k * 4 : 256 + k * 4]
+        at, lanes = (252 + k * 4, slice(0, 64)) if k < 5 else (232 + k * 4, slice(64, 128))
+        high = deep[at : at + 4, lanes]
         three[k] = low[:, 0:64]
         three[9 + k] = low[:, 64:128]
-        three[18 + k] = high[:, 0:64]
+        three[18 + k] = high
     shallow = whole[:, 9:14].astype(F32).reshape(160, 128)
     for kz in range(3):
         two[kz] = shallow[:144, kz * 32 : kz * 32 + 32]
 
 
-def swap(one, two, axis):
+def swap(one, two, axis, step=1):
     count = lax.axis_size(axis)
-    inside = [(i, i ^ 1) for i in range(count)]
-    outside = [(i, i + 1) for i in range(1, count - 1, 2)]
+    inside = [(i, i ^ step) for i in range(count)]
+    outside = [(i, i + step) for i in range(count - step) if i % (2 * step) >= step]
     outside = outside + [(b, a) for a, b in outside]
     return lax.ppermute(one, axis, inside), lax.ppermute(two, axis, outside)
+
+
+def swap_cores(value):
+    return lax.ppermute(value, "gz", [(i, i ^ 1) for i in range(lax.axis_size("gz"))])
 
 
 def to_all(piece, axis):
@@ -545,28 +541,43 @@
 
     field = volume.transpose(1, 2, 0, 3)
     near, far = swap(
-        lax.dynamic_slice_in_dim(field, 3 * (1 - odd_y), 5, 1),
-        lax.dynamic_slice_in_dim(field, 3 * odd_y, 5, 1),
+        lax.dynamic_slice_in_dim(volume, 5 * (1 - odd_y), 3, 2).transpose(1, 2, 0, 3),
+        lax.dynamic_slice_in_dim(volume, 5 * odd_y, 3, 2).transpose(1, 2, 0, 3),
         "ch",
     )
     low = jnp.where(odd_y == 1, near, far)
     high = jnp.where(odd_y == 1, far, near)
     mid = jnp.concatenate([low, field, high], axis=1)
+
+    four = filters_four.transpose(2, 3, 4, 1, 0).reshape(216, 128)
+    three = filters_three.transpose(2, 3, 4, 1, 0).reshape(108, 64)
+    three = jnp.pad(three, ((0, 0), (0, 64)))
+    cot = cotangent.reshape(16, 128)
+    held = jnp.concatenate(
+        [
+            cot,
+            lax.dynamic_slice_in_dim(four, 108 * odd_z, 108, 0),
+            lax.dynamic_slice_in_dim(three, 54 * odd_z, 54, 0),
+        ],
+        axis=0,
+    )
+    held = jnp.broadcast_to(held[None], (8, 178, 128))
+    w2 = band(filters_two)
+    mid, held = lax.optimization_barrier((mid, held))
     near, far = swap(
         lax.dynamic_slice_in_dim(mid, 5 * (1 - odd_z), 3, 0),
         lax.dynamic_slice_in_dim(mid, 5 * odd_z, 3, 0),
         "gz",
     )
-    w2 = band(filters_two)
-
-    four = filters_four.transpose(2, 3, 4, 1, 0).reshape(216, 128)
-    three = filters_three.transpose(2, 3, 4, 1, 0).reshape(108, 64)
-    three = jnp.pad(three, ((0, 0), (0, 64)))
-    held = jnp.concatenate([four, three], axis=0)
-    near, far, held, w2 = lax.optimization_barrier((near, far, held, w2))
-    all_of = to_all(held, "ch")
-    four = all_of[:, :216].reshape(8, 27, 8, 128)
-    three = all_of[:, 216:324, :64].reshape(8, 27, 4, 64)
+    all_of = lax.all_to_all(held, "ch", 0, 0, tiled=True)
+    cots = all_of[:, :16].reshape(128, 128)
+    mine, w2 = lax.optimization_barrier((all_of[:, 16:], w2))
+    other = swap_cores(mine)
+    first = jnp.where(odd_z == 1, other, mine)
+    second = jnp.where(odd_z == 1, mine, other)
+    four = jnp.concatenate([first[:, :108], second[:, :108]], axis=1).reshape(8, 27, 8, 128)
+    three = jnp.concatenate([first[:, 108:, :64], second[:, 108:, :64]], axis=1)
+    three = three.reshape(8, 27, 4, 64)
     w3f = three.transpose(3, 1, 0, 2).reshape(64, 864)
     w3b = three[:, ::-1].transpose(0, 2, 1, 3).reshape(32, 1728)
     w4f = four.transpose(3, 1, 0, 2).reshape(128, 1728)
@@ -575,14 +586,14 @@
     vq, sl2, vx = call(
         shallow_forward_kernel,
         (
-            shape((4, 96, 1024), BF),
+            shape((4, 96, 768), BF),
             shape((4, 128, 512), BF),
             shape((10, 48, 1280), BF),
         ),
         [
-            pltpu.VMEM((6, 256, 128), BF),
+            pltpu.VMEM((6, 192, 128), BF),
             pltpu.VMEM((6, 128, 512), BF),
-            pltpu.VMEM((14, 48, 2304), BF),
+            pltpu.VMEM((14, 48, 1792), BF),
             pltpu.SemaphoreType.DMA((2,)),
         ],
         1 << 32,
@@ -592,18 +603,25 @@
         ),
         far_out=(1, 2),
     )
-    p3, sl3, vq = call(
+    sent, edges, sl3 = call(
         middle_forward_kernel,
-        (shape((64, 128), BF), shape((2, 64, 768), BF), shape((4, 96, 1024), BF)),
-        [pltpu.VMEM((2, 64, 768), BF), pltpu.SemaphoreType.DMA((2,))],
+        (
+            shape((192, 128), BF),
+            shape((2, 128, 128), BF),
+            shape((2, 64, 512), BF),
+        ),
+        [],
         1 << 30,
-        (pos, vq, w3f, const(pool_three)),
-        far_out=(1, 2),
-    )
-    cot = cotangent.reshape(16, 128)
-    sent = jnp.concatenate([p3, cot], axis=0)
+        (pos, vq, w3f, const(pool_three), cots),
+    )
     near, far = swap(sent, sent, "gz")
-    got = to_all(jnp.stack([near, sent, far]), "ch")
+    planes = jnp.concatenate([near[:64], sent[:64], far[:64]], axis=0)
+    in1, out1 = swap(
+        jnp.concatenate([planes, edges[0]], axis=0),
+        jnp.concatenate([planes, edges[1]], axis=0),
+        "ch",
+    )
+    in2, out2 = swap(planes, planes, "ch", 2)
     p4, d3, near, far, field4, own4 = call(
         deep_kernel,
         (
@@ -617,35 +635,28 @@
         [
             pltpu.VMEM((384, 256), BF),
             pltpu.VMEM((4, 1152, 256), BF),
-            pltpu.VMEM((2, 64, 768), BF),
-            pltpu.VMEM((640, 512), BF),
             pltpu.VMEM((256, 2304), BF),
             pltpu.VMEM((512, 768), BF),
-            pltpu.SemaphoreType.DMA((4,)),
+            pltpu.SemaphoreType.DMA((2,)),
         ],
         1 << 32,
         (
-            pos, got, w4f, w4b, const(pool_four), w3b, sl3, const(deep_matrices),
+            pos, sent, near, far, in1, out1, in2, out2,
+            w4f, w4b, const(pool_four), sl3, const(gather_planes), w3b, const(deep_matrices),
         ),
-        far_in=(5, 6, 7),
+        far_in=(13, 14),
     )
     near, far = swap(near, far, "gz")
     (sent,) = call(
         grads_kernel,
-        (shape((8, 304, 128), BF),),
-        [
-            pltpu.VMEM((8, 304, 128), F32),
-            pltpu.VMEM((4, 96, 1024), BF),
-            pltpu.SemaphoreType.DMA((1,)),
-        ],
+        (shape((8, 288, 128), BF),),
+        [pltpu.VMEM((8, 288, 128), F32)],
         1 << 31,
         (pos, field4, own4, d3, p4, vq),
-        far_in=(5,),
-    )
-    near, far, sent = lax.optimization_barrier((near, far, sent))
+    )
     got = lax.all_to_all(sent, "ch", 0, 0, tiled=True)
-    grads = got[:, :288].astype(F32).sum(axis=0).astype(BF)
-    pooled_four = got[:, 288:, :16].transpose(1, 0, 2)[:, None]
+    grads = got.astype(F32).sum(axis=0).astype(BF)
+    pooled_four = got[:, 272:, :16].transpose(1, 0, 2)[:, None]
 
     (g2,) = call(
         shallow_back_kernel,
@@ -653,16 +664,15 @@
         [
             pltpu.VMEM((4, 192, 768), BF),
             pltpu.VMEM((12, 32, 1024), BF),
-            pltpu.VMEM((4, 128, 512), BF),
             pltpu.VMEM((10, 48, 1280), BF),
-            pltpu.SemaphoreType.DMA((2,)),
+            pltpu.SemaphoreType.DMA((1,)),
         ],
         1 << 32,
         (
             pos, d3, near, far, w3b,
             const(shift_straight), const(shift_cross), const(spread_two), sl2, vx,
         ),
-        far_in=(8, 9),
+        far_in=(9,),
     )
     pieces = jnp.concatenate(
         [grads.reshape(32, 9, 128), g2.astype(BF).reshape(32, 5, 128)], axis=1

time: 142 us -> 131 us (0.923)
  waiting for transfers between devices: 29.8 us -> 20.7 us
  Pallas kernels: 21.8 us -> 17.7 us
  blocking collectives: 31.2 us -> 33.3 us
    all_to_all x3 -> x1, starting transfers between devices: 20.3 us -> 4.91 us  [to_all(): return lax.all_to_all(copies, axis, 0, 0, tiled=True)]
    all_to_all x3 -> x1, waiting for transfers between devices: 22.1 us -> 10.2 us  [to_all(): return lax.all_to_all(copies, axis, 0, 0, tiled=True)]
    all_to_all x0 -> x1, starting transfers between devices: none -> 7.83 us  [body(): all_of = lax.all_to_all(held, 'ch', 0, 0, tiled=True)]
    ppermute x8 -> x12, waiting for transfers between devices: 3.86 us -> 10.5 us  [swap(): return (lax.ppermute(one, axis, inside), lax.ppermute(two, axis, outside))]
    ppermute x8 -> x12, starting transfers between devices: 23.4 us -> 29.6 us  [swap(): return (lax.ppermute(one, axis, inside), lax.ppermute(two, axis, outside))]
    pallas_call x6, Pallas kernels: 21.8 us -> 17.7 us  [call(): pl.pallas_call(kernel, out_shape=tuple((pltpu.HBM(o.shape, o.dtype) if n...]
    all_to_all x1, waiting for transfers between devices: 3.81 us -> 0.01 us  [body(): got = lax.all_to_all(sent, 'ch', 0, 0, tiled=True)]
    all_to_all x1, blocking collectives: 7.43 us -> 9.47 us  [to_all(): return lax.all_to_all(copies, axis, 0, 0, tiled=True)]
  transfers between devices with their start and end apart: 12 -> 16, of which waited for: 7 -> 5; matrix products, arithmetic and copies ran while one was open for 4% -> 4% of each run, Pallas kernels for 9% -> 6%
where the time goes in v3:
time: 131 us
  starting transfers between devices  47.7 us (36%)
  blocking collectives  33.3 us (25%)
  waiting for transfers between devices  20.7 us (16%)
  Pallas kernels  17.7 us (14%)
  local copies, waits for them, and re-layouts  8.17 us (6%)
  other arithmetic  1.69 us (1%)
  between operations  1.31 us (1%)
    ppermute x12, starting transfers between devices, swap(): return (lax.ppermute(one, axis, inside), lax.ppermute(two, axis, outside))  29.6 us
    all_to_all x1, blocking collectives, body(): lax.all_to_all(pieces, 'gz', 0, 0, tiled=True).astype(F32).sum(axis=0)  23.9 us
    pallas_call x6, Pallas kernels, call(): pl.pallas_call(kernel, out_shape=tuple((pltpu.HBM(o.shape, o.dtype) if n...  17.7 us
    ppermute x12, waiting for transfers between devices, swap(): return (lax.ppermute(one, axis, inside), lax.ppermute(two, axis, outside))  10.5 us
    all_to_all x1, waiting for transfers between devices, to_all(): return lax.all_to_all(copies, axis, 0, 0, tiled=True)  10.2 us
    all_to_all x1, blocking collectives, to_all(): return lax.all_to_all(copies, axis, 0, 0, tiled=True)  9.47 us
    all_to_all x1, starting transfers between devices, body(): all_of = lax.all_to_all(held, 'ch', 0, 0, tiled=True)  7.83 us
    all_to_all x1, starting transfers between devices, to_all(): return lax.all_to_all(copies, axis, 0, 0, tiled=True)  4.91 us
  transfers between devices with their start and end apart: 16, of which 5 were waited for; matrix products, arithmetic and copies ran while one was open for 4% of the time, Pallas kernels for 6%

profile of v3, /device:TPU:1, one launch (start us, length us, event | category | flops | bytes accessed | tf_op | source)
XLA Modules:
  0.0 130.5 jit_solution(5385814782499344114)
XLA Ops:
  0.7 1.2 copy.94
  1.9 2.6 %collective-permute-start = (bf16[8,3,16,128]{3,2,1,0:T(8,128)(2,1)S(1)}, bf16[8,3,16,128]{3,2,1,0:T(8,128)(2,1)S(1)}, u32[]{:S(2)}, u32[]{:S(2)}) collective-permute-start(bf16[8,3,16,128]{3,2,1,0:T(8,128)(2,1)S(1)} %get-tuple-element.68), channel_id=1, source_target_pairs={{0,1},{1,0},{2,3},{3,2},{4,5},{5,4},{6,7},{7,6},{8,9},{9,8},{10,11... | collective-permute-start | bytes 294920 | tf_op jit(solution)/shard_map/ppermute | solution.py:513
  4.4 0.7 collective-permute-start.1
  5.1 0.9 reshape.76
  6.0 0.8 reshape.78
  7.0 0.8 broadcast_in_dim.8
  7.7 7.8 %all-to-all-start = ((bf16[8,178,128]{2,1,0:T(8,128)(2,1)}), bf16[8,178,128]{2,1,0:T(8,128)(2,1)S(1)}, u32[]{:S(2)}, u32[]{:S(2)}) async-start(bf16[8,178,128]{2,1,0:T(8,128)(2,1)} %broadcast_in_dim.8), calls=%async_computation | async-start | bytes 753664 | tf_op jit(solution)/shard_map/all_to_all | solution.py:572
  15.6 0.1 copy.78
  15.7 0.3 pad_bitcast_fusion.3
  16.1 7.3 %collective-permute-start.3 = (bf16[3,14,16,128]{3,2,1,0:T(8,128)(2,1)S(1)}, bf16[3,14,16,128]{3,2,1,0:T(8,128)(2,1)S(1)}, u32[]{:S(2)}, u32[]{:S(2)}) collective-permute-start(bf16[3,14,16,128]{3,2,1,0:T(8,128)(2,1)S(1)} %get-tuple-element.64), channel_id=1, source_target_pairs={{8,16},{24,32},{40,48},{56,64},{72,80},{88,96},{104,112},{120,128}... | collective-permute-start | bytes 516104 | tf_op jit(solution)/shard_map/ppermute | solution.py:513
  23.4 0.1 collective-permute-start.2
  23.5 0.5 pad_maximum_fusion
  24.0 0.5 reshape.80.w2
  24.5 0.1 pad_add_fusion.pos
  24.7 1.3 %collective-permute-start.4 = (bf16[8,162,128]{2,0,1:T(8,128)(2,1)S(1)}, bf16[8,162,128]{2,0,1:T(8,128)(2,1)S(1)}, u32[]{:S(2)}, u32[]{:S(2)}) collective-permute-start(bf16[8,162,128]{2,0,1:T(8,128)(2,1)S(1)} %copy.91), channel_id=1, source_target_pairs={{0,8},{8,0},{16,24},{24,16},{32,40},{40,32},{48,56},{56,48},{64,72... | collective-permute-start | bytes 995336 | tf_op jit(solution)/shard_map/ppermute | solution.py:517
  26.0 2.3 %collective-permute-done.3.far = bf16[3,14,16,128]{3,2,1,0:T(8,128)(2,1)S(1)} collective-permute-done((bf16[3,14,16,128]{3,2,1,0:T(8,128)(2,1)S(1)}, bf16[3,14,16,128]{3,2,1,0:T(8,128)(2,1)S(1)}, u32[]{:S(2)}, u32[]{:S(2)}) %collective-permute-start.3) | collective-permute-done | bytes 172064 | tf_op jit(solution)/shard_map/ppermute | solution.py:513
  28.3 4.6 %shard_map.174 = (bf16[4,96,768]{2,1,0:T(8,128)(2,1)S(1)}, bf16[4,128,512]{2,1,0:T(8,128)(2,1)}, bf16[10,48,1280]{2,1,0:T(8,128)(2,1)}) custom-call(s32[2]{0:T(128)S(1)} %pad_add_fusion.pos, bf16[3,14,16,128]{3,2,1,0:T(8,128)(2,1)S(1)} %collective-permute-done.2.near, bf16[8,14,16,128]{3,2,1,0:T(8,128)(2,1)S(1)} %pad_maximum_fusion.1.mid, ...), custom_call_target="tpu_custom_call" | custom-call | flops 4294967296 | bytes 1048576 | tf_op jit(solution)/shard_map/pallas_call | solution.py:160
  33.2 0.1 copy.82
  33.2 0.1 copy.83.w3
  33.4 0.4 copy-done.7
  33.8 1.2 shard_map.175
  34.9 2.8 %collective-permute-start.6 = (bf16[192,128]{1,0:T(8,128)(2,1)S(1)}, bf16[192,128]{1,0:T(8,128)(2,1)S(1)}, u32[]{:S(2)}, u32[]{:S(2)}) collective-permute-start(bf16[192,128]{1,0:T(8,128)(2,1)S(1)} %get-tuple-element.28.own3), channel_id=1, source_target_pairs={{8,16},{24,32},{40,48},{56,64},{72,80},{88,96},{104,112},{120,128}... | collective-permute-start | bytes 147464 | tf_op jit(solution)/shard_map/ppermute | solution.py:513
  37.8 0.1 collective-permute-start.5
  38.1 3.2 %collective-permute-done.6.far = bf16[192,128]{1,0:T(8,128)(2,1)S(1)} collective-permute-done((bf16[192,128]{1,0:T(8,128)(2,1)S(1)}, bf16[192,128]{1,0:T(8,128)(2,1)S(1)}, u32[]{:S(2)}, u32[]{:S(2)}) %collective-permute-start.6) | collective-permute-done | bytes 49184 | tf_op jit(solution)/shard_map/ppermute | solution.py:513
  41.3 0.6 pad_maximum_fusion.8
  41.9 0.7 collective-permute-start.10
  42.5 4.3 %collective-permute-start.9 = (bf16[192,128]{1,0:T(8,128)(2,1)}, bf16[192,128]{1,0:T(8,128)(2,1)S(1)}, u32[]{:S(2)}, u32[]{:S(2)}) collective-permute-start(bf16[192,128]{1,0:T(8,128)(2,1)} %pad_maximum_fusion.8), channel_id=1, source_target_pairs={{0,2},{1,3},{2,0},{3,1},{4,6},{5,7},{6,4},{7,5},{8,10},{9,11},{10,... | collective-permute-start | bytes 147464 | tf_op jit(solution)/shard_map/ppermute | solution.py:513
  46.8 0.7 collective-permute-start.8
  47.5 2.8 %collective-permute-start.7 = (bf16[320,128]{1,0:T(8,128)(2,1)S(1)}, bf16[320,128]{1,0:T(8,128)(2,1)S(1)}, u32[]{:S(2)}, u32[]{:S(2)}) collective-permute-start(bf16[320,128]{1,0:T(8,128)(2,1)S(1)} %get-tuple-element.79), channel_id=1, source_target_pairs={{0,1},{1,0},{2,3},{3,2},{4,5},{5,4},{6,7},{7,6},{8,9},{9,8},{10,11... | collective-permute-start | bytes 245768 | tf_op jit(solution)/shard_map/ppermute | solution.py:513
  50.4 0.1 copy.86
  50.5 0.9 reshape.87.w3b
  51.4 0.2 copy.87.w4f
  51.7 2.7 %collective-permute-done.7.in1 = bf16[320,128]{1,0:T(8,128)(2,1)S(1)} collective-permute-done((bf16[320,128]{1,0:T(8,128)(2,1)S(1)}, bf16[320,128]{1,0:T(8,128)(2,1)S(1)}, u32[]{:S(2)}, u32[]{:S(2)}) %collective-permute-start.7) | collective-permute-done | bytes 81952 | tf_op jit(solution)/shard_map/ppermute | solution.py:513
  54.4 4.8 %shard_map.176 = (f32[128,128]{1,0:T(8,128)S(1)}, bf16[2,64,768]{2,1,0:T(8,128)(2,1)S(1)}, bf16[64,768]{1,0:T(8,128)(2,1)S(1)}, bf16[64,768]{1,0:T(8,128)(2,1)S(...) custom-call(s32[2]{0:T(128)S(1)} %pad_add_fusion.pos, ...), custom_call_target="tpu_custom_call" | custom-call | flops 4294967296 | bytes 1048576 | tf_op jit(solution)/shard_map/pallas_call | solution.py:160
  59.3 2.4 %shard_map.177 = bf16[8,288,128]{2,1,0:T(8,128)(2,1)} custom-call(s32[2]{0:T(128)S(1)} %pad_add_fusion.pos, bf16[6,576,256]{2,1,0:T(8,128)(2,1)S(1)} %get-tuple-element.31.field, bf16[2,128,256]{2,1,0:T(8,128)(2,1)S(1)} %get-tuple-element.32.own, bf16[2,64,768]{2,1,0:T(8,128)(2,1)S(1)} %get-tuple-element.33.d3, f32[128,128]{1,0:T(8,128)S(1)} %get-tuple-element.34.p4, ...), custom_call_target="tpu_custom_call" | custom-call | flops 2147483648 | bytes 1048576 | tf_op jit(solution)/shard_map/pallas_call | solution.py:160
  61.7 4.0 %all-to-all-start.1 = ((bf16[8,288,128]{2,1,0:T(8,128)(2,1)}), bf16[8,288,128]{2,1,0:T(8,128)(2,1)S(1)}, u32[]{:S(2)}, u32[]{:S(2)}) async-start(bf16[8,288,128]{2,1,0:T(8,128)(2,1)} %shard_map.177), calls=%async_computation.1 | async-start | bytes 1179648 | tf_op jit(solution)/shard_map/all_to_all | solution.py:657
  65.6 1.1 collective-permute-start.11
  66.7 6.7 %collective-permute-start.12 = (bf16[64,768]{1,0:T(8,128)(2,1)S(1)}, bf16[64,768]{1,0:T(8,128)(2,1)S(1)}, u32[]{:S(2)}, u32[]{:S(2)}) collective-permute-start(bf16[64,768]{1,0:T(8,128)(2,1)S(1)} %get-tuple-element.36), channel_id=1, source_target_pairs={{8,16},{24,32},{40,48},{56,64},{72,80},{88,96},{104,112},{120,128}... | collective-permute-start | bytes 294920 | tf_op jit(solution)/shard_map/ppermute | solution.py:513
  73.4 2.3 %collective-permute-done.12.far = bf16[64,768]{1,0:T(8,128)(2,1)S(1)} collective-permute-done((bf16[64,768]{1,0:T(8,128)(2,1)S(1)}, bf16[64,768]{1,0:T(8,128)(2,1)S(1)}, u32[]{:S(2)}, u32[]{:S(2)}) %collective-permute-start.12) | collective-permute-done | bytes 98336 | tf_op jit(solution)/shard_map/ppermute | solution.py:513
  75.7 3.3 %shard_map.178 = f32[160,128]{1,0:T(8,128)S(1)} custom-call(s32[2]{0:T(128)S(1)} %pad_add_fusion.pos, bf16[2,64,768]{2,1,0:T(8,128)(2,1)S(1)} %get-tuple-element.33.d3, bf16[64,768]{1,0:T(8,128)(2,1)S(1)} %collective-permute-done.11.near, bf16[64,768]{1,0:T(8,128)(2,1)S(1)} %collective-permute-done.12.far, bf16[32,1728]{1,0:T(8,128)(2,1)S(1)} %copy-done.1, ...), custom_call_target="tpu_custom_call" | custom-call | flops 4294967296 | bytes 1048576 | tf_op jit(solution)/shard_map/pallas_call | solution.py:160
  79.1 0.1 reduce_sum.30
  79.3 23.9 %all_to_all.25 = bf16[32,14,128]{2,1,0:T(8,128)(2,1)S(1)} all-to-all(bf16[32,14,128]{2,1,0:T(8,128)(2,1)S(1)} %pad_maximum_fusion.4), channel_id=1, replica_groups=mesh['gz'=32,'ch'=8] {'gz'}, dimensions={0} | all-to-all | bytes 229376 | tf_op jit(solution)/shard_map/all_to_all | solution.py:680
  103.2 9.5 %all_to_all.26 = bf16[8,5,128]{2,1,0:T(8,128)(2,1)S(1)} all-to-all(bf16[8,5,128]{2,1,0:T(8,128)(2,1)S(1)} %broadcast_in_dim.10), channel_id=1, replica_groups=mesh['gz'=32,'ch'=8] {'ch'}, dimensions={0} | all-to-all | bytes 20480 | tf_op jit(solution)/shard_map/all_to_all | solution.py:523
  112.7 0.7 broadcast_in_dim.11
  113.4 4.9 %all-to-all-start.4 = ((bf16[32,14,128]{2,1,0:T(8,128)(2,1)}), bf16[32,14,128]{2,1,0:T(8,128)(2,1)S(1)}, u32[]{:S(2)}, u32[]{:S(2)}) async-start(bf16[32,14,128]{2,1,0:T(8,128)(2,1)} %broadcast_in_dim.11), calls=%async_computation.4 | async-start | bytes 262144 | tf_op jit(solution)/shard_map/all_to_all | solution.py:523
  118.3 0.6 copy.89
  118.9 10.2 %all-to-all-done.4.whole = bf16[32,14,128]{2,1,0:T(8,128)(2,1)S(1)} async-done(((bf16[32,14,128]{2,1,0:T(8,128)(2,1)}), bf16[32,14,128]{2,1,0:T(8,128)(2,1)S(1)}, u32[]{:S(2)}, u32[]{:S(2)}) %all-to-all-start.4) | async-done | bytes 114720 | tf_op jit(solution)/shard_map/all_to_all | solution.py:523
  129.1 1.4 %shard_map.179 = (f32[216,128]{1,0:T(8,128)}, f32[27,4,64]{2,1,0:T(4,128)}, f32[3,144,32]{2,1,0:T(8,128)}) custom-call(s32[2]{0:T(128)S(1)} %pad_add_fusion.pos, bf16[32,14,128]{2,1,0:T(8,128)(2,1)S(1)} %all-to-all-done.4.whole), custom_call_target="tpu_custom_call" | custom-call | flops 1048576 | bytes 1048576 | tf_op jit(solution)/shard_map/pallas_call | solution.py:160
  (72 shorter events, 1.0 us)
Async XLA Ops:
  0.6 6.1 %copy-start = (bf16[128,8,3,3,3]{0,1,4,3,2:T(8,128)(2,1)S(1)}, bf16[128,8,3,3,3]{0,1,4,3,2:T(8,128)(2,1)}, u32[]{:S(2)}) copy-start(bf16[128,8,3,3,3]{0,1,4,3,2:T(8,128)(2,1)} %param.18) | copy-start | bytes 165892
  0.7 14.9 %copy-start.12 = (bf16[32,16,3,3,3]{0,1,4,3,2:T(8,128)(2,1)S(1)}, bf16[32,16,3,3,3]{0,1,4,3,2:T(8,128)(2,1)}, u32[]{:S(2)}) copy-start(bf16[32,16,3,3,3]{0,1,4,3,2:T(8,128)(2,1)} %param.16) | copy-start | bytes 82948
  1.9 5.0 %collective-permute-start = (bf16[8,3,16,128]{3,2,1,0:T(8,128)(2,1)S(1)}, bf16[8,3,16,128]{3,2,1,0:T(8,128)(2,1)S(1)}, u32[]{:S(2)}, u32[]{:S(2)}) collective-permute-start(bf16[8,3,16,128]{3,2,1,0:T(8,128)(2,1)S(1)} %get-tuple-element.68), channel_id=1, source_target_pairs={{0,1},{1,0},{2,3},{3,2},{4,5},{5,4},{6,7},{7,6},{8,9},{9,8},{10,11... | collective-permute-start | bytes 294920 | tf_op jit(solution)/shard_map/ppermute | solution.py:513
  4.4 2.4 %collective-permute-start.1 = (bf16[8,3,16,128]{3,2,1,0:T(8,128)(2,1)S(1)}, bf16[8,3,16,128]{3,2,1,0:T(8,128)(2,1)S(1)}, u32[]{:S(2)}, u32[]{:S(2)}) collective-permute-start(bf16[8,3,16,128]{3,2,1,0:T(8,128)(2,1)S(1)} %get-tuple-element.69), channel_id=1, source_target_pairs={{1,2},{3,4},{5,6},{2,1},{4,3},{6,5},{9,10},{11,12},{13,14},{10,9},... | collective-permute-start | bytes 294920 | tf_op jit(solution)/shard_map/ppermute | solution.py:513
  7.7 16.9 %all-to-all-start = ((bf16[8,178,128]{2,1,0:T(8,128)(2,1)}), bf16[8,178,128]{2,1,0:T(8,128)(2,1)S(1)}, u32[]{:S(2)}, u32[]{:S(2)}) async-start(bf16[8,178,128]{2,1,0:T(8,128)(2,1)} %broadcast_in_dim.8), calls=%async_computation | async-start | bytes 753664 | tf_op jit(solution)/shard_map/all_to_all | solution.py:572
  16.0 12.3 %copy-start.8 = (bf16[128,256]{1,0:T(8,128)(2,1)S(1)}, bf16[128,256]{1,0:T(8,128)(2,1)}, u32[]{:S(2)}) copy-start(bf16[128,256]{1,0:T(8,128)(2,1)} %constant.65.clone.shift3) | copy-start | bytes 196612
  16.1 12.3 %copy-start.9 = (bf16[256,128]{1,0:T(8,128)(2,1)S(1)}, bf16[256,128]{1,0:T(8,128)(2,1)}, u32[]{:S(2)}) copy-start(bf16[256,128]{1,0:T(8,128)(2,1)} %constant.64.clone.pool2) | copy-start | bytes 196612
  16.1 12.3 %copy-start.10 = (bf16[128,256]{1,0:T(8,128)(2,1)S(1)}, bf16[128,256]{1,0:T(8,128)(2,1)}, u32[]{:S(2)}) copy-start(bf16[128,256]{1,0:T(8,128)(2,1)} %constant.63.clone.shift2) | copy-start | bytes 196612
  16.1 12.2 %collective-permute-start.3 = (bf16[3,14,16,128]{3,2,1,0:T(8,128)(2,1)S(1)}, bf16[3,14,16,128]{3,2,1,0:T(8,128)(2,1)S(1)}, u32[]{:S(2)}, u32[]{:S(2)}) collective-permute-start(bf16[3,14,16,128]{3,2,1,0:T(8,128)(2,1)S(1)} %get-tuple-element.64), channel_id=1, source_target_pairs={{8,16},{24,32},{40,48},{56,64},{72,80},{88,96},{104,112},{120,128}... | collective-permute-start | bytes 516104 | tf_op jit(solution)/shard_map/ppermute | solution.py:513
  23.4 4.9 %collective-permute-start.2 = (bf16[3,14,16,128]{3,2,1,0:T(8,128)(2,1)S(1)}, bf16[3,14,16,128]{3,2,1,0:T(8,128)(2,1)S(1)}, u32[]{:S(2)}, u32[]{:S(2)}) collective-permute-start(bf16[3,14,16,128]{3,2,1,0:T(8,128)(2,1)S(1)} %get-tuple-element.65), channel_id=1, source_target_pairs={{0,8},{8,0},{16,24},{24,16},{32,40},{40,32},{48,56},{56,48},{64,72... | collective-permute-start | bytes 516104 | tf_op jit(solution)/shard_map/ppermute | solution.py:513
  24.7 8.3 %collective-permute-start.4 = (bf16[8,162,128]{2,0,1:T(8,128)(2,1)S(1)}, bf16[8,162,128]{2,0,1:T(8,128)(2,1)S(1)}, u32[]{:S(2)}, u32[]{:S(2)}) collective-permute-start(bf16[8,162,128]{2,0,1:T(8,128)(2,1)S(1)} %copy.91), channel_id=1, source_target_pairs={{0,8},{8,0},{16,24},{24,16},{32,40},{40,32},{48,56},{56,48},{64,72... | collective-permute-start | bytes 995336 | tf_op jit(solution)/shard_map/ppermute | solution.py:517
  32.9 0.8 copy-start.7
  34.9 6.3 %collective-permute-start.6 = (bf16[192,128]{1,0:T(8,128)(2,1)S(1)}, bf16[192,128]{1,0:T(8,128)(2,1)S(1)}, u32[]{:S(2)}, u32[]{:S(2)}) collective-permute-start(bf16[192,128]{1,0:T(8,128)(2,1)S(1)} %get-tuple-element.28.own3), channel_id=1, source_target_pairs={{8,16},{24,32},{40,48},{56,64},{72,80},{88,96},{104,112},{120,128}... | collective-permute-start | bytes 147464 | tf_op jit(solution)/shard_map/ppermute | solution.py:513
  37.8 3.5 %collective-permute-start.5 = (bf16[192,128]{1,0:T(8,128)(2,1)S(1)}, bf16[192,128]{1,0:T(8,128)(2,1)S(1)}, u32[]{:S(2)}, u32[]{:S(2)}) collective-permute-start(bf16[192,128]{1,0:T(8,128)(2,1)S(1)} %get-tuple-element.28.own3), channel_id=1, source_target_pairs={{0,8},{8,0},{16,24},{24,16},{32,40},{40,32},{48,56},{56,48},{64,72... | collective-permute-start | bytes 147464 | tf_op jit(solution)/shard_map/ppermute | solution.py:513
  38.0 16.4 %copy-start.2 = (bf16[640,512]{1,0:T(8,128)(2,1)S(1)}, bf16[640,512]{1,0:T(8,128)(2,1)}, u32[]{:S(2)}) copy-start(bf16[640,512]{1,0:T(8,128)(2,1)} %constant.68.clone.planes_of) | copy-start | bytes 1966084
  38.1 16.3 %copy-start.6 = (bf16[256,128]{1,0:T(8,128)(2,1)S(1)}, bf16[256,128]{1,0:T(8,128)(2,1)}, u32[]{:S(2)}) copy-start(bf16[256,128]{1,0:T(8,128)(2,1)} %constant.67.clone.pool4) | copy-start | bytes 196612
  41.9 9.7 %collective-permute-start.10 = (bf16[192,128]{1,0:T(8,128)(2,1)}, bf16[192,128]{1,0:T(8,128)(2,1)S(1)}, u32[]{:S(2)}, u32[]{:S(2)}) collective-permute-start(bf16[192,128]{1,0:T(8,128)(2,1)} %pad_maximum_fusion.8), channel_id=1, source_target_pairs={{2,4},{3,5},{4,2},{5,3},{10,12},{11,13},{12,10},{13,11},{18,20},{1... | collective-permute-start | bytes 147464 | tf_op jit(solution)/shard_map/ppermute | solution.py:513
  42.5 9.1 %collective-permute-start.9 = (bf16[192,128]{1,0:T(8,128)(2,1)}, bf16[192,128]{1,0:T(8,128)(2,1)S(1)}, u32[]{:S(2)}, u32[]{:S(2)}) collective-permute-start(bf16[192,128]{1,0:T(8,128)(2,1)} %pad_maximum_fusion.8), channel_id=1, source_target_pairs={{0,2},{1,3},{2,0},{3,1},{4,6},{5,7},{6,4},{7,5},{8,10},{9,11},{10,... | collective-permute-start | bytes 147464 | tf_op jit(solution)/shard_map/ppermute | solution.py:513
  46.8 4.8 %collective-permute-start.8 = (bf16[320,128]{1,0:T(8,128)(2,1)S(1)}, bf16[320,128]{1,0:T(8,128)(2,1)S(1)}, u32[]{:S(2)}, u32[]{:S(2)}) collective-permute-start(bf16[320,128]{1,0:T(8,128)(2,1)S(1)} %get-tuple-element.78), channel_id=1, source_target_pairs={{1,2},{3,4},{5,6},{2,1},{4,3},{6,5},{9,10},{11,12},{13,14},{10,9},... | collective-permute-start | bytes 245768 | tf_op jit(solution)/shard_map/ppermute | solution.py:513
  47.5 6.9 %collective-permute-start.7 = (bf16[320,128]{1,0:T(8,128)(2,1)S(1)}, bf16[320,128]{1,0:T(8,128)(2,1)S(1)}, u32[]{:S(2)}, u32[]{:S(2)}) collective-permute-start(bf16[320,128]{1,0:T(8,128)(2,1)S(1)} %get-tuple-element.79), channel_id=1, source_target_pairs={{0,1},{1,0},{2,3},{3,2},{4,5},{5,4},{6,7},{7,6},{8,9},{9,8},{10,11... | collective-permute-start | bytes 245768 | tf_op jit(solution)/shard_map/ppermute | solution.py:513
  59.2 16.5 %copy-start.1 = (bf16[32,1728]{1,0:T(8,128)(2,1)S(1)}, bf16[32,1728]{1,0:T(8,128)(2,1)}, u32[]{:S(2)}) copy-start(bf16[32,1728]{1,0:T(8,128)(2,1)} %reshape.87.w3b) | copy-start | bytes 331780
  59.2 16.5 %copy-start.3 = (bf16[256,384]{1,0:T(8,128)(2,1)S(1)}, bf16[256,384]{1,0:T(8,128)(2,1)}, u32[]{:S(2)}) copy-start(bf16[256,384]{1,0:T(8,128)(2,1)} %constant.71.clone.cross) | copy-start | bytes 589828
  59.2 16.5 %copy-start.4 = (bf16[128,384]{1,0:T(8,128)(2,1)S(1)}, bf16[128,384]{1,0:T(8,128)(2,1)}, u32[]{:S(2)}) copy-start(bf16[128,384]{1,0:T(8,128)(2,1)} %constant.70.clone.straight) | copy-start | bytes 294916
  59.3 16.5 %copy-start.5 = (bf16[128,256]{1,0:T(8,128)(2,1)S(1)}, bf16[128,256]{1,0:T(8,128)(2,1)}, u32[]{:S(2)}) copy-start(bf16[128,256]{1,0:T(8,128)(2,1)} %constant.72.clone.spread2) | copy-start | bytes 196612
  59.3 16.5 %copy-start.11 = (bf16[4,128,512]{2,1,0:T(8,128)(2,1)S(1)}, bf16[4,128,512]{2,1,0:T(8,128)(2,1)}, u32[]{:S(2)}) copy-start(bf16[4,128,512]{2,1,0:T(8,128)(2,1)} %get-tuple-element.37.sl2) | copy-start | bytes 1572868
  61.7 17.4 %all-to-all-start.1 = ((bf16[8,288,128]{2,1,0:T(8,128)(2,1)}), bf16[8,288,128]{2,1,0:T(8,128)(2,1)S(1)}, u32[]{:S(2)}, u32[]{:S(2)}) async-start(bf16[8,288,128]{2,1,0:T(8,128)(2,1)} %shard_map.177), calls=%async_computation.1 | async-start | bytes 1179648 | tf_op jit(solution)/shard_map/all_to_all | solution.py:657
  65.6 7.7 %collective-permute-start.11 = (bf16[64,768]{1,0:T(8,128)(2,1)S(1)}, bf16[64,768]{1,0:T(8,128)(2,1)S(1)}, u32[]{:S(2)}, u32[]{:S(2)}) collective-permute-start(bf16[64,768]{1,0:T(8,128)(2,1)S(1)} %get-tuple-element.35), channel_id=1, source_target_pairs={{0,8},{8,0},{16,24},{24,16},{32,40},{40,32},{48,56},{56,48},{64,72... | collective-permute-start | bytes 294920 | tf_op jit(solution)/shard_map/ppermute | solution.py:513
  66.7 9.0 %collective-permute-start.12 = (bf16[64,768]{1,0:T(8,128)(2,1)S(1)}, bf16[64,768]{1,0:T(8,128)(2,1)S(1)}, u32[]{:S(2)}, u32[]{:S(2)}) collective-permute-start(bf16[64,768]{1,0:T(8,128)(2,1)S(1)} %get-tuple-element.36), channel_id=1, source_target_pairs={{8,16},{24,32},{40,48},{56,64},{72,80},{88,96},{104,112},{120,128}... | collective-permute-start | bytes 294920 | tf_op jit(solution)/shard_map/ppermute | solution.py:513
  113.4 15.7 %all-to-all-start.4 = ((bf16[32,14,128]{2,1,0:T(8,128)(2,1)}), bf16[32,14,128]{2,1,0:T(8,128)(2,1)S(1)}, u32[]{:S(2)}, u32[]{:S(2)}) async-start(bf16[32,14,128]{2,1,0:T(8,128)(2,1)} %broadcast_in_dim.11), calls=%async_computation.4 | async-start | bytes 262144 | tf_op jit(solution)/shard_map/all_to_all | solution.py:523

commit v4 on v3

--- a/solution.py
+++ b/solution.py
@@ -79,15 +79,13 @@
 
 
 def shift_planes():
-    out = np.zeros((8, 32, 3, 3, 8, 32), np.float32)
-    for ky in range(3):
-        for kx in range(3):
-            for y in range(8):
-                for x in range(32):
-                    sy, sx = y + ky, x + kx - 1
-                    if sy < 8 and 0 <= sx < 32:
-                        out[sy, sx, ky, kx, y, x] = 1
-    return out.reshape(256, 2304)
+    out = np.zeros((8, 32, 3, 8, 32), np.float32)
+    for kx in range(3):
+        for y in range(8):
+            for x in range(32):
+                if 0 <= x + kx - 1 < 32:
+                    out[y, x + kx - 1, kx, y, x] = 1
+    return out.reshape(256, 768)
 
 
 def pool_four():
@@ -115,13 +113,6 @@
     return out.reshape(128, 256)
 
 
-def deep_matrices():
-    out = np.zeros((768, 2304), np.float32)
-    out[:256] = shift_planes()
-    out[256:768, :768] = spread_three()
-    return out
-
-
 def const(build):
     return jnp.asarray(build(), BF)
 
@@ -132,6 +123,14 @@
 
 def dot_nt(a, b):
     return lax.dot_general(a, b, (((1,), (1,)), ((), ())), preferred_element_type=F32)
+
+
+def fold_rows(parts):
+    third = parts.shape[0] // 3
+    total = parts[:third]
+    for ky in (1, 2):
+        total = total + pltpu.roll(parts[ky * third : (ky + 1) * third], 256 - 32 * ky, 1)
+    return total
 
 
 def sigmoid(u):
@@ -170,13 +169,6 @@
     )(*args)
 
 
-def copies(pairs, sems):
-    out = [pltpu.make_async_copy(a, b, sems.at[n]) for n, (a, b) in enumerate(pairs)]
-    for copy in out:
-        copy.start()
-    return out
-
-
 def shallow_forward_kernel(
     pos, near, mid, far, w2, shift2, pool2, shift3, vq, sl2_far, vx_far, sums, sl2, vx, sems
 ):
@@ -209,7 +201,7 @@
     vx_copy.start()
     filters = w2[...]
 
-    @pl.loop(0, 6, unroll=2)
+    @pl.loop(0, 6, unroll=3)
     def _(zc):
         zg = 4 * gz + zc - 1
         z_in = jnp.logical_and(zg >= 0, zg < 128)
@@ -285,13 +277,12 @@
 
 
 def deep_kernel(
-    pos, own3, near, far, in1, out1, in2, out2, w4f, w4b, pool4, sl3, planes_of, w3b, matrices,
-    p4, d3, near_out, far_out, field, own,
-    planes, back_in, shift4, spread3, sems,
+    pos, own3, near, far, in1, out1, in2, out2, w4f, w4b, pool4, sl3, planes_of, shift4, w3b, spread_far,
+    p4, near_out, far_out, field, own,
+    planes, back_in, d3, spread3, sems,
 ):
-    shift_copy, spread_copy = copies(
-        ((matrices.at[0:256], shift4), (matrices.at[256:768, 0:768], spread3)), sems
-    )
+    spread_copy = pltpu.make_async_copy(spread_far, spread3, sems.at[0])
+    spread_copy.start()
     odd, ch = pos[0] % 2, pos[1]
 
     def pick(cond, one, two):
@@ -320,11 +311,10 @@
         for zz in range(2):
             p = 2 * zb + zz
             planes[p * 64 : p * 64 + 64] = flat[zb * 64 : zb * 64 + 64, zz * 256 : zz * 256 + 256]
-    shift_copy.wait()
-    for k in range(9):
-        moved = dot(planes[...], shift4[:, k * 256 : k * 256 + 256]).astype(BF)
+    for kx in range(3):
+        moved = dot(planes[...], shift4[:, kx * 256 : kx * 256 + 256]).astype(BF)
         for p in range(6):
-            field[p, k * 64 : k * 64 + 64] = moved[p * 64 : p * 64 + 64]
+            field[p, kx * 64 : kx * 64 + 64] = moved[p * 64 : p * 64 + 64]
 
     row = lax.broadcasted_iota(jnp.int32, (128, 256), 0)
     lane = lax.broadcasted_iota(jnp.int32, (128, 256), 1)
@@ -338,7 +328,7 @@
     pooled = None
     deltas = []
     for z in range(4):
-        pre = dot(filters, field[z : z + 3].reshape(1728, 256))
+        pre = fold_rows(dot(filters, field[z : z + 3].reshape(576, 256)))
         s = sigmoid(pre)
         wide = dot(cots[(z + 1) // 2], spread)
         delta = wide * slope_of(pre, s)
@@ -352,13 +342,14 @@
     p4[...] = dot(high, pool4[...]) + dot(low, pool4[...])
 
     stacked = jnp.concatenate(deltas, axis=0)
-    for k in range(9):
-        moved = dot(stacked, shift4[:, k * 256 : k * 256 + 256]).astype(BF)
+    for kx in range(3):
+        moved = dot(stacked, shift4[:, kx * 256 : kx * 256 + 256]).astype(BF)
         for z in range(4):
-            back_in[z, k * 128 : k * 128 + 128] = moved[z * 128 : z * 128 + 128]
+            back_in[z, kx * 128 : kx * 128 + 128] = moved[z * 128 : z * 128 + 128]
     filters = w4b[...]
     back = [
-        dot(filters, back_in[z : z + 3].reshape(3456, 256)).astype(BF) for z in range(2)
+        fold_rows(dot(filters, back_in[z : z + 3].reshape(1152, 256))).astype(BF)
+        for z in range(2)
     ]
     spread_copy.wait()
     wide = dot(jnp.concatenate(back, axis=1), spread3[...])
@@ -380,22 +371,36 @@
     far_out[...] = d3[odd]
 
 
-def grads_kernel(pos, field, own, d3, p4, vq, sent, out):
-    right = jnp.concatenate([own[0], own[1]], axis=1)
+def own_packs(pos, near, far):
+    odd = pos[0] % 2 == 1
+    one, two = near[...].astype(F32), far[...].astype(F32)
+    return jnp.where(odd, one, two).astype(BF), jnp.where(odd, two, one).astype(BF)
+
+
+def grads_kernel(pos, field, own, near, far, p4, vq, sent, out):
+    packs = own_packs(pos, near, far)
+    rows = []
+    for ky in range(3):
+        moved = [own[z].astype(F32) for z in range(2)]
+        if ky > 0:
+            moved = [pltpu.roll(m, 32 * ky, 1) for m in moved]
+        rows.append(jnp.concatenate([m.astype(BF) for m in moved], axis=1))
+    right = jnp.concatenate(rows, axis=0)
     for kz in range(3):
         left = jnp.concatenate([field[1 + kz], field[2 + kz]], axis=1)
         res = dot_nt(left, right)
         for k in range(9):
             for c in range(8):
                 at = (kz * 9 + k) * 8
-                out[c, at : at + 8] = res[k * 64 + c * 8 : k * 64 + c * 8 + 8]
+                row, lane = k % 3 * 64 + c * 8, k // 3 * 128
+                out[c, at : at + 8] = res[row : row + 8, lane : lane + 128]
     total = None
     zero = jnp.zeros((64, 512), BF)
     for j in range(4):
         rows = []
         for kz in range(3):
             zp = j - kz
-            rows.append(d3[zp, :, 128:640] if 0 <= zp < 2 else zero)
+            rows.append(packs[zp][:, 128:640] if 0 <= zp < 2 else zero)
         left = jnp.concatenate(
             [vq[j, :, ky * 128 : ky * 128 + 512] for ky in range(3)], axis=0
         )
@@ -415,24 +420,20 @@
 
 
 def shallow_back_kernel(
-    pos, d3, near, far, w3b, straight, cross, spread2, sl2, vx_far,
+    pos, own_near, own_far, near, far, w3b, straight, cross, spread2, sl2, vx_far,
     g2, ds, d2, vx, sems,
 ):
     vx_copy = pltpu.make_async_copy(vx_far, vx, sems.at[0])
     vx_copy.start()
 
-    def rows_of(ref, lead=None):
-        parts = []
-        for y in range(6):
-            lanes = slice(y * 128, y * 128 + 128)
-            parts.append(ref[:, lanes] if lead is None else ref[lead, :, lanes])
-        return jnp.concatenate(parts, axis=0)
+    def rows_of(value):
+        return jnp.concatenate([value[:, y * 128 : y * 128 + 128] for y in range(6)], axis=0)
 
     odd = pos[0] % 2 == 1
     one, two = rows_of(near).astype(F32), rows_of(far).astype(F32)
     above = jnp.where(odd, one, two).astype(BF)
     below = jnp.where(odd, two, one).astype(BF)
-    first, second = rows_of(d3, 0), rows_of(d3, 1)
+    first, second = [rows_of(pack) for pack in own_packs(pos, own_near, own_far)]
     direct, across = straight[...], cross[...]
     sources = (
         (jnp.concatenate([above, second], axis=1), across),
@@ -452,17 +453,12 @@
     filters = w3b[...]
     backs = []
     for zp in range(2):
-        for q in range(2):
-            rhs = jnp.concatenate(
-                [
-                    ds[zp + kz, :, (2 * q + ky) * 128 : (2 * q + ky + 2) * 128]
-                    for kz in range(3)
-                    for ky in range(3)
-                ],
-                axis=0,
-            )
-            back = dot(filters, rhs).astype(BF)
-            backs += [back[:, :128], back[:, 128:]]
+        parts = dot(filters, ds[zp : zp + 3].reshape(576, 768))
+        for y in range(4):
+            back = parts[0:32, y * 128 : y * 128 + 128]
+            for ky in (1, 2):
+                back = back + parts[ky * 32 : ky * 32 + 32, (y + ky) * 128 : (y + ky + 1) * 128]
+            backs.append(back.astype(BF))
     wide = dot(jnp.concatenate(backs, axis=0), spread2[...])
     for zp in range(2):
         for y in range(4):
@@ -563,7 +559,6 @@
     )
     held = jnp.broadcast_to(held[None], (8, 178, 128))
     w2 = band(filters_two)
-    mid, held = lax.optimization_barrier((mid, held))
     near, far = swap(
         lax.dynamic_slice_in_dim(mid, 5 * (1 - odd_z), 3, 0),
         lax.dynamic_slice_in_dim(mid, 5 * odd_z, 3, 0),
@@ -579,9 +574,11 @@
     three = jnp.concatenate([first[:, 108:, :64], second[:, 108:, :64]], axis=1)
     three = three.reshape(8, 27, 4, 64)
     w3f = three.transpose(3, 1, 0, 2).reshape(64, 864)
-    w3b = three[:, ::-1].transpose(0, 2, 1, 3).reshape(32, 1728)
-    w4f = four.transpose(3, 1, 0, 2).reshape(128, 1728)
-    w4b = four[:, ::-1].transpose(0, 2, 1, 3).reshape(64, 3456)
+    back = three[:, ::-1].reshape(8, 3, 3, 3, 4, 64)
+    w3b = back.transpose(2, 0, 4, 1, 3, 5).reshape(96, 576)
+    w4f = four.reshape(8, 3, 3, 3, 8, 128).transpose(2, 5, 1, 3, 0, 4).reshape(384, 576)
+    back = four[:, ::-1].reshape(8, 3, 3, 3, 8, 128)
+    w4b = back.transpose(2, 0, 4, 1, 3, 5).reshape(192, 1152)
 
     vq, sl2, vx = call(
         shallow_forward_kernel,
@@ -615,6 +612,7 @@
         (pos, vq, w3f, const(pool_three), cots),
     )
     near, far = swap(sent, sent, "gz")
+    near, w4f, w4b, w3b = lax.optimization_barrier((near, w4f, w4b, w3b))
     planes = jnp.concatenate([near[:64], sent[:64], far[:64]], axis=0)
     in1, out1 = swap(
         jnp.concatenate([planes, edges[0]], axis=0),
@@ -622,37 +620,37 @@
         "ch",
     )
     in2, out2 = swap(planes, planes, "ch", 2)
-    p4, d3, near, far, field4, own4 = call(
+    p4, own_near, own_far, field4, own4 = call(
         deep_kernel,
         (
             shape((128, 128), F32),
-            shape((2, 64, 768), BF),
             shape((64, 768), BF),
             shape((64, 768), BF),
-            shape((6, 576, 256), BF),
+            shape((6, 192, 256), BF),
             shape((2, 128, 256), BF),
         ),
         [
             pltpu.VMEM((384, 256), BF),
-            pltpu.VMEM((4, 1152, 256), BF),
-            pltpu.VMEM((256, 2304), BF),
+            pltpu.VMEM((4, 384, 256), BF),
+            pltpu.VMEM((2, 64, 768), BF),
             pltpu.VMEM((512, 768), BF),
-            pltpu.SemaphoreType.DMA((2,)),
+            pltpu.SemaphoreType.DMA((1,)),
         ],
         1 << 32,
         (
             pos, sent, near, far, in1, out1, in2, out2,
-            w4f, w4b, const(pool_four), sl3, const(gather_planes), w3b, const(deep_matrices),
+            w4f, w4b, const(pool_four), sl3, const(gather_planes), const(shift_planes),
+            w3b, const(spread_three),
         ),
-        far_in=(13, 14),
-    )
-    near, far = swap(near, far, "gz")
+        far_in=(14, 15),
+    )
+    near, far = swap(own_near, own_far, "gz")
     (sent,) = call(
         grads_kernel,
         (shape((8, 288, 128), BF),),
         [pltpu.VMEM((8, 288, 128), F32)],
         1 << 31,
-        (pos, field4, own4, d3, p4, vq),
+        (pos, field4, own4, own_near, own_far, p4, vq),
     )
     got = lax.all_to_all(sent, "ch", 0, 0, tiled=True)
     grads = got.astype(F32).sum(axis=0).astype(BF)
@@ -669,10 +667,10 @@
         ],
         1 << 32,
         (
-            pos, d3, near, far, w3b,
+            pos, own_near, own_far, near, far, w3b,
             const(shift_straight), const(shift_cross), const(spread_two), sl2, vx,
         ),
-        far_in=(9,),
+        far_in=(10,),
     )
     pieces = jnp.concatenate(
         [grads.reshape(32, 9, 128), g2.astype(BF).reshape(32, 5, 128)], axis=1

time: 131 us -> 127 us (0.969)
  waiting for transfers between devices: 20.7 us -> 15.2 us
  local copies, waits for them, and re-layouts: 8.17 us -> 10.5 us
  starting transfers between devices: 47.7 us -> 49.3 us
    ppermute x12, waiting for transfers between devices: 10.5 us -> 5.04 us  [swap(): return (lax.ppermute(one, axis, inside), lax.ppermute(two, axis, outside))]
    ppermute x12, starting transfers between devices: 29.6 us -> 31.5 us  [swap(): return (lax.ppermute(one, axis, inside), lax.ppermute(two, axis, outside))]
    unnamed x28 -> x31, local copies, waits for them, and re-layouts: 2.25 us -> 3.16 us
  transfers between devices with their start and end apart: 16 -> 16, of which waited for: 5 -> 5; matrix products, arithmetic and copies ran while one was open for 4% -> 7% of each run, Pallas kernels for 6% -> 6%
where the time goes in v4:
time: 127 us
  starting transfers between devices  49.3 us (39%)
  blocking collectives  32.5 us (26%)
  Pallas kernels  16.7 us (13%)
  waiting for transfers between devices  15.2 us (12%)
  local copies, waits for them, and re-layouts  10.5 us (8%)
  between operations  1.32 us (1%)
    ppermute x12, starting transfers between devices, swap(): return (lax.ppermute(one, axis, inside), lax.ppermute(two, axis, outside))  31.5 us
    all_to_all x1, blocking collectives, body(): lax.all_to_all(pieces, 'gz', 0, 0, tiled=True).astype(F32).sum(axis=0)  22.7 us
    pallas_call x6, Pallas kernels, call(): pl.pallas_call(kernel, out_shape=tuple((pltpu.HBM(o.shape, o.dtype) if n...  16.7 us
    all_to_all x1, waiting for transfers between devices, to_all(): return lax.all_to_all(copies, axis, 0, 0, tiled=True)  10.2 us
    all_to_all x1, blocking collectives, to_all(): return lax.all_to_all(copies, axis, 0, 0, tiled=True)  9.78 us
    all_to_all x1, starting transfers between devices, body(): all_of = lax.all_to_all(held, 'ch', 0, 0, tiled=True)  7.08 us
    all_to_all x1, starting transfers between devices, to_all(): return lax.all_to_all(copies, axis, 0, 0, tiled=True)  5.08 us
    ppermute x12, waiting for transfers between devices, swap(): return (lax.ppermute(one, axis, inside), lax.ppermute(two, axis, outside))  5.04 us
  transfers between devices with their start and end apart: 16, of which 5 were waited for; matrix products, arithmetic and copies ran while one was open for 7% of the time, Pallas kernels for 6%

profile of v4, /device:TPU:1, one launch (start us, length us, event | category | flops | bytes accessed | tf_op | source)
XLA Modules:
  0.0 126.6 jit_solution(7264347787640112225)
XLA Ops:
  0.7 1.2 copy.106
  1.9 2.6 %collective-permute-start = (bf16[8,3,16,128]{3,2,1,0:T(8,128)(2,1)S(1)}, bf16[8,3,16,128]{3,2,1,0:T(8,128)(2,1)S(1)}, u32[]{:S(2)}, u32[]{:S(2)}) collective-permute-start(bf16[8,3,16,128]{3,2,1,0:T(8,128)(2,1)S(1)} %get-tuple-element.70), channel_id=1, source_target_pairs={{0,1},{1,0},{2,3},{3,2},{4,5},{5,4},{6,7},{7,6},{8,9},{9,8},{10,11... | collective-permute-start | bytes 294920 | tf_op jit(solution)/shard_map/ppermute | solution.py:509
  4.4 0.7 collective-permute-start.1
  5.1 0.9 reshape.82
  6.0 0.8 reshape.84
  6.8 0.8 broadcast_in_dim.8
  7.6 7.1 %all-to-all-start = ((bf16[8,178,128]{2,1,0:T(8,128)(2,1)}), bf16[8,178,128]{2,1,0:T(8,128)(2,1)S(1)}, u32[]{:S(2)}, u32[]{:S(2)}) async-start(bf16[8,178,128]{2,1,0:T(8,128)(2,1)} %broadcast_in_dim.8), calls=%async_computation | async-start | bytes 753664 | tf_op jit(solution)/shard_map/all_to_all | solution.py:567
  14.7 0.1 copy.84
  14.9 0.3 pad_bitcast_fusion.3
  15.3 6.3 %collective-permute-start.3 = (bf16[3,14,16,128]{3,2,1,0:T(8,128)(2,1)S(1)}, bf16[3,14,16,128]{3,2,1,0:T(8,128)(2,1)S(1)}, u32[]{:S(2)}, u32[]{:S(2)}) collective-permute-start(bf16[3,14,16,128]{3,2,1,0:T(8,128)(2,1)S(1)} %get-tuple-element.66), channel_id=1, source_target_pairs={{8,16},{24,32},{40,48},{56,64},{72,80},{88,96},{104,112},{120,128}... | collective-permute-start | bytes 516104 | tf_op jit(solution)/shard_map/ppermute | solution.py:509
  21.6 0.1 collective-permute-start.2
  21.7 0.5 pad_maximum_fusion
  22.3 0.5 reshape.86.w2
  22.9 1.4 %collective-permute-start.4 = (bf16[8,162,128]{2,0,1:T(8,128)(2,1)S(1)}, bf16[8,162,128]{2,0,1:T(8,128)(2,1)S(1)}, u32[]{:S(2)}, u32[]{:S(2)}) collective-permute-start(bf16[8,162,128]{2,0,1:T(8,128)(2,1)S(1)} %copy.100), channel_id=1, source_target_pairs={{0,8},{8,0},{16,24},{24,16},{32,40},{40,32},{48,56},{56,48},{64,72... | collective-permute-start | bytes 995336 | tf_op jit(solution)/shard_map/ppermute | solution.py:513
  24.3 2.0 %collective-permute-done.3.far = bf16[3,14,16,128]{3,2,1,0:T(8,128)(2,1)S(1)} collective-permute-done((bf16[3,14,16,128]{3,2,1,0:T(8,128)(2,1)S(1)}, bf16[3,14,16,128]{3,2,1,0:T(8,128)(2,1)S(1)}, u32[]{:S(2)}, u32[]{:S(2)}) %collective-permute-start.3) | collective-permute-done | bytes 172064 | tf_op jit(solution)/shard_map/ppermute | solution.py:509
  26.3 4.4 %shard_map.183 = (bf16[4,96,768]{2,1,0:T(8,128)(2,1)S(1)}, bf16[4,128,512]{2,1,0:T(8,128)(2,1)}, bf16[10,48,1280]{2,1,0:T(8,128)(2,1)}) custom-call(s32[2]{0:T(128)S(1)} %pad_add_fusion.pos, bf16[3,14,16,128]{3,2,1,0:T(8,128)(2,1)S(1)} %collective-permute-done.2.near, bf16[8,14,16,128]{3,2,1,0:T(8,128)(2,1)S(1)} %pad_maximum_fusion.1.mid, ...), custom_call_target="tpu_custom_call" | custom-call | flops 4294967296 | bytes 1048576 | tf_op jit(solution)/shard_map/pallas_call | solution.py:159
  31.0 0.1 copy.88
  31.1 0.1 copy.89.w3
  31.2 0.5 copy-done.8
  31.6 1.2 shard_map.184
  32.8 3.0 %collective-permute-start.6 = (bf16[192,128]{1,0:T(8,128)(2,1)S(1)}, bf16[192,128]{1,0:T(8,128)(2,1)S(1)}, u32[]{:S(2)}, u32[]{:S(2)}) collective-permute-start(bf16[192,128]{1,0:T(8,128)(2,1)S(1)} %get-tuple-element.27.own3), channel_id=1, source_target_pairs={{8,16},{24,32},{40,48},{56,64},{72,80},{88,96},{104,112},{120,128}... | collective-permute-start | bytes 147464 | tf_op jit(solution)/shard_map/ppermute | solution.py:509
  35.8 0.1 collective-permute-start.5
  36.0 0.2 copy.94
  36.2 0.9 reshape.95.w3b
  37.3 0.4 copy.91
  37.7 0.8 copy.105
  38.5 0.6 collective-permute-done.6.far
  39.1 0.7 collective-permute-start.8
  39.8 4.5 %collective-permute-start.7 = (bf16[320,128]{1,0:T(8,128)(2,1)S(1)}, bf16[320,128]{1,0:T(8,128)(2,1)S(1)}, u32[]{:S(2)}, u32[]{:S(2)}) collective-permute-start(bf16[320,128]{1,0:T(8,128)(2,1)S(1)} %get-tuple-element.81), channel_id=1, source_target_pairs={{0,1},{1,0},{2,3},{3,2},{4,5},{5,4},{6,7},{7,6},{8,9},{9,8},{10,11... | collective-permute-start | bytes 245768 | tf_op jit(solution)/shard_map/ppermute | solution.py:509
  44.3 0.7 collective-permute-start.10
  45.0 3.7 %collective-permute-start.9 = (bf16[192,128]{1,0:T(8,128)(2,1)S(1)}, bf16[192,128]{1,0:T(8,128)(2,1)S(1)}, u32[]{:S(2)}, u32[]{:S(2)}) collective-permute-start(bf16[192,128]{1,0:T(8,128)(2,1)S(1)} %pad_maximum_fusion.8), channel_id=1, source_target_pairs={{0,2},{1,3},{2,0},{3,1},{4,6},{5,7},{6,4},{7,5},{8,10},{9,11},{10,... | collective-permute-start | bytes 147464 | tf_op jit(solution)/shard_map/ppermute | solution.py:509
  48.6 1.3 copy.95.w4f
  49.9 0.2 collective-permute-done.9.in2
  50.2 4.1 %shard_map.185 = (f32[128,128]{1,0:T(8,128)S(1)}, bf16[64,768]{1,0:T(8,128)(2,1)S(1)}, bf16[64,768]{1,0:T(8,128)(2,1)S(1)}, bf16[6,192,256]{2,1,0:T(8,128)(2,1)S(1)}, bf16[2,128,256]{2,1,0:T(8,128)(2,1)S(1)}) custom-call(s32[2]{0:T(128)S(1)} %pad_add_fusion.pos, bf16[192,128]{1,0:T(8,128)(2,1)S(1)} %get-tuple-element.27.own3, ...), custom_call_target="tpu_custom_call" | custom-call | flops 4294967296 | bytes 1048576 | tf_op jit(solution)/shard_map/pallas_call | solution.py:159
  54.3 2.4 %shard_map.186 = bf16[8,288,128]{2,1,0:T(8,128)(2,1)} custom-call(s32[2]{0:T(128)S(1)} %pad_add_fusion.pos, bf16[6,192,256]{2,1,0:T(8,128)(2,1)S(1)} %get-tuple-element.34.field, bf16[2,128,256]{2,1,0:T(8,128)(2,1)S(1)} %get-tuple-element.35.own, bf16[64,768]{1,0:T(8,128)(2,1)S(1)} %get-tuple-element.36.near.own_near, ...), custom_call_target="tpu_custom_call" | custom-call | flops 2147483648 | bytes 1048576 | tf_op jit(solution)/shard_map/pallas_call | solution.py:159
  56.7 4.2 %all-to-all-start.1 = ((bf16[8,288,128]{2,1,0:T(8,128)(2,1)}), bf16[8,288,128]{2,1,0:T(8,128)(2,1)S(1)}, u32[]{:S(2)}, u32[]{:S(2)}) async-start(bf16[8,288,128]{2,1,0:T(8,128)(2,1)} %shard_map.186), calls=%async_computation.1 | async-start | bytes 1179648 | tf_op jit(solution)/shard_map/all_to_all | solution.py:655
  60.9 2.6 %collective-permute-start.11 = (bf16[64,768]{1,0:T(8,128)(2,1)S(1)}, bf16[64,768]{1,0:T(8,128)(2,1)S(1)}, u32[]{:S(2)}, u32[]{:S(2)}) collective-permute-start(bf16[64,768]{1,0:T(8,128)(2,1)S(1)} %get-tuple-element.36.near.own_near), channel_id=1, source_target_pairs={{0,8},{8,0},{16,24},{24,16},{32,40},{40,32},{48,56},{56,48},{64,72... | collective-permute-start | bytes 294920 | tf_op jit(solution)/shard_map/ppermute | solution.py:509
  63.5 6.8 %collective-permute-start.12 = (bf16[64,768]{1,0:T(8,128)(2,1)S(1)}, bf16[64,768]{1,0:T(8,128)(2,1)S(1)}, u32[]{:S(2)}, u32[]{:S(2)}) collective-permute-start(bf16[64,768]{1,0:T(8,128)(2,1)S(1)} %get-tuple-element.37.far.own_far), channel_id=1, source_target_pairs={{8,16},{24,32},{40,48},{56,64},{72,80},{88,96},{104,112},{120,128}... | collective-permute-start | bytes 294920 | tf_op jit(solution)/shard_map/ppermute | solution.py:509
  70.3 2.3 %collective-permute-done.12.far = bf16[64,768]{1,0:T(8,128)(2,1)S(1)} collective-permute-done((bf16[64,768]{1,0:T(8,128)(2,1)S(1)}, bf16[64,768]{1,0:T(8,128)(2,1)S(1)}, u32[]{:S(2)}, u32[]{:S(2)}) %collective-permute-start.12) | collective-permute-done | bytes 98336 | tf_op jit(solution)/shard_map/ppermute | solution.py:509
  72.6 3.2 %shard_map.187 = f32[160,128]{1,0:T(8,128)S(1)} custom-call(s32[2]{0:T(128)S(1)} %pad_add_fusion.pos, bf16[64,768]{1,0:T(8,128)(2,1)S(1)} %get-tuple-element.36.near.own_near, bf16[64,768]{1,0:T(8,128)(2,1)S(1)} %get-tuple-element.37.far.own_far, bf16[64,768]{1,0:T(8,128)(2,1)S(1)} %collective-permute-done.11.near, ...), custom_call_target="tpu_custom_call" | custom-call | flops 4294967296 | bytes 1048576 | tf_op jit(solution)/shard_map/pallas_call | solution.py:159
  75.8 0.1 reduce_sum.30
  76.0 22.7 %all_to_all.25 = bf16[32,14,128]{2,1,0:T(8,128)(2,1)S(1)} all-to-all(bf16[32,14,128]{2,1,0:T(8,128)(2,1)S(1)} %pad_maximum_fusion.4), channel_id=1, replica_groups=mesh['gz'=32,'ch'=8] {'gz'}, dimensions={0} | all-to-all | bytes 229376 | tf_op jit(solution)/shard_map/all_to_all | solution.py:678
  98.8 9.8 %all_to_all.26 = bf16[8,5,128]{2,1,0:T(8,128)(2,1)S(1)} all-to-all(bf16[8,5,128]{2,1,0:T(8,128)(2,1)S(1)} %broadcast_in_dim.10), channel_id=1, replica_groups=mesh['gz'=32,'ch'=8] {'ch'}, dimensions={0} | all-to-all | bytes 20480 | tf_op jit(solution)/shard_map/all_to_all | solution.py:519
  108.6 0.7 broadcast_in_dim.11
  109.3 5.1 %all-to-all-start.4 = ((bf16[32,14,128]{2,1,0:T(8,128)(2,1)}), bf16[32,14,128]{2,1,0:T(8,128)(2,1)S(1)}, u32[]{:S(2)}, u32[]{:S(2)}) async-start(bf16[32,14,128]{2,1,0:T(8,128)(2,1)} %broadcast_in_dim.11), calls=%async_computation.4 | async-start | bytes 262144 | tf_op jit(solution)/shard_map/all_to_all | solution.py:519
  114.4 0.6 copy.97
  115.0 10.2 %all-to-all-done.4.whole = bf16[32,14,128]{2,1,0:T(8,128)(2,1)S(1)} async-done(((bf16[32,14,128]{2,1,0:T(8,128)(2,1)}), bf16[32,14,128]{2,1,0:T(8,128)(2,1)S(1)}, u32[]{:S(2)}, u32[]{:S(2)}) %all-to-all-start.4) | async-done | bytes 114720 | tf_op jit(solution)/shard_map/all_to_all | solution.py:519
  125.1 1.4 %shard_map.188 = (f32[216,128]{1,0:T(8,128)}, f32[27,4,64]{2,1,0:T(4,128)}, f32[3,144,32]{2,1,0:T(8,128)}) custom-call(s32[2]{0:T(128)S(1)} %pad_add_fusion.pos, bf16[32,14,128]{2,1,0:T(8,128)(2,1)S(1)} %all-to-all-done.4.whole), custom_call_target="tpu_custom_call" | custom-call | flops 1048576 | bytes 1048576 | tf_op jit(solution)/shard_map/pallas_call | solution.py:159
  (76 shorter events, 1.1 us)
Async XLA Ops:
  0.6 6.1 %copy-start = (bf16[128,8,3,3,3]{0,1,4,3,2:T(8,128)(2,1)S(1)}, bf16[128,8,3,3,3]{0,1,4,3,2:T(8,128)(2,1)}, u32[]{:S(2)}) copy-start(bf16[128,8,3,3,3]{0,1,4,3,2:T(8,128)(2,1)} %param.19) | copy-start | bytes 165892
  0.7 14.0 %copy-start.13 = (bf16[32,16,3,3,3]{0,1,4,3,2:T(8,128)(2,1)S(1)}, bf16[32,16,3,3,3]{0,1,4,3,2:T(8,128)(2,1)}, u32[]{:S(2)}) copy-start(bf16[32,16,3,3,3]{0,1,4,3,2:T(8,128)(2,1)} %param.17) | copy-start | bytes 82948
  1.9 13.2 %collective-permute-start = (bf16[8,3,16,128]{3,2,1,0:T(8,128)(2,1)S(1)}, bf16[8,3,16,128]{3,2,1,0:T(8,128)(2,1)S(1)}, u32[]{:S(2)}, u32[]{:S(2)}) collective-permute-start(bf16[8,3,16,128]{3,2,1,0:T(8,128)(2,1)S(1)} %get-tuple-element.70), channel_id=1, source_target_pairs={{0,1},{1,0},{2,3},{3,2},{4,5},{5,4},{6,7},{7,6},{8,9},{9,8},{10,11... | collective-permute-start | bytes 294920 | tf_op jit(solution)/shard_map/ppermute | solution.py:509
  4.4 10.7 %collective-permute-start.1 = (bf16[8,3,16,128]{3,2,1,0:T(8,128)(2,1)S(1)}, bf16[8,3,16,128]{3,2,1,0:T(8,128)(2,1)S(1)}, u32[]{:S(2)}, u32[]{:S(2)}) collective-permute-start(bf16[8,3,16,128]{3,2,1,0:T(8,128)(2,1)S(1)} %get-tuple-element.71), channel_id=1, source_target_pairs={{1,2},{3,4},{5,6},{2,1},{4,3},{6,5},{9,10},{11,12},{13,14},{10,9},... | collective-permute-start | bytes 294920 | tf_op jit(solution)/shard_map/ppermute | solution.py:509
  7.6 15.2 %all-to-all-start = ((bf16[8,178,128]{2,1,0:T(8,128)(2,1)}), bf16[8,178,128]{2,1,0:T(8,128)(2,1)S(1)}, u32[]{:S(2)}, u32[]{:S(2)}) async-start(bf16[8,178,128]{2,1,0:T(8,128)(2,1)} %broadcast_in_dim.8), calls=%async_computation | async-start | bytes 753664 | tf_op jit(solution)/shard_map/all_to_all | solution.py:567
  15.3 11.0 %collective-permute-start.3 = (bf16[3,14,16,128]{3,2,1,0:T(8,128)(2,1)S(1)}, bf16[3,14,16,128]{3,2,1,0:T(8,128)(2,1)S(1)}, u32[]{:S(2)}, u32[]{:S(2)}) collective-permute-start(bf16[3,14,16,128]{3,2,1,0:T(8,128)(2,1)S(1)} %get-tuple-element.66), channel_id=1, source_target_pairs={{8,16},{24,32},{40,48},{56,64},{72,80},{88,96},{104,112},{120,128}... | collective-permute-start | bytes 516104 | tf_op jit(solution)/shard_map/ppermute | solution.py:509
  21.6 4.7 %collective-permute-start.2 = (bf16[3,14,16,128]{3,2,1,0:T(8,128)(2,1)S(1)}, bf16[3,14,16,128]{3,2,1,0:T(8,128)(2,1)S(1)}, u32[]{:S(2)}, u32[]{:S(2)}) collective-permute-start(bf16[3,14,16,128]{3,2,1,0:T(8,128)(2,1)S(1)} %get-tuple-element.67), channel_id=1, source_target_pairs={{0,8},{8,0},{16,24},{24,16},{32,40},{40,32},{48,56},{56,48},{64,72... | collective-permute-start | bytes 516104 | tf_op jit(solution)/shard_map/ppermute | solution.py:509
  22.2 4.1 %copy-start.9 = (bf16[128,256]{1,0:T(8,128)(2,1)S(1)}, bf16[128,256]{1,0:T(8,128)(2,1)}, u32[]{:S(2)}) copy-start(bf16[128,256]{1,0:T(8,128)(2,1)} %constant.67.clone.shift3) | copy-start | bytes 196612
  22.2 4.0 %copy-start.10 = (bf16[256,128]{1,0:T(8,128)(2,1)S(1)}, bf16[256,128]{1,0:T(8,128)(2,1)}, u32[]{:S(2)}) copy-start(bf16[256,128]{1,0:T(8,128)(2,1)} %constant.66.clone.pool2) | copy-start | bytes 196612
  22.3 4.0 %copy-start.11 = (bf16[128,256]{1,0:T(8,128)(2,1)S(1)}, bf16[128,256]{1,0:T(8,128)(2,1)}, u32[]{:S(2)}) copy-start(bf16[128,256]{1,0:T(8,128)(2,1)} %constant.65.clone.shift2) | copy-start | bytes 196612
  22.9 7.8 %collective-permute-start.4 = (bf16[8,162,128]{2,0,1:T(8,128)(2,1)S(1)}, bf16[8,162,128]{2,0,1:T(8,128)(2,1)S(1)}, u32[]{:S(2)}, u32[]{:S(2)}) collective-permute-start(bf16[8,162,128]{2,0,1:T(8,128)(2,1)S(1)} %copy.100), channel_id=1, source_target_pairs={{0,8},{8,0},{16,24},{24,16},{32,40},{40,32},{48,56},{56,48},{64,72... | collective-permute-start | bytes 995336 | tf_op jit(solution)/shard_map/ppermute | solution.py:513
  30.8 0.8 copy-start.8
  32.8 6.3 %collective-permute-start.6 = (bf16[192,128]{1,0:T(8,128)(2,1)S(1)}, bf16[192,128]{1,0:T(8,128)(2,1)S(1)}, u32[]{:S(2)}, u32[]{:S(2)}) collective-permute-start(bf16[192,128]{1,0:T(8,128)(2,1)S(1)} %get-tuple-element.27.own3), channel_id=1, source_target_pairs={{8,16},{24,32},{40,48},{56,64},{72,80},{88,96},{104,112},{120,128}... | collective-permute-start | bytes 147464 | tf_op jit(solution)/shard_map/ppermute | solution.py:509
  35.8 2.7 %collective-permute-start.5 = (bf16[192,128]{1,0:T(8,128)(2,1)S(1)}, bf16[192,128]{1,0:T(8,128)(2,1)S(1)}, u32[]{:S(2)}, u32[]{:S(2)}) collective-permute-start(bf16[192,128]{1,0:T(8,128)(2,1)S(1)} %get-tuple-element.27.own3), channel_id=1, source_target_pairs={{0,8},{8,0},{16,24},{24,16},{32,40},{40,32},{48,56},{56,48},{64,72... | collective-permute-start | bytes 147464 | tf_op jit(solution)/shard_map/ppermute | solution.py:509
  37.7 12.5 %copy-start.2 = (bf16[640,512]{1,0:T(8,128)(2,1)S(1)}, bf16[640,512]{1,0:T(8,128)(2,1)}, u32[]{:S(2)}) copy-start(bf16[640,512]{1,0:T(8,128)(2,1)} %constant.70.clone.planes_of) | copy-start | bytes 1966084
  37.7 12.5 %copy-start.3 = (bf16[256,768]{1,0:T(8,128)(2,1)S(1)}, bf16[256,768]{1,0:T(8,128)(2,1)}, u32[]{:S(2)}) copy-start(bf16[256,768]{1,0:T(8,128)(2,1)} %constant.71.clone.shift4) | copy-start | bytes 1179652
  37.7 12.5 %copy-start.7 = (bf16[256,128]{1,0:T(8,128)(2,1)S(1)}, bf16[256,128]{1,0:T(8,128)(2,1)}, u32[]{:S(2)}) copy-start(bf16[256,128]{1,0:T(8,128)(2,1)} %constant.69.clone.pool4) | copy-start | bytes 196612
  39.1 11.0 %collective-permute-start.8 = (bf16[320,128]{1,0:T(8,128)(2,1)S(1)}, bf16[320,128]{1,0:T(8,128)(2,1)S(1)}, u32[]{:S(2)}, u32[]{:S(2)}) collective-permute-start(bf16[320,128]{1,0:T(8,128)(2,1)S(1)} %get-tuple-element.80), channel_id=1, source_target_pairs={{1,2},{3,4},{5,6},{2,1},{4,3},{6,5},{9,10},{11,12},{13,14},{10,9},... | collective-permute-start | bytes 245768 | tf_op jit(solution)/shard_map/ppermute | solution.py:509
  39.8 10.3 %collective-permute-start.7 = (bf16[320,128]{1,0:T(8,128)(2,1)S(1)}, bf16[320,128]{1,0:T(8,128)(2,1)S(1)}, u32[]{:S(2)}, u32[]{:S(2)}) collective-permute-start(bf16[320,128]{1,0:T(8,128)(2,1)S(1)} %get-tuple-element.81), channel_id=1, source_target_pairs={{0,1},{1,0},{2,3},{3,2},{4,5},{5,4},{6,7},{7,6},{8,9},{9,8},{10,11... | collective-permute-start | bytes 245768 | tf_op jit(solution)/shard_map/ppermute | solution.py:509
  44.3 5.6 %collective-permute-start.10 = (bf16[192,128]{1,0:T(8,128)(2,1)S(1)}, bf16[192,128]{1,0:T(8,128)(2,1)S(1)}, u32[]{:S(2)}, u32[]{:S(2)}) collective-permute-start(bf16[192,128]{1,0:T(8,128)(2,1)S(1)} %pad_maximum_fusion.8), channel_id=1, source_target_pairs={{2,4},{3,5},{4,2},{5,3},{10,12},{11,13},{12,10},{13,11},{18,20},{1... | collective-permute-start | bytes 147464 | tf_op jit(solution)/shard_map/ppermute | solution.py:509
  45.0 5.2 %collective-permute-start.9 = (bf16[192,128]{1,0:T(8,128)(2,1)S(1)}, bf16[192,128]{1,0:T(8,128)(2,1)S(1)}, u32[]{:S(2)}, u32[]{:S(2)}) collective-permute-start(bf16[192,128]{1,0:T(8,128)(2,1)S(1)} %pad_maximum_fusion.8), channel_id=1, source_target_pairs={{0,2},{1,3},{2,0},{3,1},{4,6},{5,7},{6,4},{7,5},{8,10},{9,11},{10,... | collective-permute-start | bytes 147464 | tf_op jit(solution)/shard_map/ppermute | solution.py:509
  54.3 18.3 %copy-start.1 = (bf16[96,576]{1,0:T(8,128)(2,1)S(1)}, bf16[96,576]{1,0:T(8,128)(2,1)}, u32[]{:S(2)}) copy-start(bf16[96,576]{1,0:T(8,128)(2,1)} %reshape.95.w3b) | copy-start | bytes 331780
  54.3 18.3 %copy-start.4 = (bf16[256,384]{1,0:T(8,128)(2,1)S(1)}, bf16[256,384]{1,0:T(8,128)(2,1)}, u32[]{:S(2)}) copy-start(bf16[256,384]{1,0:T(8,128)(2,1)} %constant.74.clone.cross) | copy-start | bytes 589828
  54.3 18.3 %copy-start.5 = (bf16[128,384]{1,0:T(8,128)(2,1)S(1)}, bf16[128,384]{1,0:T(8,128)(2,1)}, u32[]{:S(2)}) copy-start(bf16[128,384]{1,0:T(8,128)(2,1)} %constant.73.clone.straight) | copy-start | bytes 294916
  54.3 18.3 %copy-start.6 = (bf16[128,256]{1,0:T(8,128)(2,1)S(1)}, bf16[128,256]{1,0:T(8,128)(2,1)}, u32[]{:S(2)}) copy-start(bf16[128,256]{1,0:T(8,128)(2,1)} %constant.75.clone.spread2) | copy-start | bytes 196612
  54.3 18.3 %copy-start.12 = (bf16[4,128,512]{2,1,0:T(8,128)(2,1)S(1)}, bf16[4,128,512]{2,1,0:T(8,128)(2,1)}, u32[]{:S(2)}) copy-start(bf16[4,128,512]{2,1,0:T(8,128)(2,1)} %get-tuple-element.39.sl2) | copy-start | bytes 1572868
  56.7 19.1 %all-to-all-start.1 = ((bf16[8,288,128]{2,1,0:T(8,128)(2,1)}), bf16[8,288,128]{2,1,0:T(8,128)(2,1)S(1)}, u32[]{:S(2)}, u32[]{:S(2)}) async-start(bf16[8,288,128]{2,1,0:T(8,128)(2,1)} %shard_map.186), calls=%async_computation.1 | async-start | bytes 1179648 | tf_op jit(solution)/shard_map/all_to_all | solution.py:655
  60.9 9.4 %collective-permute-start.11 = (bf16[64,768]{1,0:T(8,128)(2,1)S(1)}, bf16[64,768]{1,0:T(8,128)(2,1)S(1)}, u32[]{:S(2)}, u32[]{:S(2)}) collective-permute-start(bf16[64,768]{1,0:T(8,128)(2,1)S(1)} %get-tuple-element.36.near.own_near), channel_id=1, source_target_pairs={{0,8},{8,0},{16,24},{24,16},{32,40},{40,32},{48,56},{56,48},{64,72... | collective-permute-start | bytes 294920 | tf_op jit(solution)/shard_map/ppermute | solution.py:509
  63.5 9.1 %collective-permute-start.12 = (bf16[64,768]{1,0:T(8,128)(2,1)S(1)}, bf16[64,768]{1,0:T(8,128)(2,1)S(1)}, u32[]{:S(2)}, u32[]{:S(2)}) collective-permute-start(bf16[64,768]{1,0:T(8,128)(2,1)S(1)} %get-tuple-element.37.far.own_far), channel_id=1, source_target_pairs={{8,16},{24,32},{40,48},{56,64},{72,80},{88,96},{104,112},{120,128}... | collective-permute-start | bytes 294920 | tf_op jit(solution)/shard_map/ppermute | solution.py:509
  109.3 15.9 %all-to-all-start.4 = ((bf16[32,14,128]{2,1,0:T(8,128)(2,1)}), bf16[32,14,128]{2,1,0:T(8,128)(2,1)S(1)}, u32[]{:S(2)}, u32[]{:S(2)}) async-start(bf16[32,14,128]{2,1,0:T(8,128)(2,1)} %broadcast_in_dim.11), calls=%async_computation.4 | async-start | bytes 262144 | tf_op jit(solution)/shard_map/all_to_all | solution.py:519

commit v5 on v4

--- a/solution.py
+++ b/solution.py
@@ -169,75 +169,100 @@
     )(*args)
 
 
-def shallow_forward_kernel(
-    pos, near, mid, far, w2, shift2, pool2, shift3, vq, sl2_far, vx_far, sums, sl2, vx, sems
-):
-    gz, ch = pos[0], pos[1]
+def shift_plane(field, shift, out):
+    sides = dot(field, shift)
+    for y in range(14):
+        lanes = slice(y * 128, y * 128 + 128)
+        rows = slice(y * 16, y * 16 + 16)
+        out[0:16, lanes] = sides[rows, :128].astype(BF)
+        out[16:32, lanes] = field[rows]
+        out[32:48, lanes] = sides[rows, 128:].astype(BF)
+
+
+def layer_two(pos, zc, planes, filters, sums, slopes):
+    zg = 4 * pos[0] + zc - 1
+    z_in = jnp.logical_and(zg >= 0, zg < 128)
+    for q, (ya, yb) in enumerate(((1, 2), (3, 4), (0, 5))):
+        rhs = jnp.concatenate(
+            [
+                jnp.concatenate(
+                    [
+                        plane[:, (2 * ya + yy) * 128 : (2 * ya + yy + 1) * 128],
+                        plane[:, (2 * yb + yy) * 128 : (2 * yb + yy + 1) * 128],
+                    ],
+                    axis=1,
+                )
+                for plane in planes
+                for yy in range(4)
+            ],
+            axis=0,
+        )
+        pre = dot(filters, rhs)
+        s = sigmoid(pre)
+        a = act_of(pre, s)
+        if q < 2 and slopes is not None:
+            slopes[:, q * 256 : q * 256 + 256] = slope_of(pre, s).astype(BF)
+        total = (a[0:32] + a[32:64]) + (a[64:96] + a[96:128])
+        for c, yc in enumerate((ya, yb)):
+            yg = 4 * pos[1] + yc - 1
+            inside = jnp.logical_and(z_in, jnp.logical_and(yg >= 0, yg < 32))
+            cell = jnp.where(inside, total[:, c * 128 : c * 128 + 128], 0.0)
+            sums[yc * 32 : yc * 32 + 32] = cell.astype(BF)
+
+
+def inner_forward_kernel(pos, mid, w2, shift2, sums, slopes_far, vx_far, vm, slopes, sems):
     shift = shift2[...]
 
-    odd = gz % 2 == 1
-    for which, first, count in ((0, 0, 3), (1, 3, 8), (2, 11, 3)):
-
-        @pl.loop(0, count, unroll=2 if count == 8 else 3)
-        def _(z):
-            if which == 1:
-                field = mid[z].reshape(224, 128)
-            else:
-                one, two = near[z].reshape(224, 128), far[z].reshape(224, 128)
-                if which == 2:
-                    one, two = two, one
-                field = jnp.where(odd, one.astype(F32), two.astype(F32)).astype(BF)
-            sides = dot(field, shift)
-            for y in range(14):
-                lanes = slice(y * 128, y * 128 + 128)
-                rows = slice(y * 16, y * 16 + 16)
-                vx[z + first, 0:16, lanes] = sides[rows, :128].astype(BF)
-                vx[z + first, 16:32, lanes] = field[rows]
-                vx[z + first, 32:48, lanes] = sides[rows, 128:].astype(BF)
-
-    vx_copy = pltpu.make_async_copy(
-        vx.at[2:12, :, 256:1536], vx_far, sems.at[0]
-    )
+    @pl.loop(0, 8, unroll=2)
+    def _(z):
+        shift_plane(mid[z].reshape(224, 128), shift, vm.at[z])
+
+    vx_copy = pltpu.make_async_copy(vm.at[:, :, 256:1536], vx_far, sems.at[0])
     vx_copy.start()
     filters = w2[...]
-
-    @pl.loop(0, 6, unroll=3)
-    def _(zc):
-        zg = 4 * gz + zc - 1
-        z_in = jnp.logical_and(zg >= 0, zg < 128)
-        for q, (ya, yb) in enumerate(((1, 2), (3, 4), (0, 5))):
-            rhs = jnp.concatenate(
-                [
-                    jnp.concatenate(
-                        [
-                            vx[2 * zc + zz, :, (2 * ya + yy) * 128 : (2 * ya + yy + 1) * 128],
-                            vx[2 * zc + zz, :, (2 * yb + yy) * 128 : (2 * yb + yy + 1) * 128],
-                        ],
-                        axis=1,
-                    )
-                    for zz in range(4)
-                    for yy in range(4)
-                ],
-                axis=0,
-            )
-            pre = dot(filters, rhs)
-            s = sigmoid(pre)
-            a = act_of(pre, s)
-            if q < 2:
-                sl2[zc, :, q * 256 : q * 256 + 256] = slope_of(pre, s).astype(BF)
-            total = (a[0:32] + a[32:64]) + (a[64:96] + a[96:128])
-            for c, yc in enumerate((ya, yb)):
-                yg = 4 * ch + yc - 1
-                inside = jnp.logical_and(z_in, jnp.logical_and(yg >= 0, yg < 32))
-                cell = jnp.where(inside, total[:, c * 128 : c * 128 + 128], 0.0)
-                sums[zc, yc * 32 : yc * 32 + 32] = cell.astype(BF)
-
-    sl2_copy = pltpu.make_async_copy(sl2.at[1:5], sl2_far, sems.at[1])
-    sl2_copy.start()
+    for n in range(2):
+        planes = [vm.at[1 + 2 * n + zz] for zz in range(4)]
+        layer_two(pos, n + 2, planes, filters, sums.at[n], slopes.at[n])
+    slopes_copy = pltpu.make_async_copy(slopes, slopes_far, sems.at[1])
+    slopes_copy.start()
+    vx_copy.wait()
+    slopes_copy.wait()
+
+
+def outer_forward_kernel(
+    pos, near, mid, far, inner, w2, shift2, pool2, shift3, vq, slopes_far, vx_far,
+    sums, slopes, vh, sems,
+):
+    odd = pos[0] % 2 == 1
+    shift = shift2[...]
+    for z in range(3):
+        one = near[z].reshape(224, 128).astype(F32)
+        two = far[z].reshape(224, 128).astype(F32)
+        shift_plane(jnp.where(odd, one, two).astype(BF), shift, vh.at[z])
+        shift_plane(jnp.where(odd, two, one).astype(BF), shift, vh.at[9 + z])
+        shift_plane(mid[z].reshape(224, 128), shift, vh.at[3 + z])
+        shift_plane(mid[5 + z].reshape(224, 128), shift, vh.at[6 + z])
+    late = [
+        pltpu.make_async_copy(vh.at[2, :, 256:1536], vx_far.at[0], sems.at[0]),
+        pltpu.make_async_copy(vh.at[9, :, 256:1536], vx_far.at[1], sems.at[1]),
+        pltpu.make_async_copy(slopes.at[0], slopes_far.at[0], sems.at[2]),
+        pltpu.make_async_copy(slopes.at[1], slopes_far.at[1], sems.at[3]),
+    ]
+    late[0].start()
+    late[1].start()
+    filters = w2[...]
+    held = [vh.at[z] for z in range(6)] + [None, None] + [vh.at[z] for z in range(6, 12)]
+    for zc, at, slot in ((1, 1, 0), (4, 2, 1), (0, 0, None), (5, 3, None)):
+        out = None if slot is None else slopes.at[slot]
+        layer_two(pos, zc, held[2 * zc : 2 * zc + 4], filters, sums.at[at], out)
+        if slot is not None:
+            late[2 + slot].start()
+
     pool = pool2[...]
     halves = shift3[...]
+    cells = [sums[0], sums[1], inner[0], inner[1], sums[2], sums[3]]
     for j in range(4):
-        pair = jnp.concatenate([sums[j], sums[j + 2]], axis=1)
+        pair = jnp.concatenate([cells[j], cells[j + 2]], axis=1)
         pooled = dot(pair, pool).astype(BF)
         sides = dot(pooled, halves)
         for y in range(6):
@@ -246,8 +271,8 @@
             vq[j, 0:32, lanes] = sides[rows, :128].astype(BF)
             vq[j, 32:64, lanes] = pooled[rows]
             vq[j, 64:96, lanes] = sides[rows, 128:].astype(BF)
-    vx_copy.wait()
-    sl2_copy.wait()
+    for copy in late:
+        copy.wait()
 
 
 def middle_forward_kernel(pos, vq, w3, pool3, cot, sent, edges, sl3):
@@ -420,11 +445,17 @@
 
 
 def shallow_back_kernel(
-    pos, own_near, own_far, near, far, w3b, straight, cross, spread2, sl2, vx_far,
+    pos, own_near, own_far, near, far, w3b, straight, cross, spread2, sl2_mid, sl2_edge, vx_mid, vx_edge,
     g2, ds, d2, vx, sems,
 ):
-    vx_copy = pltpu.make_async_copy(vx_far, vx, sems.at[0])
-    vx_copy.start()
+    vx_copies = [
+        pltpu.make_async_copy(vx_mid, vx.at[1:9], sems.at[0]),
+        pltpu.make_async_copy(vx_edge.at[0], vx.at[0], sems.at[1]),
+        pltpu.make_async_copy(vx_edge.at[1], vx.at[9], sems.at[2]),
+    ]
+    for copy in vx_copies:
+        copy.start()
+    sl2 = (sl2_edge.at[0], sl2_mid.at[0], sl2_mid.at[1], sl2_edge.at[1])
 
     def rows_of(value):
         return jnp.concatenate([value[:, y * 128 : y * 128 + 128] for y in range(6)], axis=0)
@@ -469,13 +500,16 @@
                 for dz in range(2):
                     for dy in range(2):
                         rows = slice((dz * 2 + dy) * 32, (dz * 2 + dy) * 32 + 32)
-                        slope = sl2[z, rows, y * 128 : y * 128 + 128].astype(F32)
+                        slope = sl2[z][rows, y * 128 : y * 128 + 128].astype(F32)
                         lanes = slice((2 * y + dy) * 128, (2 * y + dy) * 128 + 128)
                         d2[2 * z + dz + 2, :, lanes] = (value * slope).astype(BF)
 
-    vx_copy.wait()
+    vx_copies[0].wait()
     total = None
-    for z in range(10):
+    for z in (1, 2, 3, 4, 5, 6, 7, 8, 0, 9):
+        if z == 0:
+            vx_copies[1].wait()
+            vx_copies[2].wait()
         left = jnp.concatenate(
             [vx[z, :, ky * 128 : ky * 128 + 1024] for ky in range(3)], axis=0
         )
@@ -558,15 +592,15 @@
         axis=0,
     )
     held = jnp.broadcast_to(held[None], (8, 178, 128))
-    w2 = band(filters_two)
     near, far = swap(
         lax.dynamic_slice_in_dim(mid, 5 * (1 - odd_z), 3, 0),
         lax.dynamic_slice_in_dim(mid, 5 * odd_z, 3, 0),
         "gz",
     )
+    near, two = lax.optimization_barrier((near, filters_two))
+    w2 = band(two)
     all_of = lax.all_to_all(held, "ch", 0, 0, tiled=True)
-    cots = all_of[:, :16].reshape(128, 128)
-    mine, w2 = lax.optimization_barrier((all_of[:, 16:], w2))
+    mine, cots = lax.optimization_barrier((all_of[:, 16:], all_of[:, :16].reshape(128, 128)))
     other = swap_cores(mine)
     first = jnp.where(odd_z == 1, other, mine)
     second = jnp.where(odd_z == 1, mine, other)
@@ -580,22 +614,38 @@
     back = four[:, ::-1].reshape(8, 3, 3, 3, 8, 128)
     w4b = back.transpose(2, 0, 4, 1, 3, 5).reshape(192, 1152)
 
-    vq, sl2, vx = call(
-        shallow_forward_kernel,
+    inner, sl2_mid, vx_mid = call(
+        inner_forward_kernel,
+        (
+            shape((2, 192, 128), BF),
+            shape((2, 128, 512), BF),
+            shape((8, 48, 1280), BF),
+        ),
+        [
+            pltpu.VMEM((8, 48, 1792), BF),
+            pltpu.VMEM((2, 128, 512), BF),
+            pltpu.SemaphoreType.DMA((2,)),
+        ],
+        1 << 31,
+        (pos, mid, w2, const(shift_rows)),
+        far_out=(1, 2),
+    )
+    vq, sl2_edge, vx_edge = call(
+        outer_forward_kernel,
         (
             shape((4, 96, 768), BF),
-            shape((4, 128, 512), BF),
-            shape((10, 48, 1280), BF),
+            shape((2, 128, 512), BF),
+            shape((2, 48, 1280), BF),
         ),
         [
-            pltpu.VMEM((6, 192, 128), BF),
-            pltpu.VMEM((6, 128, 512), BF),
-            pltpu.VMEM((14, 48, 1792), BF),
-            pltpu.SemaphoreType.DMA((2,)),
+            pltpu.VMEM((4, 192, 128), BF),
+            pltpu.VMEM((2, 128, 512), BF),
+            pltpu.VMEM((12, 48, 1792), BF),
+            pltpu.SemaphoreType.DMA((4,)),
         ],
         1 << 32,
         (
-            pos, near, mid, far, w2,
+            pos, near, mid, far, inner, w2,
             const(shift_rows), const(pool_two), const(shift_halves),
         ),
         far_out=(1, 2),
@@ -663,14 +713,15 @@
             pltpu.VMEM((4, 192, 768), BF),
             pltpu.VMEM((12, 32, 1024), BF),
             pltpu.VMEM((10, 48, 1280), BF),
-            pltpu.SemaphoreType.DMA((1,)),
+            pltpu.SemaphoreType.DMA((3,)),
         ],
         1 << 32,
         (
             pos, own_near, own_far, near, far, w3b,
-            const(shift_straight), const(shift_cross), const(spread_two), sl2, vx,
+            const(shift_straight), const(shift_cross), const(spread_two),
+            sl2_mid, sl2_edge, vx_mid, vx_edge,
         ),
-        far_in=(10,),
+        far_in=(11, 12),
     )
     pieces = jnp.concatenate(
         [grads.reshape(32, 9, 128), g2.astype(BF).reshape(32, 5, 128)], axis=1

time: 127 us -> 126 us (level)
  waiting for transfers between devices: 15.2 us -> 13 us
  starting transfers between devices: 49.3 us -> 48 us
    ppermute x12, waiting for transfers between devices: 5.04 us -> 2.81 us  [swap(): return (lax.ppermute(one, axis, inside), lax.ppermute(two, axis, outside))]
    unnamed x31 -> x37, local copies, waits for them, and re-layouts: 3.16 us -> 5.05 us
    ppermute x1, starting transfers between devices: 1.42 us -> 0.09 us  [swap_cores(): lax.ppermute(value, 'gz', [(i, i ^ 1) for i in range(lax.axis_size('gz'))])]
    pallas_call x6 -> x7, Pallas kernels: 16.7 us -> 17.6 us  [call(): pl.pallas_call(kernel, out_shape=tuple((pltpu.HBM(o.shape, o.dtype) if n...]
  transfers between devices with their start and end apart: 16 -> 16, of which waited for: 5 -> 3; matrix products, arithmetic and copies ran while one was open for 7% -> 6% of each run, Pallas kernels for 6% -> 7%
where the time goes in v5:
time: 126 us; the launch traced here: 125 us
  starting transfers between devices  48 us (38%)
  blocking collectives  33.3 us (26%)
  Pallas kernels  17.6 us (14%)
  waiting for transfers between devices  13 us (10%)
  local copies, waits for them, and re-layouts  10.9 us (9%)
  between operations  1.35 us (1%)
    ppermute x12, starting transfers between devices, swap(): return (lax.ppermute(one, axis, inside), lax.ppermute(two, axis, outside))  32 us
    all_to_all x1, blocking collectives, body(): lax.all_to_all(pieces, 'gz', 0, 0, tiled=True).astype(F32).sum(axis=0)  22.4 us
    pallas_call x7, Pallas kernels, call(): pl.pallas_call(kernel, out_shape=tuple((pltpu.HBM(o.shape, o.dtype) if n...  17.6 us
    all_to_all x1, blocking collectives, to_all(): return lax.all_to_all(copies, axis, 0, 0, tiled=True)  10.9 us
    all_to_all x1, waiting for transfers between devices, to_all(): return lax.all_to_all(copies, axis, 0, 0, tiled=True)  10.2 us
    all_to_all x1, starting transfers between devices, body(): all_of = lax.all_to_all(held, 'ch', 0, 0, tiled=True)  7.08 us
    unnamed x37, local copies, waits for them, and re-layouts  5.05 us
    all_to_all x1, starting transfers between devices, to_all(): return lax.all_to_all(copies, axis, 0, 0, tiled=True)  5.02 us
  transfers between devices with their start and end apart: 16, of which 3 were waited for; matrix products, arithmetic and copies ran while one was open for 6% of the time, Pallas kernels for 7%

profile of v5, /device:TPU:1, one launch (start us, length us, event | category | flops | bytes accessed | tf_op | source)
XLA Modules:
  0.0 125.2 jit_solution(9250691229656479691)
XLA Ops:
  0.7 1.1 copy.107
  1.8 2.6 %collective-permute-start = (bf16[8,3,16,128]{3,2,1,0:T(8,128)(2,1)S(1)}, bf16[8,3,16,128]{3,2,1,0:T(8,128)(2,1)S(1)}, u32[]{:S(2)}, u32[]{:S(2)}) collective-permute-start(bf16[8,3,16,128]{3,2,1,0:T(8,128)(2,1)S(1)} %get-tuple-element.80), channel_id=1, source_target_pairs={{0,1},{1,0},{2,3},{3,2},{4,5},{5,4},{6,7},{7,6},{8,9},{9,8},{10,11... | collective-permute-start | bytes 294920 | tf_op jit(solution)/shard_map/ppermute | solution.py:543
  4.4 0.7 collective-permute-start.1
  5.1 0.1 reshape.84
  5.2 0.6 copy-done.16
  5.9 0.8 broadcast_in_dim.8
  6.7 7.1 %all-to-all-start = ((bf16[8,178,128]{2,1,0:T(8,128)(2,1)}), bf16[8,178,128]{2,1,0:T(8,128)(2,1)S(1)}, u32[]{:S(2)}, u32[]{:S(2)}) async-start(bf16[8,178,128]{2,1,0:T(8,128)(2,1)} %broadcast_in_dim.8), calls=%async_computation | async-start | bytes 753664 | tf_op jit(solution)/shard_map/all_to_all | solution.py:602
  14.0 1.6 %collective-permute-start.2 = (bf16[3,14,16,128]{3,2,1,0:T(8,128)(2,1)S(1)}, bf16[3,14,16,128]{3,2,1,0:T(8,128)(2,1)S(1)}, u32[]{:S(2)}, u32[]{:S(2)}) collective-permute-start(bf16[3,14,16,128]{3,2,1,0:T(8,128)(2,1)S(1)} %get-tuple-element.77), channel_id=1, source_target_pairs={{0,8},{8,0},{16,24},{24,16},{32,40},{40,32},{48,56},{56,48},{64,72... | collective-permute-start | bytes 516104 | tf_op jit(solution)/shard_map/ppermute | solution.py:543
  15.7 4.8 %collective-permute-start.3 = (bf16[3,14,16,128]{3,2,1,0:T(8,128)(2,1)S(1)}, bf16[3,14,16,128]{3,2,1,0:T(8,128)(2,1)S(1)}, u32[]{:S(2)}, u32[]{:S(2)}) collective-permute-start(bf16[3,14,16,128]{3,2,1,0:T(8,128)(2,1)S(1)} %get-tuple-element.76), channel_id=1, source_target_pairs={{8,16},{24,32},{40,48},{56,64},{72,80},{88,96},{104,112},{120,128}... | collective-permute-start | bytes 516104 | tf_op jit(solution)/shard_map/ppermute | solution.py:543
  20.5 0.1 copy.84
  20.6 0.3 pad_bitcast_fusion.3
  20.9 0.5 pad_maximum_fusion
  21.4 0.5 reshape.83.w2
  21.9 0.3 copy-done.9
  22.3 2.9 %shard_map.192 = (bf16[2,192,128]{2,1,0:T(8,128)(2,1)S(1)}, bf16[2,128,512]{2,1,0:T(8,128)(2,1)}, bf16[8,48,1280]{2,1,0:T(8,128)(2,1)}) custom-call(s32[2]{0:T(128)S(1)} %pad_add_fusion.pos, bf16[8,14,16,128]{3,2,1,0:T(8,128)(2,1)S(1)} %pad_maximum_fusion.1.mid, bf16[128,768]{1,0:T(8,128)(2,1)S(1)} %reshape.83.w2, bf16[128,256]{1,0:T(8,128)(2,1)S(1)} %copy-done.9), custom_call_target="tpu_custom_call" | custom-call | flops 2147483648 | bytes 1048576 | tf_op jit(solution)/shard_map/pallas_call | solution.py:159
  25.3 0.1 collective-permute-start.4
  25.4 0.6 copy-done.11
  26.1 2.4 %shard_map.193 = (bf16[4,96,768]{2,1,0:T(8,128)(2,1)S(1)}, bf16[2,128,512]{2,1,0:T(8,128)(2,1)}, bf16[2,48,1280]{2,1,0:T(8,128)(2,1)}) custom-call(s32[2]{0:T(128)S(1)} %pad_add_fusion.pos, bf16[3,14,16,128]{3,2,1,0:T(8,128)(2,1)S(1)} %collective-permute-done.2.near, bf16[8,14,16,128]{3,2,1,0:T(8,128)(2,1)S(1)} %pad_maximum_fusion.1.mid, ...), custom_call_target="tpu_custom_call" | custom-call | flops 4294967296 | bytes 1048576 | tf_op jit(solution)/shard_map/pallas_call | solution.py:159
  28.8 0.1 copy.89
  28.9 0.1 copy.90.w3
  29.0 0.7 copy-done.8
  29.7 1.2 shard_map.194
  30.9 4.9 %collective-permute-start.6 = (bf16[192,128]{1,0:T(8,128)(2,1)S(1)}, bf16[192,128]{1,0:T(8,128)(2,1)S(1)}, u32[]{:S(2)}, u32[]{:S(2)}) collective-permute-start(bf16[192,128]{1,0:T(8,128)(2,1)S(1)} %get-tuple-element.35.own3), channel_id=1, source_target_pairs={{8,16},{24,32},{40,48},{56,64},{72,80},{88,96},{104,112},{120,128}... | collective-permute-start | bytes 147464 | tf_op jit(solution)/shard_map/ppermute | solution.py:543
  35.8 0.1 collective-permute-start.5
  36.0 0.2 copy.95
  36.1 0.9 reshape.95.w3b
  37.2 0.4 copy.92
  37.6 0.9 copy.106
  38.5 0.8 collective-permute-start.8
  39.3 4.3 %collective-permute-start.7 = (bf16[320,128]{1,0:T(8,128)(2,1)S(1)}, bf16[320,128]{1,0:T(8,128)(2,1)S(1)}, u32[]{:S(2)}, u32[]{:S(2)}) collective-permute-start(bf16[320,128]{1,0:T(8,128)(2,1)S(1)} %get-tuple-element.91), channel_id=1, source_target_pairs={{0,1},{1,0},{2,3},{3,2},{4,5},{5,4},{6,7},{7,6},{8,9},{9,8},{10,11... | collective-permute-start | bytes 245768 | tf_op jit(solution)/shard_map/ppermute | solution.py:543
  43.6 0.8 collective-permute-start.10
  44.4 3.6 %collective-permute-start.9 = (bf16[192,128]{1,0:T(8,128)(2,1)S(1)}, bf16[192,128]{1,0:T(8,128)(2,1)S(1)}, u32[]{:S(2)}, u32[]{:S(2)}) collective-permute-start(bf16[192,128]{1,0:T(8,128)(2,1)S(1)} %pad_maximum_fusion.8), channel_id=1, source_target_pairs={{0,2},{1,3},{2,0},{3,1},{4,6},{5,7},{6,4},{7,5},{8,10},{9,11},{10,... | collective-permute-start | bytes 147464 | tf_op jit(solution)/shard_map/ppermute | solution.py:543
  48.0 1.3 %copy.96.w4f = bf16[384,576]{1,0:T(8,128)(2,1)S(1)} copy(bf16[384,576]{0,1:T(8,128)(2,1)} %bitcast.76) | data formatting | bytes 884736 | tf_op jit(solution)/shard_map/optimization_barrier | solution.py:665
  49.2 0.2 collective-permute-done.9.in2
  49.5 4.1 %shard_map.195 = (f32[128,128]{1,0:T(8,128)S(1)}, bf16[64,768]{1,0:T(8,128)(2,1)S(1)}, bf16[64,768]{1,0:T(8,128)(2,1)S(1)}, bf16[6,192,256]{2,1,0:T(8,128)(2,1)S(1)}, bf16[2,128,256]{2,1,0:T(8,128)(2,1)S(1)}) custom-call(s32[2]{0:T(128)S(1)} %pad_add_fusion.pos, bf16[192,128]{1,0:T(8,128)(2,1)S(1)} %get-tuple-element.35.own3, ...), custom_call_target="tpu_custom_call" | custom-call | flops 4294967296 | bytes 1048576 | tf_op jit(solution)/shard_map/pallas_call | solution.py:159
  53.6 2.4 %shard_map.196 = bf16[8,288,128]{2,1,0:T(8,128)(2,1)} custom-call(s32[2]{0:T(128)S(1)} %pad_add_fusion.pos, bf16[6,192,256]{2,1,0:T(8,128)(2,1)S(1)} %get-tuple-element.42.field, bf16[2,128,256]{2,1,0:T(8,128)(2,1)S(1)} %get-tuple-element.43.own, bf16[64,768]{1,0:T(8,128)(2,1)S(1)} %get-tuple-element.44.near.own_near, ...), custom_call_target="tpu_custom_call" | custom-call | flops 2147483648 | bytes 1048576 | tf_op jit(solution)/shard_map/pallas_call | solution.py:159
  56.0 3.8 %all-to-all-start.1 = ((bf16[8,288,128]{2,1,0:T(8,128)(2,1)}), bf16[8,288,128]{2,1,0:T(8,128)(2,1)S(1)}, u32[]{:S(2)}, u32[]{:S(2)}) async-start(bf16[8,288,128]{2,1,0:T(8,128)(2,1)} %shard_map.196), calls=%async_computation.1 | async-start | bytes 1179648 | tf_op jit(solution)/shard_map/all_to_all | solution.py:705
  59.8 2.7 %collective-permute-start.11 = (bf16[64,768]{1,0:T(8,128)(2,1)S(1)}, bf16[64,768]{1,0:T(8,128)(2,1)S(1)}, u32[]{:S(2)}, u32[]{:S(2)}) collective-permute-start(bf16[64,768]{1,0:T(8,128)(2,1)S(1)} %get-tuple-element.44.near.own_near), channel_id=1, source_target_pairs={{0,8},{8,0},{16,24},{24,16},{32,40},{40,32},{48,56},{56,48},{64,72... | collective-permute-start | bytes 294920 | tf_op jit(solution)/shard_map/ppermute | solution.py:543
  62.5 5.2 %collective-permute-start.12 = (bf16[64,768]{1,0:T(8,128)(2,1)S(1)}, bf16[64,768]{1,0:T(8,128)(2,1)S(1)}, u32[]{:S(2)}, u32[]{:S(2)}) collective-permute-start(bf16[64,768]{1,0:T(8,128)(2,1)S(1)} %get-tuple-element.45.far.own_far), channel_id=1, source_target_pairs={{8,16},{24,32},{40,48},{56,64},{72,80},{88,96},{104,112},{120,128}... | collective-permute-start | bytes 294920 | tf_op jit(solution)/shard_map/ppermute | solution.py:543
  67.8 2.6 %collective-permute-done.12.far = bf16[64,768]{1,0:T(8,128)(2,1)S(1)} collective-permute-done((bf16[64,768]{1,0:T(8,128)(2,1)S(1)}, bf16[64,768]{1,0:T(8,128)(2,1)S(1)}, u32[]{:S(2)}, u32[]{:S(2)}) %collective-permute-start.12) | collective-permute-done | bytes 98336 | tf_op jit(solution)/shard_map/ppermute | solution.py:543
  70.4 3.2 %shard_map.197 = f32[160,128]{1,0:T(8,128)S(1)} custom-call(s32[2]{0:T(128)S(1)} %pad_add_fusion.pos, bf16[64,768]{1,0:T(8,128)(2,1)S(1)} %get-tuple-element.44.near.own_near, bf16[64,768]{1,0:T(8,128)(2,1)S(1)} %get-tuple-element.45.far.own_far, bf16[64,768]{1,0:T(8,128)(2,1)S(1)} %collective-permute-done.11.near, ...), custom_call_target="tpu_custom_call" | custom-call | flops 4294967296 | bytes 1048576 | tf_op jit(solution)/shard_map/pallas_call | solution.py:159
  73.9 22.4 %all_to_all.25 = bf16[32,14,128]{2,1,0:T(8,128)(2,1)S(1)} all-to-all(bf16[32,14,128]{2,1,0:T(8,128)(2,1)S(1)} %pad_maximum_fusion.4), channel_id=1, replica_groups=mesh['gz'=32,'ch'=8] {'gz'}, dimensions={0} | all-to-all | bytes 229376 | tf_op jit(solution)/shard_map/all_to_all | solution.py:729
  96.4 10.9 %all_to_all.26 = bf16[8,5,128]{2,1,0:T(8,128)(2,1)S(1)} all-to-all(bf16[8,5,128]{2,1,0:T(8,128)(2,1)S(1)} %broadcast_in_dim.10), channel_id=1, replica_groups=mesh['gz'=32,'ch'=8] {'ch'}, dimensions={0} | all-to-all | bytes 20480 | tf_op jit(solution)/shard_map/all_to_all | solution.py:553
  107.3 0.7 broadcast_in_dim.11
  108.0 5.0 %all-to-all-start.4 = ((bf16[32,14,128]{2,1,0:T(8,128)(2,1)}), bf16[32,14,128]{2,1,0:T(8,128)(2,1)S(1)}, u32[]{:S(2)}, u32[]{:S(2)}) async-start(bf16[32,14,128]{2,1,0:T(8,128)(2,1)} %broadcast_in_dim.11), calls=%async_computation.4 | async-start | bytes 262144 | tf_op jit(solution)/shard_map/all_to_all | solution.py:553
  113.0 0.6 copy.98
  113.6 10.2 %all-to-all-done.4.whole = bf16[32,14,128]{2,1,0:T(8,128)(2,1)S(1)} async-done(((bf16[32,14,128]{2,1,0:T(8,128)(2,1)}), bf16[32,14,128]{2,1,0:T(8,128)(2,1)S(1)}, u32[]{:S(2)}, u32[]{:S(2)}) %all-to-all-start.4) | async-done | bytes 114720 | tf_op jit(solution)/shard_map/all_to_all | solution.py:553
  123.8 1.4 %shard_map.198 = (f32[216,128]{1,0:T(8,128)}, f32[27,4,64]{2,1,0:T(4,128)}, f32[3,144,32]{2,1,0:T(8,128)}) custom-call(s32[2]{0:T(128)S(1)} %pad_add_fusion.pos, bf16[32,14,128]{2,1,0:T(8,128)(2,1)S(1)} %all-to-all-done.4.whole), custom_call_target="tpu_custom_call" | custom-call | flops 1048576 | bytes 1048576 | tf_op jit(solution)/shard_map/pallas_call | solution.py:159
  (83 shorter events, 1.3 us)
Async XLA Ops:
  0.6 5.2 %copy-start = (bf16[128,8,3,3,3]{0,1,4,3,2:T(8,128)(2,1)S(1)}, bf16[128,8,3,3,3]{0,1,4,3,2:T(8,128)(2,1)}, u32[]{:S(2)}) copy-start(bf16[128,8,3,3,3]{0,1,4,3,2:T(8,128)(2,1)} %param.20) | copy-start | bytes 165892
  1.8 3.3 %copy-start.15 = (bf16[16,1,8,16]{3,2,1,0:T(8,128)(2,1)S(1)}, bf16[16,1,8,16]{3,2,1,0:T(8,128)(2,1)}, u32[]{:S(2)}) copy-start(bf16[16,1,8,16]{3,2,1,0:T(8,128)(2,1)} %param.21) | copy-start | bytes 12292
  1.8 12.0 %collective-permute-start = (bf16[8,3,16,128]{3,2,1,0:T(8,128)(2,1)S(1)}, bf16[8,3,16,128]{3,2,1,0:T(8,128)(2,1)S(1)}, u32[]{:S(2)}, u32[]{:S(2)}) collective-permute-start(bf16[8,3,16,128]{3,2,1,0:T(8,128)(2,1)S(1)} %get-tuple-element.80), channel_id=1, source_target_pairs={{0,1},{1,0},{2,3},{3,2},{4,5},{5,4},{6,7},{7,6},{8,9},{9,8},{10,11... | collective-permute-start | bytes 294920 | tf_op jit(solution)/shard_map/ppermute | solution.py:543
  4.4 9.4 %collective-permute-start.1 = (bf16[8,3,16,128]{3,2,1,0:T(8,128)(2,1)S(1)}, bf16[8,3,16,128]{3,2,1,0:T(8,128)(2,1)S(1)}, u32[]{:S(2)}, u32[]{:S(2)}) collective-permute-start(bf16[8,3,16,128]{3,2,1,0:T(8,128)(2,1)S(1)} %get-tuple-element.81), channel_id=1, source_target_pairs={{1,2},{3,4},{5,6},{2,1},{4,3},{6,5},{9,10},{11,12},{13,14},{10,9},... | collective-permute-start | bytes 294920 | tf_op jit(solution)/shard_map/ppermute | solution.py:543
  5.1 0.7 copy-start.16
  6.7 18.4 %all-to-all-start = ((bf16[8,178,128]{2,1,0:T(8,128)(2,1)}), bf16[8,178,128]{2,1,0:T(8,128)(2,1)S(1)}, u32[]{:S(2)}, u32[]{:S(2)}) async-start(bf16[8,178,128]{2,1,0:T(8,128)(2,1)} %broadcast_in_dim.8), calls=%async_computation | async-start | bytes 753664 | tf_op jit(solution)/shard_map/all_to_all | solution.py:602
  13.9 6.5 %copy-start.14 = (bf16[32,16,3,3,3]{0,1,4,3,2:T(8,128)(2,1)S(1)}, bf16[32,16,3,3,3]{0,1,4,3,2:T(8,128)(2,1)}, u32[]{:S(2)}) copy-start(bf16[32,16,3,3,3]{0,1,4,3,2:T(8,128)(2,1)} %param.18) | copy-start | bytes 82948
  14.0 6.5 %collective-permute-start.2 = (bf16[3,14,16,128]{3,2,1,0:T(8,128)(2,1)S(1)}, bf16[3,14,16,128]{3,2,1,0:T(8,128)(2,1)S(1)}, u32[]{:S(2)}, u32[]{:S(2)}) collective-permute-start(bf16[3,14,16,128]{3,2,1,0:T(8,128)(2,1)S(1)} %get-tuple-element.77), channel_id=1, source_target_pairs={{0,8},{8,0},{16,24},{24,16},{32,40},{40,32},{48,56},{56,48},{64,72... | collective-permute-start | bytes 516104 | tf_op jit(solution)/shard_map/ppermute | solution.py:543
  15.7 9.7 %collective-permute-start.3 = (bf16[3,14,16,128]{3,2,1,0:T(8,128)(2,1)S(1)}, bf16[3,14,16,128]{3,2,1,0:T(8,128)(2,1)S(1)}, u32[]{:S(2)}, u32[]{:S(2)}) collective-permute-start(bf16[3,14,16,128]{3,2,1,0:T(8,128)(2,1)S(1)} %get-tuple-element.76), channel_id=1, source_target_pairs={{8,16},{24,32},{40,48},{56,64},{72,80},{88,96},{104,112},{120,128}... | collective-permute-start | bytes 516104 | tf_op jit(solution)/shard_map/ppermute | solution.py:543
  21.4 0.8 copy-start.9
  25.2 0.8 copy-start.11
  25.3 0.9 copy-start.10
  25.3 3.3 %collective-permute-start.4 = (bf16[8,162,128]{2,0,1:T(8,128)(2,1)S(1)}, bf16[8,162,128]{2,0,1:T(8,128)(2,1)S(1)}, u32[]{:S(2)}, u32[]{:S(2)}) collective-permute-start(bf16[8,162,128]{2,0,1:T(8,128)(2,1)S(1)} %copy.101), channel_id=1, source_target_pairs={{0,8},{8,0},{16,24},{24,16},{32,40},{40,32},{48,56},{56,48},{64,72... | collective-permute-start | bytes 995336 | tf_op jit(solution)/shard_map/ppermute | solution.py:547
  28.9 0.8 copy-start.8
  30.9 7.6 %collective-permute-start.6 = (bf16[192,128]{1,0:T(8,128)(2,1)S(1)}, bf16[192,128]{1,0:T(8,128)(2,1)S(1)}, u32[]{:S(2)}, u32[]{:S(2)}) collective-permute-start(bf16[192,128]{1,0:T(8,128)(2,1)S(1)} %get-tuple-element.35.own3), channel_id=1, source_target_pairs={{8,16},{24,32},{40,48},{56,64},{72,80},{88,96},{104,112},{120,128}... | collective-permute-start | bytes 147464 | tf_op jit(solution)/shard_map/ppermute | solution.py:543
  35.8 2.7 %collective-permute-start.5 = (bf16[192,128]{1,0:T(8,128)(2,1)S(1)}, bf16[192,128]{1,0:T(8,128)(2,1)S(1)}, u32[]{:S(2)}, u32[]{:S(2)}) collective-permute-start(bf16[192,128]{1,0:T(8,128)(2,1)S(1)} %get-tuple-element.35.own3), channel_id=1, source_target_pairs={{0,8},{8,0},{16,24},{24,16},{32,40},{40,32},{48,56},{56,48},{64,72... | collective-permute-start | bytes 147464 | tf_op jit(solution)/shard_map/ppermute | solution.py:543
  38.5 11.0 %copy-start.2 = (bf16[640,512]{1,0:T(8,128)(2,1)S(1)}, bf16[640,512]{1,0:T(8,128)(2,1)}, u32[]{:S(2)}) copy-start(bf16[640,512]{1,0:T(8,128)(2,1)} %constant.70.clone.planes_of) | copy-start | bytes 1966084
  38.5 11.0 %collective-permute-start.8 = (bf16[320,128]{1,0:T(8,128)(2,1)S(1)}, bf16[320,128]{1,0:T(8,128)(2,1)S(1)}, u32[]{:S(2)}, u32[]{:S(2)}) collective-permute-start(bf16[320,128]{1,0:T(8,128)(2,1)S(1)} %get-tuple-element.90), channel_id=1, source_target_pairs={{1,2},{3,4},{5,6},{2,1},{4,3},{6,5},{9,10},{11,12},{13,14},{10,9},... | collective-permute-start | bytes 245768 | tf_op jit(solution)/shard_map/ppermute | solution.py:543
  39.3 10.2 %collective-permute-start.7 = (bf16[320,128]{1,0:T(8,128)(2,1)S(1)}, bf16[320,128]{1,0:T(8,128)(2,1)S(1)}, u32[]{:S(2)}, u32[]{:S(2)}) collective-permute-start(bf16[320,128]{1,0:T(8,128)(2,1)S(1)} %get-tuple-element.91), channel_id=1, source_target_pairs={{0,1},{1,0},{2,3},{3,2},{4,5},{5,4},{6,7},{7,6},{8,9},{9,8},{10,11... | collective-permute-start | bytes 245768 | tf_op jit(solution)/shard_map/ppermute | solution.py:543
  43.6 5.9 %copy-start.3 = (bf16[256,768]{1,0:T(8,128)(2,1)S(1)}, bf16[256,768]{1,0:T(8,128)(2,1)}, u32[]{:S(2)}) copy-start(bf16[256,768]{1,0:T(8,128)(2,1)} %constant.71.clone.shift4) | copy-start | bytes 1179652
  43.6 5.9 %copy-start.7 = (bf16[256,128]{1,0:T(8,128)(2,1)S(1)}, bf16[256,128]{1,0:T(8,128)(2,1)}, u32[]{:S(2)}) copy-start(bf16[256,128]{1,0:T(8,128)(2,1)} %constant.69.clone.pool4) | copy-start | bytes 196612
  43.6 5.7 %collective-permute-start.10 = (bf16[192,128]{1,0:T(8,128)(2,1)S(1)}, bf16[192,128]{1,0:T(8,128)(2,1)S(1)}, u32[]{:S(2)}, u32[]{:S(2)}) collective-permute-start(bf16[192,128]{1,0:T(8,128)(2,1)S(1)} %pad_maximum_fusion.8), channel_id=1, source_target_pairs={{2,4},{3,5},{4,2},{5,3},{10,12},{11,13},{12,10},{13,11},{18,20},{1... | collective-permute-start | bytes 147464 | tf_op jit(solution)/shard_map/ppermute | solution.py:543
  44.4 5.1 %collective-permute-start.9 = (bf16[192,128]{1,0:T(8,128)(2,1)S(1)}, bf16[192,128]{1,0:T(8,128)(2,1)S(1)}, u32[]{:S(2)}, u32[]{:S(2)}) collective-permute-start(bf16[192,128]{1,0:T(8,128)(2,1)S(1)} %pad_maximum_fusion.8), channel_id=1, source_target_pairs={{0,2},{1,3},{2,0},{3,1},{4,6},{5,7},{6,4},{7,5},{8,10},{9,11},{10,... | collective-permute-start | bytes 147464 | tf_op jit(solution)/shard_map/ppermute | solution.py:543
  56.0 14.4 %copy-start.1 = (bf16[96,576]{1,0:T(8,128)(2,1)S(1)}, bf16[96,576]{1,0:T(8,128)(2,1)}, u32[]{:S(2)}) copy-start(bf16[96,576]{1,0:T(8,128)(2,1)} %reshape.95.w3b) | copy-start | bytes 331780
  56.0 14.4 %copy-start.4 = (bf16[256,384]{1,0:T(8,128)(2,1)S(1)}, bf16[256,384]{1,0:T(8,128)(2,1)}, u32[]{:S(2)}) copy-start(bf16[256,384]{1,0:T(8,128)(2,1)} %constant.74.clone.cross) | copy-start | bytes 589828
  56.0 14.4 %copy-start.5 = (bf16[128,384]{1,0:T(8,128)(2,1)S(1)}, bf16[128,384]{1,0:T(8,128)(2,1)}, u32[]{:S(2)}) copy-start(bf16[128,384]{1,0:T(8,128)(2,1)} %constant.73.clone.straight) | copy-start | bytes 294916
  56.0 14.4 %copy-start.6 = (bf16[128,256]{1,0:T(8,128)(2,1)S(1)}, bf16[128,256]{1,0:T(8,128)(2,1)}, u32[]{:S(2)}) copy-start(bf16[128,256]{1,0:T(8,128)(2,1)} %constant.75.clone.spread2) | copy-start | bytes 196612
  56.0 14.4 %copy-start.12 = (bf16[2,128,512]{2,1,0:T(8,128)(2,1)S(1)}, bf16[2,128,512]{2,1,0:T(8,128)(2,1)}, u32[]{:S(2)}) copy-start(bf16[2,128,512]{2,1,0:T(8,128)(2,1)} %get-tuple-element.47.sl2_mid) | copy-start | bytes 786436
  56.0 14.4 %copy-start.13 = (bf16[2,128,512]{2,1,0:T(8,128)(2,1)S(1)}, bf16[2,128,512]{2,1,0:T(8,128)(2,1)}, u32[]{:S(2)}) copy-start(bf16[2,128,512]{2,1,0:T(8,128)(2,1)} %get-tuple-element.48.sl2_edge) | copy-start | bytes 786436
  56.0 17.7 %all-to-all-start.1 = ((bf16[8,288,128]{2,1,0:T(8,128)(2,1)}), bf16[8,288,128]{2,1,0:T(8,128)(2,1)S(1)}, u32[]{:S(2)}, u32[]{:S(2)}) async-start(bf16[8,288,128]{2,1,0:T(8,128)(2,1)} %shard_map.196), calls=%async_computation.1 | async-start | bytes 1179648 | tf_op jit(solution)/shard_map/all_to_all | solution.py:705
  59.8 8.0 %collective-permute-start.11 = (bf16[64,768]{1,0:T(8,128)(2,1)S(1)}, bf16[64,768]{1,0:T(8,128)(2,1)S(1)}, u32[]{:S(2)}, u32[]{:S(2)}) collective-permute-start(bf16[64,768]{1,0:T(8,128)(2,1)S(1)} %get-tuple-element.44.near.own_near), channel_id=1, source_target_pairs={{0,8},{8,0},{16,24},{24,16},{32,40},{40,32},{48,56},{56,48},{64,72... | collective-permute-start | bytes 294920 | tf_op jit(solution)/shard_map/ppermute | solution.py:543
  62.5 7.8 %collective-permute-start.12 = (bf16[64,768]{1,0:T(8,128)(2,1)S(1)}, bf16[64,768]{1,0:T(8,128)(2,1)S(1)}, u32[]{:S(2)}, u32[]{:S(2)}) collective-permute-start(bf16[64,768]{1,0:T(8,128)(2,1)S(1)} %get-tuple-element.45.far.own_far), channel_id=1, source_target_pairs={{8,16},{24,32},{40,48},{56,64},{72,80},{88,96},{104,112},{120,128}... | collective-permute-start | bytes 294920 | tf_op jit(solution)/shard_map/ppermute | solution.py:543
  108.0 15.8 %all-to-all-start.4 = ((bf16[32,14,128]{2,1,0:T(8,128)(2,1)}), bf16[32,14,128]{2,1,0:T(8,128)(2,1)S(1)}, u32[]{:S(2)}, u32[]{:S(2)}) async-start(bf16[32,14,128]{2,1,0:T(8,128)(2,1)} %broadcast_in_dim.11), calls=%async_computation.4 | async-start | bytes 262144 | tf_op jit(solution)/shard_map/all_to_all | solution.py:553

commit v6 on v5

--- a/solution.py
+++ b/solution.py
@@ -230,10 +230,11 @@
 
 
 def outer_forward_kernel(
-    pos, near, mid, far, inner, w2, shift2, pool2, shift3, vq, slopes_far, vx_far,
+    pos, near, mid, far, inner, w2, shift2, pool2, shift3, pool3, vq, pool3_out, slopes_far, vx_far,
     sums, slopes, vh, sems,
 ):
     odd = pos[0] % 2 == 1
+    pool3_out[...] = pool3[...]
     shift = shift2[...]
     for z in range(3):
         one = near[z].reshape(224, 128).astype(F32)
@@ -630,10 +631,11 @@
         (pos, mid, w2, const(shift_rows)),
         far_out=(1, 2),
     )
-    vq, sl2_edge, vx_edge = call(
+    vq, pool3, sl2_edge, vx_edge = call(
         outer_forward_kernel,
         (
             shape((4, 96, 768), BF),
+            shape((256, 128), BF),
             shape((2, 128, 512), BF),
             shape((2, 48, 1280), BF),
         ),
@@ -646,9 +648,9 @@
         1 << 32,
         (
             pos, near, mid, far, inner, w2,
-            const(shift_rows), const(pool_two), const(shift_halves),
+            const(shift_rows), const(pool_two), const(shift_halves), const(pool_three),
         ),
-        far_out=(1, 2),
+        far_out=(2, 3),
     )
     sent, edges, sl3 = call(
         middle_forward_kernel,
@@ -659,7 +661,7 @@
         ),
         [],
         1 << 30,
-        (pos, vq, w3f, const(pool_three), cots),
+        (pos, vq, w3f, pool3, cots),
     )
     near, far = swap(sent, sent, "gz")
     near, w4f, w4b, w3b = lax.optimization_barrier((near, w4f, w4b, w3b))

time: 126 us -> 125 us (level)
  no operation moved by 1% of the time
where the time goes in v6:
time: 125 us
  starting transfers between devices  48 us (38%)
  blocking collectives  33.3 us (27%)
  Pallas kernels  17.6 us (14%)
  waiting for transfers between devices  13 us (10%)
  local copies, waits for them, and re-layouts  10.3 us (8%)
  between operations  1.35 us (1%)
    ppermute x12, starting transfers between devices, swap(): return (lax.ppermute(one, axis, inside), lax.ppermute(two, axis, outside))  32 us
    all_to_all x1, blocking collectives, body(): lax.all_to_all(pieces, 'gz', 0, 0, tiled=True).astype(F32).sum(axis=0)  22.5 us
    pallas_call x7, Pallas kernels, call(): pl.pallas_call(kernel, out_shape=tuple((pltpu.HBM(o.shape, o.dtype) if n...  17.6 us
    all_to_all x1, blocking collectives, to_all(): return lax.all_to_all(copies, axis, 0, 0, tiled=True)  10.8 us
    all_to_all x1, waiting for transfers between devices, to_all(): return lax.all_to_all(copies, axis, 0, 0, tiled=True)  10.2 us
    all_to_all x1, starting transfers between devices, body(): all_of = lax.all_to_all(held, 'ch', 0, 0, tiled=True)  7.08 us
    all_to_all x1, starting transfers between devices, to_all(): return lax.all_to_all(copies, axis, 0, 0, tiled=True)  5.02 us
    unnamed x37, local copies, waits for them, and re-layouts  4.37 us
  transfers between devices with their start and end apart: 16, of which 3 were waited for; matrix products, arithmetic and copies ran while one was open for 6% of the time, Pallas kernels for 7%

profile of v6, /device:TPU:1, one launch (start us, length us, event | category | flops | bytes accessed | tf_op | source)
XLA Modules:
  0.0 124.6 jit_solution(5133698383309898005)
XLA Ops:
  0.7 1.1 copy.107
  1.8 2.6 %collective-permute-start = (bf16[8,3,16,128]{3,2,1,0:T(8,128)(2,1)S(1)}, bf16[8,3,16,128]{3,2,1,0:T(8,128)(2,1)S(1)}, u32[]{:S(2)}, u32[]{:S(2)}) collective-permute-start(bf16[8,3,16,128]{3,2,1,0:T(8,128)(2,1)S(1)} %get-tuple-element.82), channel_id=1, source_target_pairs={{0,1},{1,0},{2,3},{3,2},{4,5},{5,4},{6,7},{7,6},{8,9},{9,8},{10,11... | collective-permute-start | bytes 294920 | tf_op jit(solution)/shard_map/ppermute | solution.py:544
  4.4 0.7 collective-permute-start.1
  5.1 0.1 reshape.84
  5.2 0.6 copy-done.16
  5.9 0.8 broadcast_in_dim.8
  6.7 7.1 %all-to-all-start = ((bf16[8,178,128]{2,1,0:T(8,128)(2,1)}), bf16[8,178,128]{2,1,0:T(8,128)(2,1)S(1)}, u32[]{:S(2)}, u32[]{:S(2)}) async-start(bf16[8,178,128]{2,1,0:T(8,128)(2,1)} %broadcast_in_dim.8), calls=%async_computation | async-start | bytes 753664 | tf_op jit(solution)/shard_map/all_to_all | solution.py:603
  14.0 1.6 %collective-permute-start.2 = (bf16[3,14,16,128]{3,2,1,0:T(8,128)(2,1)S(1)}, bf16[3,14,16,128]{3,2,1,0:T(8,128)(2,1)S(1)}, u32[]{:S(2)}, u32[]{:S(2)}) collective-permute-start(bf16[3,14,16,128]{3,2,1,0:T(8,128)(2,1)S(1)} %get-tuple-element.79), channel_id=1, source_target_pairs={{0,8},{8,0},{16,24},{24,16},{32,40},{40,32},{48,56},{56,48},{64,72... | collective-permute-start | bytes 516104 | tf_op jit(solution)/shard_map/ppermute | solution.py:544
  15.7 4.8 %collective-permute-start.3 = (bf16[3,14,16,128]{3,2,1,0:T(8,128)(2,1)S(1)}, bf16[3,14,16,128]{3,2,1,0:T(8,128)(2,1)S(1)}, u32[]{:S(2)}, u32[]{:S(2)}) collective-permute-start(bf16[3,14,16,128]{3,2,1,0:T(8,128)(2,1)S(1)} %get-tuple-element.78), channel_id=1, source_target_pairs={{8,16},{24,32},{40,48},{56,64},{72,80},{88,96},{104,112},{120,128}... | collective-permute-start | bytes 516104 | tf_op jit(solution)/shard_map/ppermute | solution.py:544
  20.5 0.1 copy.84
  20.6 0.3 pad_bitcast_fusion.3
  20.9 0.5 pad_maximum_fusion
  21.4 0.5 reshape.83.w2
  21.9 0.3 copy-done.8
  22.3 2.9 %shard_map.192 = (bf16[2,192,128]{2,1,0:T(8,128)(2,1)S(1)}, bf16[2,128,512]{2,1,0:T(8,128)(2,1)}, bf16[8,48,1280]{2,1,0:T(8,128)(2,1)}) custom-call(s32[2]{0:T(128)S(1)} %pad_add_fusion.pos, bf16[8,14,16,128]{3,2,1,0:T(8,128)(2,1)S(1)} %pad_maximum_fusion.1.mid, bf16[128,768]{1,0:T(8,128)(2,1)S(1)} %reshape.83.w2, bf16[128,256]{1,0:T(8,128)(2,1)S(1)} %copy-done.8), custom_call_target="tpu_custom_call" | custom-call | flops 2147483648 | bytes 1048576 | tf_op jit(solution)/shard_map/pallas_call | solution.py:159
  25.3 0.1 collective-permute-start.4
  25.4 0.6 copy-done.10
  26.1 2.4 %shard_map.193 = (bf16[4,96,768]{2,1,0:T(8,128)(2,1)S(1)}, bf16[256,128]{1,0:T(8,128)(2,1)S(1)}, bf16[2,128,512]{2,1,0:T(8,128)(2,1)}, bf16[2,48,1280]{2,1,0:T(8,128)(2,1)}) custom-call(s32[2]{0:T(128)S(1)} %pad_add_fusion.pos, bf16[3,14,16,128]{3,2,1,0:T(8,128)(2,1)S(1)} %collective-permute-done.2.near, bf16[8,14,16,128]{3,2,1,0:T(8,128)(2,1)S(1)} %pad_maximum_fusion.1.mid, ...), custom_call_target="tpu_custom_call" | custom-call | flops 4294967296 | bytes 1048576 | tf_op jit(solution)/shard_map/pallas_call | solution.py:159
  28.8 0.1 copy.89
  28.9 0.1 copy.90.w3
  29.0 1.2 shard_map.194
  30.2 4.9 %collective-permute-start.6 = (bf16[192,128]{1,0:T(8,128)(2,1)S(1)}, bf16[192,128]{1,0:T(8,128)(2,1)S(1)}, u32[]{:S(2)}, u32[]{:S(2)}) collective-permute-start(bf16[192,128]{1,0:T(8,128)(2,1)S(1)} %get-tuple-element.37.own3), channel_id=1, source_target_pairs={{8,16},{24,32},{40,48},{56,64},{72,80},{88,96},{104,112},{120,128}... | collective-permute-start | bytes 147464 | tf_op jit(solution)/shard_map/ppermute | solution.py:544
  35.1 0.1 collective-permute-start.5
  35.3 0.2 copy.95
  35.4 0.9 reshape.95.w3b
  36.5 0.4 copy.92
  36.9 0.9 copy.106
  37.8 0.8 collective-permute-start.8
  38.6 4.3 %collective-permute-start.7 = (bf16[320,128]{1,0:T(8,128)(2,1)S(1)}, bf16[320,128]{1,0:T(8,128)(2,1)S(1)}, u32[]{:S(2)}, u32[]{:S(2)}) collective-permute-start(bf16[320,128]{1,0:T(8,128)(2,1)S(1)} %get-tuple-element.93), channel_id=1, source_target_pairs={{0,1},{1,0},{2,3},{3,2},{4,5},{5,4},{6,7},{7,6},{8,9},{9,8},{10,11... | collective-permute-start | bytes 245768 | tf_op jit(solution)/shard_map/ppermute | solution.py:544
  42.9 0.8 collective-permute-start.10
  43.7 3.6 %collective-permute-start.9 = (bf16[192,128]{1,0:T(8,128)(2,1)S(1)}, bf16[192,128]{1,0:T(8,128)(2,1)S(1)}, u32[]{:S(2)}, u32[]{:S(2)}) collective-permute-start(bf16[192,128]{1,0:T(8,128)(2,1)S(1)} %pad_maximum_fusion.8), channel_id=1, source_target_pairs={{0,2},{1,3},{2,0},{3,1},{4,6},{5,7},{6,4},{7,5},{8,10},{9,11},{10,... | collective-permute-start | bytes 147464 | tf_op jit(solution)/shard_map/ppermute | solution.py:544
  47.3 1.3 %copy.96.w4f = bf16[384,576]{1,0:T(8,128)(2,1)S(1)} copy(bf16[384,576]{0,1:T(8,128)(2,1)} %bitcast.76) | data formatting | bytes 884736 | tf_op jit(solution)/shard_map/optimization_barrier | solution.py:667
  48.6 0.2 collective-permute-done.9.in2
  48.8 4.1 %shard_map.195 = (f32[128,128]{1,0:T(8,128)S(1)}, bf16[64,768]{1,0:T(8,128)(2,1)S(1)}, bf16[64,768]{1,0:T(8,128)(2,1)S(1)}, bf16[6,192,256]{2,1,0:T(8,128)(2,1)S(1)}, bf16[2,128,256]{2,1,0:T(8,128)(2,1)S(1)}) custom-call(s32[2]{0:T(128)S(1)} %pad_add_fusion.pos, bf16[192,128]{1,0:T(8,128)(2,1)S(1)} %get-tuple-element.37.own3, ...), custom_call_target="tpu_custom_call" | custom-call | flops 4294967296 | bytes 1048576 | tf_op jit(solution)/shard_map/pallas_call | solution.py:159
  52.9 2.4 %shard_map.196 = bf16[8,288,128]{2,1,0:T(8,128)(2,1)} custom-call(s32[2]{0:T(128)S(1)} %pad_add_fusion.pos, bf16[6,192,256]{2,1,0:T(8,128)(2,1)S(1)} %get-tuple-element.44.field, bf16[2,128,256]{2,1,0:T(8,128)(2,1)S(1)} %get-tuple-element.45.own, bf16[64,768]{1,0:T(8,128)(2,1)S(1)} %get-tuple-element.46.near.own_near, ...), custom_call_target="tpu_custom_call" | custom-call | flops 2147483648 | bytes 1048576 | tf_op jit(solution)/shard_map/pallas_call | solution.py:159
  55.3 3.8 %all-to-all-start.1 = ((bf16[8,288,128]{2,1,0:T(8,128)(2,1)}), bf16[8,288,128]{2,1,0:T(8,128)(2,1)S(1)}, u32[]{:S(2)}, u32[]{:S(2)}) async-start(bf16[8,288,128]{2,1,0:T(8,128)(2,1)} %shard_map.196), calls=%async_computation.1 | async-start | bytes 1179648 | tf_op jit(solution)/shard_map/all_to_all | solution.py:707
  59.1 2.7 %collective-permute-start.11 = (bf16[64,768]{1,0:T(8,128)(2,1)S(1)}, bf16[64,768]{1,0:T(8,128)(2,1)S(1)}, u32[]{:S(2)}, u32[]{:S(2)}) collective-permute-start(bf16[64,768]{1,0:T(8,128)(2,1)S(1)} %get-tuple-element.46.near.own_near), channel_id=1, source_target_pairs={{0,8},{8,0},{16,24},{24,16},{32,40},{40,32},{48,56},{56,48},{64,72... | collective-permute-start | bytes 294920 | tf_op jit(solution)/shard_map/ppermute | solution.py:544
  61.9 5.2 %collective-permute-start.12 = (bf16[64,768]{1,0:T(8,128)(2,1)S(1)}, bf16[64,768]{1,0:T(8,128)(2,1)S(1)}, u32[]{:S(2)}, u32[]{:S(2)}) collective-permute-start(bf16[64,768]{1,0:T(8,128)(2,1)S(1)} %get-tuple-element.47.far.own_far), channel_id=1, source_target_pairs={{8,16},{24,32},{40,48},{56,64},{72,80},{88,96},{104,112},{120,128}... | collective-permute-start | bytes 294920 | tf_op jit(solution)/shard_map/ppermute | solution.py:544
  67.1 2.6 %collective-permute-done.12.far = bf16[64,768]{1,0:T(8,128)(2,1)S(1)} collective-permute-done((bf16[64,768]{1,0:T(8,128)(2,1)S(1)}, bf16[64,768]{1,0:T(8,128)(2,1)S(1)}, u32[]{:S(2)}, u32[]{:S(2)}) %collective-permute-start.12) | collective-permute-done | bytes 98336 | tf_op jit(solution)/shard_map/ppermute | solution.py:544
  69.7 3.2 %shard_map.197 = f32[160,128]{1,0:T(8,128)S(1)} custom-call(s32[2]{0:T(128)S(1)} %pad_add_fusion.pos, bf16[64,768]{1,0:T(8,128)(2,1)S(1)} %get-tuple-element.46.near.own_near, bf16[64,768]{1,0:T(8,128)(2,1)S(1)} %get-tuple-element.47.far.own_far, bf16[64,768]{1,0:T(8,128)(2,1)S(1)} %collective-permute-done.11.near, ...), custom_call_target="tpu_custom_call" | custom-call | flops 4294967296 | bytes 1048576 | tf_op jit(solution)/shard_map/pallas_call | solution.py:159
  73.0 0.1 reduce_sum.30
  73.2 22.5 %all_to_all.25 = bf16[32,14,128]{2,1,0:T(8,128)(2,1)S(1)} all-to-all(bf16[32,14,128]{2,1,0:T(8,128)(2,1)S(1)} %pad_maximum_fusion.4), channel_id=1, replica_groups=mesh['gz'=32,'ch'=8] {'gz'}, dimensions={0} | all-to-all | bytes 229376 | tf_op jit(solution)/shard_map/all_to_all | solution.py:731
  95.7 10.8 %all_to_all.26 = bf16[8,5,128]{2,1,0:T(8,128)(2,1)S(1)} all-to-all(bf16[8,5,128]{2,1,0:T(8,128)(2,1)S(1)} %broadcast_in_dim.10), channel_id=1, replica_groups=mesh['gz'=32,'ch'=8] {'ch'}, dimensions={0} | all-to-all | bytes 20480 | tf_op jit(solution)/shard_map/all_to_all | solution.py:554
  106.6 0.7 broadcast_in_dim.11
  107.3 5.0 %all-to-all-start.4 = ((bf16[32,14,128]{2,1,0:T(8,128)(2,1)}), bf16[32,14,128]{2,1,0:T(8,128)(2,1)S(1)}, u32[]{:S(2)}, u32[]{:S(2)}) async-start(bf16[32,14,128]{2,1,0:T(8,128)(2,1)} %broadcast_in_dim.11), calls=%async_computation.4 | async-start | bytes 262144 | tf_op jit(solution)/shard_map/all_to_all | solution.py:554
  112.3 0.6 copy.98
  112.9 10.2 %all-to-all-done.4.whole = bf16[32,14,128]{2,1,0:T(8,128)(2,1)S(1)} async-done(((bf16[32,14,128]{2,1,0:T(8,128)(2,1)}), bf16[32,14,128]{2,1,0:T(8,128)(2,1)S(1)}, u32[]{:S(2)}, u32[]{:S(2)}) %all-to-all-start.4) | async-done | bytes 114720 | tf_op jit(solution)/shard_map/all_to_all | solution.py:554
  123.1 1.4 %shard_map.198 = (f32[216,128]{1,0:T(8,128)}, f32[27,4,64]{2,1,0:T(4,128)}, f32[3,144,32]{2,1,0:T(8,128)}) custom-call(s32[2]{0:T(128)S(1)} %pad_add_fusion.pos, bf16[32,14,128]{2,1,0:T(8,128)(2,1)S(1)} %all-to-all-done.4.whole), custom_call_target="tpu_custom_call" | custom-call | flops 1048576 | bytes 1048576 | tf_op jit(solution)/shard_map/pallas_call | solution.py:159
  (83 shorter events, 1.2 us)
Async XLA Ops:
  0.6 5.2 %copy-start = (bf16[128,8,3,3,3]{0,1,4,3,2:T(8,128)(2,1)S(1)}, bf16[128,8,3,3,3]{0,1,4,3,2:T(8,128)(2,1)}, u32[]{:S(2)}) copy-start(bf16[128,8,3,3,3]{0,1,4,3,2:T(8,128)(2,1)} %param.20) | copy-start | bytes 165892
  1.8 3.3 %copy-start.15 = (bf16[16,1,8,16]{3,2,1,0:T(8,128)(2,1)S(1)}, bf16[16,1,8,16]{3,2,1,0:T(8,128)(2,1)}, u32[]{:S(2)}) copy-start(bf16[16,1,8,16]{3,2,1,0:T(8,128)(2,1)} %param.21) | copy-start | bytes 12292
  1.8 12.0 %collective-permute-start = (bf16[8,3,16,128]{3,2,1,0:T(8,128)(2,1)S(1)}, bf16[8,3,16,128]{3,2,1,0:T(8,128)(2,1)S(1)}, u32[]{:S(2)}, u32[]{:S(2)}) collective-permute-start(bf16[8,3,16,128]{3,2,1,0:T(8,128)(2,1)S(1)} %get-tuple-element.82), channel_id=1, source_target_pairs={{0,1},{1,0},{2,3},{3,2},{4,5},{5,4},{6,7},{7,6},{8,9},{9,8},{10,11... | collective-permute-start | bytes 294920 | tf_op jit(solution)/shard_map/ppermute | solution.py:544
  4.4 9.4 %collective-permute-start.1 = (bf16[8,3,16,128]{3,2,1,0:T(8,128)(2,1)S(1)}, bf16[8,3,16,128]{3,2,1,0:T(8,128)(2,1)S(1)}, u32[]{:S(2)}, u32[]{:S(2)}) collective-permute-start(bf16[8,3,16,128]{3,2,1,0:T(8,128)(2,1)S(1)} %get-tuple-element.83), channel_id=1, source_target_pairs={{1,2},{3,4},{5,6},{2,1},{4,3},{6,5},{9,10},{11,12},{13,14},{10,9},... | collective-permute-start | bytes 294920 | tf_op jit(solution)/shard_map/ppermute | solution.py:544
  5.1 0.7 copy-start.16
  6.7 18.4 %all-to-all-start = ((bf16[8,178,128]{2,1,0:T(8,128)(2,1)}), bf16[8,178,128]{2,1,0:T(8,128)(2,1)S(1)}, u32[]{:S(2)}, u32[]{:S(2)}) async-start(bf16[8,178,128]{2,1,0:T(8,128)(2,1)} %broadcast_in_dim.8), calls=%async_computation | async-start | bytes 753664 | tf_op jit(solution)/shard_map/all_to_all | solution.py:603
  13.9 6.5 %copy-start.14 = (bf16[32,16,3,3,3]{0,1,4,3,2:T(8,128)(2,1)S(1)}, bf16[32,16,3,3,3]{0,1,4,3,2:T(8,128)(2,1)}, u32[]{:S(2)}) copy-start(bf16[32,16,3,3,3]{0,1,4,3,2:T(8,128)(2,1)} %param.18) | copy-start | bytes 82948
  14.0 6.5 %collective-permute-start.2 = (bf16[3,14,16,128]{3,2,1,0:T(8,128)(2,1)S(1)}, bf16[3,14,16,128]{3,2,1,0:T(8,128)(2,1)S(1)}, u32[]{:S(2)}, u32[]{:S(2)}) collective-permute-start(bf16[3,14,16,128]{3,2,1,0:T(8,128)(2,1)S(1)} %get-tuple-element.79), channel_id=1, source_target_pairs={{0,8},{8,0},{16,24},{24,16},{32,40},{40,32},{48,56},{56,48},{64,72... | collective-permute-start | bytes 516104 | tf_op jit(solution)/shard_map/ppermute | solution.py:544
  15.7 9.7 %collective-permute-start.3 = (bf16[3,14,16,128]{3,2,1,0:T(8,128)(2,1)S(1)}, bf16[3,14,16,128]{3,2,1,0:T(8,128)(2,1)S(1)}, u32[]{:S(2)}, u32[]{:S(2)}) collective-permute-start(bf16[3,14,16,128]{3,2,1,0:T(8,128)(2,1)S(1)} %get-tuple-element.78), channel_id=1, source_target_pairs={{8,16},{24,32},{40,48},{56,64},{72,80},{88,96},{104,112},{120,128}... | collective-permute-start | bytes 516104 | tf_op jit(solution)/shard_map/ppermute | solution.py:544
  21.4 0.8 copy-start.8
  25.2 0.8 copy-start.10
  25.2 0.9 copy-start.11
  25.3 0.9 copy-start.9
  25.3 3.3 %collective-permute-start.4 = (bf16[8,162,128]{2,0,1:T(8,128)(2,1)S(1)}, bf16[8,162,128]{2,0,1:T(8,128)(2,1)S(1)}, u32[]{:S(2)}, u32[]{:S(2)}) collective-permute-start(bf16[8,162,128]{2,0,1:T(8,128)(2,1)S(1)} %copy.101), channel_id=1, source_target_pairs={{0,8},{8,0},{16,24},{24,16},{32,40},{40,32},{48,56},{56,48},{64,72... | collective-permute-start | bytes 995336 | tf_op jit(solution)/shard_map/ppermute | solution.py:548
  30.2 7.6 %collective-permute-start.6 = (bf16[192,128]{1,0:T(8,128)(2,1)S(1)}, bf16[192,128]{1,0:T(8,128)(2,1)S(1)}, u32[]{:S(2)}, u32[]{:S(2)}) collective-permute-start(bf16[192,128]{1,0:T(8,128)(2,1)S(1)} %get-tuple-element.37.own3), channel_id=1, source_target_pairs={{8,16},{24,32},{40,48},{56,64},{72,80},{88,96},{104,112},{120,128}... | collective-permute-start | bytes 147464 | tf_op jit(solution)/shard_map/ppermute | solution.py:544
  35.1 2.7 %collective-permute-start.5 = (bf16[192,128]{1,0:T(8,128)(2,1)S(1)}, bf16[192,128]{1,0:T(8,128)(2,1)S(1)}, u32[]{:S(2)}, u32[]{:S(2)}) collective-permute-start(bf16[192,128]{1,0:T(8,128)(2,1)S(1)} %get-tuple-element.37.own3), channel_id=1, source_target_pairs={{0,8},{8,0},{16,24},{24,16},{32,40},{40,32},{48,56},{56,48},{64,72... | collective-permute-start | bytes 147464 | tf_op jit(solution)/shard_map/ppermute | solution.py:544
  37.8 11.0 %copy-start.2 = (bf16[640,512]{1,0:T(8,128)(2,1)S(1)}, bf16[640,512]{1,0:T(8,128)(2,1)}, u32[]{:S(2)}) copy-start(bf16[640,512]{1,0:T(8,128)(2,1)} %constant.70.clone.planes_of) | copy-start | bytes 1966084
  37.8 11.0 %collective-permute-start.8 = (bf16[320,128]{1,0:T(8,128)(2,1)S(1)}, bf16[320,128]{1,0:T(8,128)(2,1)S(1)}, u32[]{:S(2)}, u32[]{:S(2)}) collective-permute-start(bf16[320,128]{1,0:T(8,128)(2,1)S(1)} %get-tuple-element.92), channel_id=1, source_target_pairs={{1,2},{3,4},{5,6},{2,1},{4,3},{6,5},{9,10},{11,12},{13,14},{10,9},... | collective-permute-start | bytes 245768 | tf_op jit(solution)/shard_map/ppermute | solution.py:544
  38.6 10.2 %collective-permute-start.7 = (bf16[320,128]{1,0:T(8,128)(2,1)S(1)}, bf16[320,128]{1,0:T(8,128)(2,1)S(1)}, u32[]{:S(2)}, u32[]{:S(2)}) collective-permute-start(bf16[320,128]{1,0:T(8,128)(2,1)S(1)} %get-tuple-element.93), channel_id=1, source_target_pairs={{0,1},{1,0},{2,3},{3,2},{4,5},{5,4},{6,7},{7,6},{8,9},{9,8},{10,11... | collective-permute-start | bytes 245768 | tf_op jit(solution)/shard_map/ppermute | solution.py:544
  42.9 5.9 %copy-start.3 = (bf16[256,768]{1,0:T(8,128)(2,1)S(1)}, bf16[256,768]{1,0:T(8,128)(2,1)}, u32[]{:S(2)}) copy-start(bf16[256,768]{1,0:T(8,128)(2,1)} %constant.71.clone.shift4) | copy-start | bytes 1179652
  42.9 5.9 %copy-start.7 = (bf16[256,128]{1,0:T(8,128)(2,1)S(1)}, bf16[256,128]{1,0:T(8,128)(2,1)}, u32[]{:S(2)}) copy-start(bf16[256,128]{1,0:T(8,128)(2,1)} %constant.69.clone.pool4) | copy-start | bytes 196612
  42.9 5.7 %collective-permute-start.10 = (bf16[192,128]{1,0:T(8,128)(2,1)S(1)}, bf16[192,128]{1,0:T(8,128)(2,1)S(1)}, u32[]{:S(2)}, u32[]{:S(2)}) collective-permute-start(bf16[192,128]{1,0:T(8,128)(2,1)S(1)} %pad_maximum_fusion.8), channel_id=1, source_target_pairs={{2,4},{3,5},{4,2},{5,3},{10,12},{11,13},{12,10},{13,11},{18,20},{1... | collective-permute-start | bytes 147464 | tf_op jit(solution)/shard_map/ppermute | solution.py:544
  43.7 5.1 %collective-permute-start.9 = (bf16[192,128]{1,0:T(8,128)(2,1)S(1)}, bf16[192,128]{1,0:T(8,128)(2,1)S(1)}, u32[]{:S(2)}, u32[]{:S(2)}) collective-permute-start(bf16[192,128]{1,0:T(8,128)(2,1)S(1)} %pad_maximum_fusion.8), channel_id=1, source_target_pairs={{0,2},{1,3},{2,0},{3,1},{4,6},{5,7},{6,4},{7,5},{8,10},{9,11},{10,... | collective-permute-start | bytes 147464 | tf_op jit(solution)/shard_map/ppermute | solution.py:544
  55.3 14.4 %copy-start.1 = (bf16[96,576]{1,0:T(8,128)(2,1)S(1)}, bf16[96,576]{1,0:T(8,128)(2,1)}, u32[]{:S(2)}) copy-start(bf16[96,576]{1,0:T(8,128)(2,1)} %reshape.95.w3b) | copy-start | bytes 331780
  55.3 14.4 %copy-start.4 = (bf16[256,384]{1,0:T(8,128)(2,1)S(1)}, bf16[256,384]{1,0:T(8,128)(2,1)}, u32[]{:S(2)}) copy-start(bf16[256,384]{1,0:T(8,128)(2,1)} %constant.74.clone.cross) | copy-start | bytes 589828
  55.3 14.4 %copy-start.5 = (bf16[128,384]{1,0:T(8,128)(2,1)S(1)}, bf16[128,384]{1,0:T(8,128)(2,1)}, u32[]{:S(2)}) copy-start(bf16[128,384]{1,0:T(8,128)(2,1)} %constant.73.clone.straight) | copy-start | bytes 294916
  55.3 14.4 %copy-start.6 = (bf16[128,256]{1,0:T(8,128)(2,1)S(1)}, bf16[128,256]{1,0:T(8,128)(2,1)}, u32[]{:S(2)}) copy-start(bf16[128,256]{1,0:T(8,128)(2,1)} %constant.75.clone.spread2) | copy-start | bytes 196612
  55.3 14.4 %copy-start.12 = (bf16[2,128,512]{2,1,0:T(8,128)(2,1)S(1)}, bf16[2,128,512]{2,1,0:T(8,128)(2,1)}, u32[]{:S(2)}) copy-start(bf16[2,128,512]{2,1,0:T(8,128)(2,1)} %get-tuple-element.49.sl2_mid) | copy-start | bytes 786436
  55.3 14.4 %copy-start.13 = (bf16[2,128,512]{2,1,0:T(8,128)(2,1)S(1)}, bf16[2,128,512]{2,1,0:T(8,128)(2,1)}, u32[]{:S(2)}) copy-start(bf16[2,128,512]{2,1,0:T(8,128)(2,1)} %get-tuple-element.50.sl2_edge) | copy-start | bytes 786436
  55.3 17.7 %all-to-all-start.1 = ((bf16[8,288,128]{2,1,0:T(8,128)(2,1)}), bf16[8,288,128]{2,1,0:T(8,128)(2,1)S(1)}, u32[]{:S(2)}, u32[]{:S(2)}) async-start(bf16[8,288,128]{2,1,0:T(8,128)(2,1)} %shard_map.196), calls=%async_computation.1 | async-start | bytes 1179648 | tf_op jit(solution)/shard_map/all_to_all | solution.py:707
  59.1 8.0 %collective-permute-start.11 = (bf16[64,768]{1,0:T(8,128)(2,1)S(1)}, bf16[64,768]{1,0:T(8,128)(2,1)S(1)}, u32[]{:S(2)}, u32[]{:S(2)}) collective-permute-start(bf16[64,768]{1,0:T(8,128)(2,1)S(1)} %get-tuple-element.46.near.own_near), channel_id=1, source_target_pairs={{0,8},{8,0},{16,24},{24,16},{32,40},{40,32},{48,56},{56,48},{64,72... | collective-permute-start | bytes 294920 | tf_op jit(solution)/shard_map/ppermute | solution.py:544
  61.9 7.8 %collective-permute-start.12 = (bf16[64,768]{1,0:T(8,128)(2,1)S(1)}, bf16[64,768]{1,0:T(8,128)(2,1)S(1)}, u32[]{:S(2)}, u32[]{:S(2)}) collective-permute-start(bf16[64,768]{1,0:T(8,128)(2,1)S(1)} %get-tuple-element.47.far.own_far), channel_id=1, source_target_pairs={{8,16},{24,32},{40,48},{56,64},{72,80},{88,96},{104,112},{120,128}... | collective-permute-start | bytes 294920 | tf_op jit(solution)/shard_map/ppermute | solution.py:544
  107.3 15.8 %all-to-all-start.4 = ((bf16[32,14,128]{2,1,0:T(8,128)(2,1)}), bf16[32,14,128]{2,1,0:T(8,128)(2,1)S(1)}, u32[]{:S(2)}, u32[]{:S(2)}) async-start(bf16[32,14,128]{2,1,0:T(8,128)(2,1)} %broadcast_in_dim.11), calls=%async_computation.4 | async-start | bytes 262144 | tf_op jit(solution)/shard_map/all_to_all | solution.py:554

commit v7 on v6

--- a/solution.py
+++ b/solution.py
@@ -517,8 +517,8 @@
         right = jnp.concatenate([d2[z + 2 - kz] for kz in range(3)], axis=0)
         part = dot_nt(left, right)
         total = part if total is None else total + part
-    g2[...] = jnp.zeros((160, 128), F32)
-    g2[0:144, 0:96] = total
+    g2[...] = jnp.zeros((160, 128), BF)
+    g2[0:144, 0:96] = total.astype(BF)
 
 
 def write_kernel(pos, whole, four, three, two):
@@ -710,7 +710,7 @@
 
     (g2,) = call(
         shallow_back_kernel,
-        (shape((160, 128), F32),),
+        (shape((160, 128), BF),),
         [
             pltpu.VMEM((4, 192, 768), BF),
             pltpu.VMEM((12, 32, 1024), BF),
@@ -726,7 +726,7 @@
         far_in=(11, 12),
     )
     pieces = jnp.concatenate(
-        [grads.reshape(32, 9, 128), g2.astype(BF).reshape(32, 5, 128)], axis=1
+        [grads.reshape(32, 9, 128), g2.reshape(32, 5, 128)], axis=1
     )
     pieces = lax.all_to_all(pieces, "gz", 0, 0, tiled=True).astype(F32).sum(axis=0)
     two = to_all(pieces[9:].astype(BF), "ch").astype(F32).sum(axis=0)

time: 125 us -> 125 us (level)
  no operation moved by 1% of the time
where the time goes in v7:
time: 125 us
  starting transfers between devices  48 us (38%)
  blocking collectives  33.3 us (27%)
  Pallas kernels  17.6 us (14%)
  waiting for transfers between devices  13 us (10%)
  local copies, waits for them, and re-layouts  10.3 us (8%)
  between operations  1.34 us (1%)
    ppermute x12, starting transfers between devices, swap(): return (lax.ppermute(one, axis, inside), lax.ppermute(two, axis, outside))  32 us
    all_to_all x1, blocking collectives, body(): lax.all_to_all(pieces, 'gz', 0, 0, tiled=True).astype(F32).sum(axis=0)  22.5 us
    pallas_call x7, Pallas kernels, call(): pl.pallas_call(kernel, out_shape=tuple((pltpu.HBM(o.shape, o.dtype) if n...  17.6 us
    all_to_all x1, blocking collectives, to_all(): return lax.all_to_all(copies, axis, 0, 0, tiled=True)  10.8 us
    all_to_all x1, waiting for transfers between devices, to_all(): return lax.all_to_all(copies, axis, 0, 0, tiled=True)  10.2 us
    all_to_all x1, starting transfers between devices, body(): all_of = lax.all_to_all(held, 'ch', 0, 0, tiled=True)  7.08 us
    all_to_all x1, starting transfers between devices, to_all(): return lax.all_to_all(copies, axis, 0, 0, tiled=True)  5.02 us
    unnamed x37, local copies, waits for them, and re-layouts  4.37 us
  transfers between devices with their start and end apart: 16, of which 3 were waited for; matrix products, arithmetic and copies ran while one was open for 6% of the time, Pallas kernels for 7%

profile of v7, /device:TPU:1, one launch (start us, length us, event | category | flops | bytes accessed | tf_op | source)
XLA Modules:
  0.0 124.5 jit_solution(736075842134043389)
XLA Ops:
  0.7 1.1 copy.107
  1.8 2.6 %collective-permute-start = (bf16[8,3,16,128]{3,2,1,0:T(8,128)(2,1)S(1)}, bf16[8,3,16,128]{3,2,1,0:T(8,128)(2,1)S(1)}, u32[]{:S(2)}, u32[]{:S(2)}) collective-permute-start(bf16[8,3,16,128]{3,2,1,0:T(8,128)(2,1)S(1)} %get-tuple-element.82), channel_id=1, source_target_pairs={{0,1},{1,0},{2,3},{3,2},{4,5},{5,4},{6,7},{7,6},{8,9},{9,8},{10,11... | collective-permute-start | bytes 294920 | tf_op jit(solution)/shard_map/ppermute | solution.py:544
  4.4 0.7 collective-permute-start.1
  5.1 0.1 reshape.84
  5.2 0.6 copy-done.16
  5.9 0.8 broadcast_in_dim.8
  6.7 7.1 %all-to-all-start = ((bf16[8,178,128]{2,1,0:T(8,128)(2,1)}), bf16[8,178,128]{2,1,0:T(8,128)(2,1)S(1)}, u32[]{:S(2)}, u32[]{:S(2)}) async-start(bf16[8,178,128]{2,1,0:T(8,128)(2,1)} %broadcast_in_dim.8), calls=%async_computation | async-start | bytes 753664 | tf_op jit(solution)/shard_map/all_to_all | solution.py:603
  14.0 1.6 %collective-permute-start.2 = (bf16[3,14,16,128]{3,2,1,0:T(8,128)(2,1)S(1)}, bf16[3,14,16,128]{3,2,1,0:T(8,128)(2,1)S(1)}, u32[]{:S(2)}, u32[]{:S(2)}) collective-permute-start(bf16[3,14,16,128]{3,2,1,0:T(8,128)(2,1)S(1)} %get-tuple-element.79), channel_id=1, source_target_pairs={{0,8},{8,0},{16,24},{24,16},{32,40},{40,32},{48,56},{56,48},{64,72... | collective-permute-start | bytes 516104 | tf_op jit(solution)/shard_map/ppermute | solution.py:544
  15.7 4.8 %collective-permute-start.3 = (bf16[3,14,16,128]{3,2,1,0:T(8,128)(2,1)S(1)}, bf16[3,14,16,128]{3,2,1,0:T(8,128)(2,1)S(1)}, u32[]{:S(2)}, u32[]{:S(2)}) collective-permute-start(bf16[3,14,16,128]{3,2,1,0:T(8,128)(2,1)S(1)} %get-tuple-element.78), channel_id=1, source_target_pairs={{8,16},{24,32},{40,48},{56,64},{72,80},{88,96},{104,112},{120,128}... | collective-permute-start | bytes 516104 | tf_op jit(solution)/shard_map/ppermute | solution.py:544
  20.5 0.1 copy.84
  20.6 0.3 pad_bitcast_fusion.3
  20.9 0.5 pad_maximum_fusion
  21.4 0.5 reshape.83.w2
  21.9 0.3 copy-done.8
  22.3 2.9 %shard_map.192 = (bf16[2,192,128]{2,1,0:T(8,128)(2,1)S(1)}, bf16[2,128,512]{2,1,0:T(8,128)(2,1)}, bf16[8,48,1280]{2,1,0:T(8,128)(2,1)}) custom-call(s32[2]{0:T(128)S(1)} %pad_add_fusion.pos, bf16[8,14,16,128]{3,2,1,0:T(8,128)(2,1)S(1)} %pad_maximum_fusion.1.mid, bf16[128,768]{1,0:T(8,128)(2,1)S(1)} %reshape.83.w2, bf16[128,256]{1,0:T(8,128)(2,1)S(1)} %copy-done.8), custom_call_target="tpu_custom_call" | custom-call | flops 2147483648 | bytes 1048576 | tf_op jit(solution)/shard_map/pallas_call | solution.py:159
  25.3 0.1 collective-permute-start.4
  25.4 0.6 copy-done.10
  26.1 2.4 %shard_map.193 = (bf16[4,96,768]{2,1,0:T(8,128)(2,1)S(1)}, bf16[256,128]{1,0:T(8,128)(2,1)S(1)}, bf16[2,128,512]{2,1,0:T(8,128)(2,1)}, bf16[2,48,1280]{2,1,0:T(8,128)(2,1)}) custom-call(s32[2]{0:T(128)S(1)} %pad_add_fusion.pos, bf16[3,14,16,128]{3,2,1,0:T(8,128)(2,1)S(1)} %collective-permute-done.2.near, bf16[8,14,16,128]{3,2,1,0:T(8,128)(2,1)S(1)} %pad_maximum_fusion.1.mid, ...), custom_call_target="tpu_custom_call" | custom-call | flops 4294967296 | bytes 1048576 | tf_op jit(solution)/shard_map/pallas_call | solution.py:159
  28.8 0.1 copy.89
  28.9 0.1 copy.90.w3
  29.0 1.2 shard_map.194
  30.2 4.9 %collective-permute-start.6 = (bf16[192,128]{1,0:T(8,128)(2,1)S(1)}, bf16[192,128]{1,0:T(8,128)(2,1)S(1)}, u32[]{:S(2)}, u32[]{:S(2)}) collective-permute-start(bf16[192,128]{1,0:T(8,128)(2,1)S(1)} %get-tuple-element.37.own3), channel_id=1, source_target_pairs={{8,16},{24,32},{40,48},{56,64},{72,80},{88,96},{104,112},{120,128}... | collective-permute-start | bytes 147464 | tf_op jit(solution)/shard_map/ppermute | solution.py:544
  35.1 0.1 collective-permute-start.5
  35.3 0.2 copy.95
  35.4 0.9 reshape.95.w3b
  36.5 0.4 copy.92
  36.9 0.9 copy.106
  37.8 0.8 collective-permute-start.8
  38.6 4.3 %collective-permute-start.7 = (bf16[320,128]{1,0:T(8,128)(2,1)S(1)}, bf16[320,128]{1,0:T(8,128)(2,1)S(1)}, u32[]{:S(2)}, u32[]{:S(2)}) collective-permute-start(bf16[320,128]{1,0:T(8,128)(2,1)S(1)} %get-tuple-element.93), channel_id=1, source_target_pairs={{0,1},{1,0},{2,3},{3,2},{4,5},{5,4},{6,7},{7,6},{8,9},{9,8},{10,11... | collective-permute-start | bytes 245768 | tf_op jit(solution)/shard_map/ppermute | solution.py:544
  42.9 0.8 collective-permute-start.10
  43.7 3.6 %collective-permute-start.9 = (bf16[192,128]{1,0:T(8,128)(2,1)S(1)}, bf16[192,128]{1,0:T(8,128)(2,1)S(1)}, u32[]{:S(2)}, u32[]{:S(2)}) collective-permute-start(bf16[192,128]{1,0:T(8,128)(2,1)S(1)} %pad_maximum_fusion.8), channel_id=1, source_target_pairs={{0,2},{1,3},{2,0},{3,1},{4,6},{5,7},{6,4},{7,5},{8,10},{9,11},{10,... | collective-permute-start | bytes 147464 | tf_op jit(solution)/shard_map/ppermute | solution.py:544
  47.3 1.3 %copy.96.w4f = bf16[384,576]{1,0:T(8,128)(2,1)S(1)} copy(bf16[384,576]{0,1:T(8,128)(2,1)} %bitcast.76) | data formatting | bytes 884736 | tf_op jit(solution)/shard_map/optimization_barrier | solution.py:667
  48.6 0.2 collective-permute-done.9.in2
  48.8 4.1 %shard_map.195 = (f32[128,128]{1,0:T(8,128)S(1)}, bf16[64,768]{1,0:T(8,128)(2,1)S(1)}, bf16[64,768]{1,0:T(8,128)(2,1)S(1)}, bf16[6,192,256]{2,1,0:T(8,128)(2,1)S(1)}, bf16[2,128,256]{2,1,0:T(8,128)(2,1)S(1)}) custom-call(s32[2]{0:T(128)S(1)} %pad_add_fusion.pos, bf16[192,128]{1,0:T(8,128)(2,1)S(1)} %get-tuple-element.37.own3, ...), custom_call_target="tpu_custom_call" | custom-call | flops 4294967296 | bytes 1048576 | tf_op jit(solution)/shard_map/pallas_call | solution.py:159
  52.9 2.4 %shard_map.196 = bf16[8,288,128]{2,1,0:T(8,128)(2,1)} custom-call(s32[2]{0:T(128)S(1)} %pad_add_fusion.pos, bf16[6,192,256]{2,1,0:T(8,128)(2,1)S(1)} %get-tuple-element.44.field, bf16[2,128,256]{2,1,0:T(8,128)(2,1)S(1)} %get-tuple-element.45.own, bf16[64,768]{1,0:T(8,128)(2,1)S(1)} %get-tuple-element.46.near.own_near, ...), custom_call_target="tpu_custom_call" | custom-call | flops 2147483648 | bytes 1048576 | tf_op jit(solution)/shard_map/pallas_call | solution.py:159
  55.3 3.8 %all-to-all-start.1 = ((bf16[8,288,128]{2,1,0:T(8,128)(2,1)}), bf16[8,288,128]{2,1,0:T(8,128)(2,1)S(1)}, u32[]{:S(2)}, u32[]{:S(2)}) async-start(bf16[8,288,128]{2,1,0:T(8,128)(2,1)} %shard_map.196), calls=%async_computation.1 | async-start | bytes 1179648 | tf_op jit(solution)/shard_map/all_to_all | solution.py:707
  59.1 2.7 %collective-permute-start.11 = (bf16[64,768]{1,0:T(8,128)(2,1)S(1)}, bf16[64,768]{1,0:T(8,128)(2,1)S(1)}, u32[]{:S(2)}, u32[]{:S(2)}) collective-permute-start(bf16[64,768]{1,0:T(8,128)(2,1)S(1)} %get-tuple-element.46.near.own_near), channel_id=1, source_target_pairs={{0,8},{8,0},{16,24},{24,16},{32,40},{40,32},{48,56},{56,48},{64,72... | collective-permute-start | bytes 294920 | tf_op jit(solution)/shard_map/ppermute | solution.py:544
  61.9 5.2 %collective-permute-start.12 = (bf16[64,768]{1,0:T(8,128)(2,1)S(1)}, bf16[64,768]{1,0:T(8,128)(2,1)S(1)}, u32[]{:S(2)}, u32[]{:S(2)}) collective-permute-start(bf16[64,768]{1,0:T(8,128)(2,1)S(1)} %get-tuple-element.47.far.own_far), channel_id=1, source_target_pairs={{8,16},{24,32},{40,48},{56,64},{72,80},{88,96},{104,112},{120,128}... | collective-permute-start | bytes 294920 | tf_op jit(solution)/shard_map/ppermute | solution.py:544
  67.1 2.6 %collective-permute-done.12.far = bf16[64,768]{1,0:T(8,128)(2,1)S(1)} collective-permute-done((bf16[64,768]{1,0:T(8,128)(2,1)S(1)}, bf16[64,768]{1,0:T(8,128)(2,1)S(1)}, u32[]{:S(2)}, u32[]{:S(2)}) %collective-permute-start.12) | collective-permute-done | bytes 98336 | tf_op jit(solution)/shard_map/ppermute | solution.py:544
  69.7 3.2 %shard_map.197 = bf16[160,128]{1,0:T(8,128)(2,1)S(1)} custom-call(s32[2]{0:T(128)S(1)} %pad_add_fusion.pos, bf16[64,768]{1,0:T(8,128)(2,1)S(1)} %get-tuple-element.46.near.own_near, bf16[64,768]{1,0:T(8,128)(2,1)S(1)} %get-tuple-element.47.far.own_far, bf16[64,768]{1,0:T(8,128)(2,1)S(1)} %collective-permute-done.11.near, ...), custom_call_target="tpu_custom_call" | custom-call | flops 4294967296 | bytes 1048576 | tf_op jit(solution)/shard_map/pallas_call | solution.py:159
  73.0 0.1 reduce_sum.30
  73.2 22.5 %all_to_all.25 = bf16[32,14,128]{2,1,0:T(8,128)(2,1)S(1)} all-to-all(bf16[32,14,128]{2,1,0:T(8,128)(2,1)S(1)} %pad_maximum_fusion.4), channel_id=1, replica_groups=mesh['gz'=32,'ch'=8] {'gz'}, dimensions={0} | all-to-all | bytes 229376 | tf_op jit(solution)/shard_map/all_to_all | solution.py:731
  95.7 10.8 %all_to_all.26 = bf16[8,5,128]{2,1,0:T(8,128)(2,1)S(1)} all-to-all(bf16[8,5,128]{2,1,0:T(8,128)(2,1)S(1)} %broadcast_in_dim.10), channel_id=1, replica_groups=mesh['gz'=32,'ch'=8] {'ch'}, dimensions={0} | all-to-all | bytes 20480 | tf_op jit(solution)/shard_map/all_to_all | solution.py:554
  106.6 0.7 broadcast_in_dim.11
  107.3 5.0 %all-to-all-start.4 = ((bf16[32,14,128]{2,1,0:T(8,128)(2,1)}), bf16[32,14,128]{2,1,0:T(8,128)(2,1)S(1)}, u32[]{:S(2)}, u32[]{:S(2)}) async-start(bf16[32,14,128]{2,1,0:T(8,128)(2,1)} %broadcast_in_dim.11), calls=%async_computation.4 | async-start | bytes 262144 | tf_op jit(solution)/shard_map/all_to_all | solution.py:554
  112.3 0.6 copy.98
  112.9 10.2 %all-to-all-done.4.whole = bf16[32,14,128]{2,1,0:T(8,128)(2,1)S(1)} async-done(((bf16[32,14,128]{2,1,0:T(8,128)(2,1)}), bf16[32,14,128]{2,1,0:T(8,128)(2,1)S(1)}, u32[]{:S(2)}, u32[]{:S(2)}) %all-to-all-start.4) | async-done | bytes 114720 | tf_op jit(solution)/shard_map/all_to_all | solution.py:554
  123.1 1.4 %shard_map.198 = (f32[216,128]{1,0:T(8,128)}, f32[27,4,64]{2,1,0:T(4,128)}, f32[3,144,32]{2,1,0:T(8,128)}) custom-call(s32[2]{0:T(128)S(1)} %pad_add_fusion.pos, bf16[32,14,128]{2,1,0:T(8,128)(2,1)S(1)} %all-to-all-done.4.whole), custom_call_target="tpu_custom_call" | custom-call | flops 1048576 | bytes 1048576 | tf_op jit(solution)/shard_map/pallas_call | solution.py:159
  (82 shorter events, 1.2 us)
Async XLA Ops:
  0.6 5.2 %copy-start = (bf16[128,8,3,3,3]{0,1,4,3,2:T(8,128)(2,1)S(1)}, bf16[128,8,3,3,3]{0,1,4,3,2:T(8,128)(2,1)}, u32[]{:S(2)}) copy-start(bf16[128,8,3,3,3]{0,1,4,3,2:T(8,128)(2,1)} %param.20) | copy-start | bytes 165892
  1.8 3.3 %copy-start.15 = (bf16[16,1,8,16]{3,2,1,0:T(8,128)(2,1)S(1)}, bf16[16,1,8,16]{3,2,1,0:T(8,128)(2,1)}, u32[]{:S(2)}) copy-start(bf16[16,1,8,16]{3,2,1,0:T(8,128)(2,1)} %param.21) | copy-start | bytes 12292
  1.8 12.0 %collective-permute-start = (bf16[8,3,16,128]{3,2,1,0:T(8,128)(2,1)S(1)}, bf16[8,3,16,128]{3,2,1,0:T(8,128)(2,1)S(1)}, u32[]{:S(2)}, u32[]{:S(2)}) collective-permute-start(bf16[8,3,16,128]{3,2,1,0:T(8,128)(2,1)S(1)} %get-tuple-element.82), channel_id=1, source_target_pairs={{0,1},{1,0},{2,3},{3,2},{4,5},{5,4},{6,7},{7,6},{8,9},{9,8},{10,11... | collective-permute-start | bytes 294920 | tf_op jit(solution)/shard_map/ppermute | solution.py:544
  4.4 9.4 %collective-permute-start.1 = (bf16[8,3,16,128]{3,2,1,0:T(8,128)(2,1)S(1)}, bf16[8,3,16,128]{3,2,1,0:T(8,128)(2,1)S(1)}, u32[]{:S(2)}, u32[]{:S(2)}) collective-permute-start(bf16[8,3,16,128]{3,2,1,0:T(8,128)(2,1)S(1)} %get-tuple-element.83), channel_id=1, source_target_pairs={{1,2},{3,4},{5,6},{2,1},{4,3},{6,5},{9,10},{11,12},{13,14},{10,9},... | collective-permute-start | bytes 294920 | tf_op jit(solution)/shard_map/ppermute | solution.py:544
  5.1 0.7 copy-start.16
  6.7 18.4 %all-to-all-start = ((bf16[8,178,128]{2,1,0:T(8,128)(2,1)}), bf16[8,178,128]{2,1,0:T(8,128)(2,1)S(1)}, u32[]{:S(2)}, u32[]{:S(2)}) async-start(bf16[8,178,128]{2,1,0:T(8,128)(2,1)} %broadcast_in_dim.8), calls=%async_computation | async-start | bytes 753664 | tf_op jit(solution)/shard_map/all_to_all | solution.py:603
  13.9 6.5 %copy-start.14 = (bf16[32,16,3,3,3]{0,1,4,3,2:T(8,128)(2,1)S(1)}, bf16[32,16,3,3,3]{0,1,4,3,2:T(8,128)(2,1)}, u32[]{:S(2)}) copy-start(bf16[32,16,3,3,3]{0,1,4,3,2:T(8,128)(2,1)} %param.18) | copy-start | bytes 82948
  14.0 6.5 %collective-permute-start.2 = (bf16[3,14,16,128]{3,2,1,0:T(8,128)(2,1)S(1)}, bf16[3,14,16,128]{3,2,1,0:T(8,128)(2,1)S(1)}, u32[]{:S(2)}, u32[]{:S(2)}) collective-permute-start(bf16[3,14,16,128]{3,2,1,0:T(8,128)(2,1)S(1)} %get-tuple-element.79), channel_id=1, source_target_pairs={{0,8},{8,0},{16,24},{24,16},{32,40},{40,32},{48,56},{56,48},{64,72... | collective-permute-start | bytes 516104 | tf_op jit(solution)/shard_map/ppermute | solution.py:544
  15.7 9.7 %collective-permute-start.3 = (bf16[3,14,16,128]{3,2,1,0:T(8,128)(2,1)S(1)}, bf16[3,14,16,128]{3,2,1,0:T(8,128)(2,1)S(1)}, u32[]{:S(2)}, u32[]{:S(2)}) collective-permute-start(bf16[3,14,16,128]{3,2,1,0:T(8,128)(2,1)S(1)} %get-tuple-element.78), channel_id=1, source_target_pairs={{8,16},{24,32},{40,48},{56,64},{72,80},{88,96},{104,112},{120,128}... | collective-permute-start | bytes 516104 | tf_op jit(solution)/shard_map/ppermute | solution.py:544
  21.4 0.8 copy-start.8
  25.2 0.8 copy-start.10
  25.2 0.9 copy-start.11
  25.3 0.9 copy-start.9
  25.3 3.3 %collective-permute-start.4 = (bf16[8,162,128]{2,0,1:T(8,128)(2,1)S(1)}, bf16[8,162,128]{2,0,1:T(8,128)(2,1)S(1)}, u32[]{:S(2)}, u32[]{:S(2)}) collective-permute-start(bf16[8,162,128]{2,0,1:T(8,128)(2,1)S(1)} %copy.101), channel_id=1, source_target_pairs={{0,8},{8,0},{16,24},{24,16},{32,40},{40,32},{48,56},{56,48},{64,72... | collective-permute-start | bytes 995336 | tf_op jit(solution)/shard_map/ppermute | solution.py:548
  30.2 7.6 %collective-permute-start.6 = (bf16[192,128]{1,0:T(8,128)(2,1)S(1)}, bf16[192,128]{1,0:T(8,128)(2,1)S(1)}, u32[]{:S(2)}, u32[]{:S(2)}) collective-permute-start(bf16[192,128]{1,0:T(8,128)(2,1)S(1)} %get-tuple-element.37.own3), channel_id=1, source_target_pairs={{8,16},{24,32},{40,48},{56,64},{72,80},{88,96},{104,112},{120,128}... | collective-permute-start | bytes 147464 | tf_op jit(solution)/shard_map/ppermute | solution.py:544
  35.1 2.7 %collective-permute-start.5 = (bf16[192,128]{1,0:T(8,128)(2,1)S(1)}, bf16[192,128]{1,0:T(8,128)(2,1)S(1)}, u32[]{:S(2)}, u32[]{:S(2)}) collective-permute-start(bf16[192,128]{1,0:T(8,128)(2,1)S(1)} %get-tuple-element.37.own3), channel_id=1, source_target_pairs={{0,8},{8,0},{16,24},{24,16},{32,40},{40,32},{48,56},{56,48},{64,72... | collective-permute-start | bytes 147464 | tf_op jit(solution)/shard_map/ppermute | solution.py:544
  37.8 11.0 %copy-start.2 = (bf16[640,512]{1,0:T(8,128)(2,1)S(1)}, bf16[640,512]{1,0:T(8,128)(2,1)}, u32[]{:S(2)}) copy-start(bf16[640,512]{1,0:T(8,128)(2,1)} %constant.70.clone.planes_of) | copy-start | bytes 1966084
  37.8 11.0 %collective-permute-start.8 = (bf16[320,128]{1,0:T(8,128)(2,1)S(1)}, bf16[320,128]{1,0:T(8,128)(2,1)S(1)}, u32[]{:S(2)}, u32[]{:S(2)}) collective-permute-start(bf16[320,128]{1,0:T(8,128)(2,1)S(1)} %get-tuple-element.92), channel_id=1, source_target_pairs={{1,2},{3,4},{5,6},{2,1},{4,3},{6,5},{9,10},{11,12},{13,14},{10,9},... | collective-permute-start | bytes 245768 | tf_op jit(solution)/shard_map/ppermute | solution.py:544
  38.6 10.2 %collective-permute-start.7 = (bf16[320,128]{1,0:T(8,128)(2,1)S(1)}, bf16[320,128]{1,0:T(8,128)(2,1)S(1)}, u32[]{:S(2)}, u32[]{:S(2)}) collective-permute-start(bf16[320,128]{1,0:T(8,128)(2,1)S(1)} %get-tuple-element.93), channel_id=1, source_target_pairs={{0,1},{1,0},{2,3},{3,2},{4,5},{5,4},{6,7},{7,6},{8,9},{9,8},{10,11... | collective-permute-start | bytes 245768 | tf_op jit(solution)/shard_map/ppermute | solution.py:544
  42.9 5.9 %copy-start.3 = (bf16[256,768]{1,0:T(8,128)(2,1)S(1)}, bf16[256,768]{1,0:T(8,128)(2,1)}, u32[]{:S(2)}) copy-start(bf16[256,768]{1,0:T(8,128)(2,1)} %constant.71.clone.shift4) | copy-start | bytes 1179652
  42.9 5.9 %copy-start.7 = (bf16[256,128]{1,0:T(8,128)(2,1)S(1)}, bf16[256,128]{1,0:T(8,128)(2,1)}, u32[]{:S(2)}) copy-start(bf16[256,128]{1,0:T(8,128)(2,1)} %constant.69.clone.pool4) | copy-start | bytes 196612
  42.9 5.7 %collective-permute-start.10 = (bf16[192,128]{1,0:T(8,128)(2,1)S(1)}, bf16[192,128]{1,0:T(8,128)(2,1)S(1)}, u32[]{:S(2)}, u32[]{:S(2)}) collective-permute-start(bf16[192,128]{1,0:T(8,128)(2,1)S(1)} %pad_maximum_fusion.8), channel_id=1, source_target_pairs={{2,4},{3,5},{4,2},{5,3},{10,12},{11,13},{12,10},{13,11},{18,20},{1... | collective-permute-start | bytes 147464 | tf_op jit(solution)/shard_map/ppermute | solution.py:544
  43.7 5.1 %collective-permute-start.9 = (bf16[192,128]{1,0:T(8,128)(2,1)S(1)}, bf16[192,128]{1,0:T(8,128)(2,1)S(1)}, u32[]{:S(2)}, u32[]{:S(2)}) collective-permute-start(bf16[192,128]{1,0:T(8,128)(2,1)S(1)} %pad_maximum_fusion.8), channel_id=1, source_target_pairs={{0,2},{1,3},{2,0},{3,1},{4,6},{5,7},{6,4},{7,5},{8,10},{9,11},{10,... | collective-permute-start | bytes 147464 | tf_op jit(solution)/shard_map/ppermute | solution.py:544
  55.3 14.4 %copy-start.1 = (bf16[96,576]{1,0:T(8,128)(2,1)S(1)}, bf16[96,576]{1,0:T(8,128)(2,1)}, u32[]{:S(2)}) copy-start(bf16[96,576]{1,0:T(8,128)(2,1)} %reshape.95.w3b) | copy-start | bytes 331780
  55.3 14.4 %copy-start.4 = (bf16[256,384]{1,0:T(8,128)(2,1)S(1)}, bf16[256,384]{1,0:T(8,128)(2,1)}, u32[]{:S(2)}) copy-start(bf16[256,384]{1,0:T(8,128)(2,1)} %constant.74.clone.cross) | copy-start | bytes 589828
  55.3 14.4 %copy-start.5 = (bf16[128,384]{1,0:T(8,128)(2,1)S(1)}, bf16[128,384]{1,0:T(8,128)(2,1)}, u32[]{:S(2)}) copy-start(bf16[128,384]{1,0:T(8,128)(2,1)} %constant.73.clone.straight) | copy-start | bytes 294916
  55.3 14.4 %copy-start.6 = (bf16[128,256]{1,0:T(8,128)(2,1)S(1)}, bf16[128,256]{1,0:T(8,128)(2,1)}, u32[]{:S(2)}) copy-start(bf16[128,256]{1,0:T(8,128)(2,1)} %constant.75.clone.spread2) | copy-start | bytes 196612
  55.3 14.4 %copy-start.12 = (bf16[2,128,512]{2,1,0:T(8,128)(2,1)S(1)}, bf16[2,128,512]{2,1,0:T(8,128)(2,1)}, u32[]{:S(2)}) copy-start(bf16[2,128,512]{2,1,0:T(8,128)(2,1)} %get-tuple-element.49.sl2_mid) | copy-start | bytes 786436
  55.3 14.4 %copy-start.13 = (bf16[2,128,512]{2,1,0:T(8,128)(2,1)S(1)}, bf16[2,128,512]{2,1,0:T(8,128)(2,1)}, u32[]{:S(2)}) copy-start(bf16[2,128,512]{2,1,0:T(8,128)(2,1)} %get-tuple-element.50.sl2_edge) | copy-start | bytes 786436
  55.3 17.7 %all-to-all-start.1 = ((bf16[8,288,128]{2,1,0:T(8,128)(2,1)}), bf16[8,288,128]{2,1,0:T(8,128)(2,1)S(1)}, u32[]{:S(2)}, u32[]{:S(2)}) async-start(bf16[8,288,128]{2,1,0:T(8,128)(2,1)} %shard_map.196), calls=%async_computation.1 | async-start | bytes 1179648 | tf_op jit(solution)/shard_map/all_to_all | solution.py:707
  59.1 8.0 %collective-permute-start.11 = (bf16[64,768]{1,0:T(8,128)(2,1)S(1)}, bf16[64,768]{1,0:T(8,128)(2,1)S(1)}, u32[]{:S(2)}, u32[]{:S(2)}) collective-permute-start(bf16[64,768]{1,0:T(8,128)(2,1)S(1)} %get-tuple-element.46.near.own_near), channel_id=1, source_target_pairs={{0,8},{8,0},{16,24},{24,16},{32,40},{40,32},{48,56},{56,48},{64,72... | collective-permute-start | bytes 294920 | tf_op jit(solution)/shard_map/ppermute | solution.py:544
  61.9 7.8 %collective-permute-start.12 = (bf16[64,768]{1,0:T(8,128)(2,1)S(1)}, bf16[64,768]{1,0:T(8,128)(2,1)S(1)}, u32[]{:S(2)}, u32[]{:S(2)}) collective-permute-start(bf16[64,768]{1,0:T(8,128)(2,1)S(1)} %get-tuple-element.47.far.own_far), channel_id=1, source_target_pairs={{8,16},{24,32},{40,48},{56,64},{72,80},{88,96},{104,112},{120,128}... | collective-permute-start | bytes 294920 | tf_op jit(solution)/shard_map/ppermute | solution.py:544
  107.3 15.8 %all-to-all-start.4 = ((bf16[32,14,128]{2,1,0:T(8,128)(2,1)}), bf16[32,14,128]{2,1,0:T(8,128)(2,1)S(1)}, u32[]{:S(2)}, u32[]{:S(2)}) async-start(bf16[32,14,128]{2,1,0:T(8,128)(2,1)} %broadcast_in_dim.11), calls=%async_computation.4 | async-start | bytes 262144 | tf_op jit(solution)/shard_map/all_to_all | solution.py:554

commit v8 on v6

--- a/solution.py
+++ b/solution.py
@@ -701,7 +701,7 @@
         grads_kernel,
         (shape((8, 288, 128), BF),),
         [pltpu.VMEM((8, 288, 128), F32)],
-        1 << 31,
+        1 << 34,
         (pos, field4, own4, own_near, own_far, p4, vq),
     )
     got = lax.all_to_all(sent, "ch", 0, 0, tiled=True)

time: 125 us -> 125 us (level)
  no operation moved by 1% of the time
where the time goes in v8:
time: 125 us
  starting transfers between devices  48 us (38%)
  blocking collectives  33.3 us (27%)
  Pallas kernels  17.6 us (14%)
  waiting for transfers between devices  13 us (10%)
  local copies, waits for them, and re-layouts  10.3 us (8%)
  between operations  1.35 us (1%)
    ppermute x12, starting transfers between devices, swap(): return (lax.ppermute(one, axis, inside), lax.ppermute(two, axis, outside))  32 us
    all_to_all x1, blocking collectives, body(): lax.all_to_all(pieces, 'gz', 0, 0, tiled=True).astype(F32).sum(axis=0)  22.5 us
    pallas_call x7, Pallas kernels, call(): pl.pallas_call(kernel, out_shape=tuple((pltpu.HBM(o.shape, o.dtype) if n...  17.6 us
    all_to_all x1, blocking collectives, to_all(): return lax.all_to_all(copies, axis, 0, 0, tiled=True)  10.8 us
    all_to_all x1, waiting for transfers between devices, to_all(): return lax.all_to_all(copies, axis, 0, 0, tiled=True)  10.2 us
    all_to_all x1, starting transfers between devices, body(): all_of = lax.all_to_all(held, 'ch', 0, 0, tiled=True)  7.08 us
    all_to_all x1, starting transfers between devices, to_all(): return lax.all_to_all(copies, axis, 0, 0, tiled=True)  5.02 us
    unnamed x37, local copies, waits for them, and re-layouts  4.37 us
  transfers between devices with their start and end apart: 16, of which 3 were waited for; matrix products, arithmetic and copies ran while one was open for 6% of the time, Pallas kernels for 7%

profile of v8, /device:TPU:1, one launch (start us, length us, event | category | flops | bytes accessed | tf_op | source)
XLA Modules:
  0.0 124.6 jit_solution(5133698383309898005)
XLA Ops:
  0.7 1.1 copy.107
  1.8 2.6 %collective-permute-start = (bf16[8,3,16,128]{3,2,1,0:T(8,128)(2,1)S(1)}, bf16[8,3,16,128]{3,2,1,0:T(8,128)(2,1)S(1)}, u32[]{:S(2)}, u32[]{:S(2)}) collective-permute-start(bf16[8,3,16,128]{3,2,1,0:T(8,128)(2,1)S(1)} %get-tuple-element.82), channel_id=1, source_target_pairs={{0,1},{1,0},{2,3},{3,2},{4,5},{5,4},{6,7},{7,6},{8,9},{9,8},{10,11... | collective-permute-start | bytes 294920 | tf_op jit(solution)/shard_map/ppermute | solution.py:544
  4.4 0.7 collective-permute-start.1
  5.1 0.1 reshape.84
  5.2 0.6 copy-done.16
  5.9 0.8 broadcast_in_dim.8
  6.7 7.1 %all-to-all-start = ((bf16[8,178,128]{2,1,0:T(8,128)(2,1)}), bf16[8,178,128]{2,1,0:T(8,128)(2,1)S(1)}, u32[]{:S(2)}, u32[]{:S(2)}) async-start(bf16[8,178,128]{2,1,0:T(8,128)(2,1)} %broadcast_in_dim.8), calls=%async_computation | async-start | bytes 753664 | tf_op jit(solution)/shard_map/all_to_all | solution.py:603
  14.0 1.6 %collective-permute-start.2 = (bf16[3,14,16,128]{3,2,1,0:T(8,128)(2,1)S(1)}, bf16[3,14,16,128]{3,2,1,0:T(8,128)(2,1)S(1)}, u32[]{:S(2)}, u32[]{:S(2)}) collective-permute-start(bf16[3,14,16,128]{3,2,1,0:T(8,128)(2,1)S(1)} %get-tuple-element.79), channel_id=1, source_target_pairs={{0,8},{8,0},{16,24},{24,16},{32,40},{40,32},{48,56},{56,48},{64,72... | collective-permute-start | bytes 516104 | tf_op jit(solution)/shard_map/ppermute | solution.py:544
  15.7 4.8 %collective-permute-start.3 = (bf16[3,14,16,128]{3,2,1,0:T(8,128)(2,1)S(1)}, bf16[3,14,16,128]{3,2,1,0:T(8,128)(2,1)S(1)}, u32[]{:S(2)}, u32[]{:S(2)}) collective-permute-start(bf16[3,14,16,128]{3,2,1,0:T(8,128)(2,1)S(1)} %get-tuple-element.78), channel_id=1, source_target_pairs={{8,16},{24,32},{40,48},{56,64},{72,80},{88,96},{104,112},{120,128}... | collective-permute-start | bytes 516104 | tf_op jit(solution)/shard_map/ppermute | solution.py:544
  20.5 0.1 copy.84
  20.6 0.3 pad_bitcast_fusion.3
  20.9 0.5 pad_maximum_fusion
  21.4 0.5 reshape.83.w2
  21.9 0.3 copy-done.8
  22.3 2.9 %shard_map.192 = (bf16[2,192,128]{2,1,0:T(8,128)(2,1)S(1)}, bf16[2,128,512]{2,1,0:T(8,128)(2,1)}, bf16[8,48,1280]{2,1,0:T(8,128)(2,1)}) custom-call(s32[2]{0:T(128)S(1)} %pad_add_fusion.pos, bf16[8,14,16,128]{3,2,1,0:T(8,128)(2,1)S(1)} %pad_maximum_fusion.1.mid, bf16[128,768]{1,0:T(8,128)(2,1)S(1)} %reshape.83.w2, bf16[128,256]{1,0:T(8,128)(2,1)S(1)} %copy-done.8), custom_call_target="tpu_custom_call" | custom-call | flops 2147483648 | bytes 1048576 | tf_op jit(solution)/shard_map/pallas_call | solution.py:159
  25.3 0.1 collective-permute-start.4
  25.4 0.6 copy-done.10
  26.1 2.4 %shard_map.193 = (bf16[4,96,768]{2,1,0:T(8,128)(2,1)S(1)}, bf16[256,128]{1,0:T(8,128)(2,1)S(1)}, bf16[2,128,512]{2,1,0:T(8,128)(2,1)}, bf16[2,48,1280]{2,1,0:T(8,128)(2,1)}) custom-call(s32[2]{0:T(128)S(1)} %pad_add_fusion.pos, bf16[3,14,16,128]{3,2,1,0:T(8,128)(2,1)S(1)} %collective-permute-done.2.near, bf16[8,14,16,128]{3,2,1,0:T(8,128)(2,1)S(1)} %pad_maximum_fusion.1.mid, ...), custom_call_target="tpu_custom_call" | custom-call | flops 4294967296 | bytes 1048576 | tf_op jit(solution)/shard_map/pallas_call | solution.py:159
  28.8 0.1 copy.89
  28.9 0.1 copy.90.w3
  29.0 1.2 shard_map.194
  30.2 4.9 %collective-permute-start.6 = (bf16[192,128]{1,0:T(8,128)(2,1)S(1)}, bf16[192,128]{1,0:T(8,128)(2,1)S(1)}, u32[]{:S(2)}, u32[]{:S(2)}) collective-permute-start(bf16[192,128]{1,0:T(8,128)(2,1)S(1)} %get-tuple-element.37.own3), channel_id=1, source_target_pairs={{8,16},{24,32},{40,48},{56,64},{72,80},{88,96},{104,112},{120,128}... | collective-permute-start | bytes 147464 | tf_op jit(solution)/shard_map/ppermute | solution.py:544
  35.1 0.1 collective-permute-start.5
  35.3 0.2 copy.95
  35.4 0.9 reshape.95.w3b
  36.5 0.4 copy.92
  36.9 0.9 copy.106
  37.8 0.8 collective-permute-start.8
  38.6 4.3 %collective-permute-start.7 = (bf16[320,128]{1,0:T(8,128)(2,1)S(1)}, bf16[320,128]{1,0:T(8,128)(2,1)S(1)}, u32[]{:S(2)}, u32[]{:S(2)}) collective-permute-start(bf16[320,128]{1,0:T(8,128)(2,1)S(1)} %get-tuple-element.93), channel_id=1, source_target_pairs={{0,1},{1,0},{2,3},{3,2},{4,5},{5,4},{6,7},{7,6},{8,9},{9,8},{10,11... | collective-permute-start | bytes 245768 | tf_op jit(solution)/shard_map/ppermute | solution.py:544
  42.9 0.8 collective-permute-start.10
  43.7 3.6 %collective-permute-start.9 = (bf16[192,128]{1,0:T(8,128)(2,1)S(1)}, bf16[192,128]{1,0:T(8,128)(2,1)S(1)}, u32[]{:S(2)}, u32[]{:S(2)}) collective-permute-start(bf16[192,128]{1,0:T(8,128)(2,1)S(1)} %pad_maximum_fusion.8), channel_id=1, source_target_pairs={{0,2},{1,3},{2,0},{3,1},{4,6},{5,7},{6,4},{7,5},{8,10},{9,11},{10,... | collective-permute-start | bytes 147464 | tf_op jit(solution)/shard_map/ppermute | solution.py:544
  47.3 1.3 %copy.96.w4f = bf16[384,576]{1,0:T(8,128)(2,1)S(1)} copy(bf16[384,576]{0,1:T(8,128)(2,1)} %bitcast.76) | data formatting | bytes 884736 | tf_op jit(solution)/shard_map/optimization_barrier | solution.py:667
  48.6 0.2 collective-permute-done.9.in2
  48.8 4.1 %shard_map.195 = (f32[128,128]{1,0:T(8,128)S(1)}, bf16[64,768]{1,0:T(8,128)(2,1)S(1)}, bf16[64,768]{1,0:T(8,128)(2,1)S(1)}, bf16[6,192,256]{2,1,0:T(8,128)(2,1)S(1)}, bf16[2,128,256]{2,1,0:T(8,128)(2,1)S(1)}) custom-call(s32[2]{0:T(128)S(1)} %pad_add_fusion.pos, bf16[192,128]{1,0:T(8,128)(2,1)S(1)} %get-tuple-element.37.own3, ...), custom_call_target="tpu_custom_call" | custom-call | flops 4294967296 | bytes 1048576 | tf_op jit(solution)/shard_map/pallas_call | solution.py:159
  52.9 2.4 %shard_map.196 = bf16[8,288,128]{2,1,0:T(8,128)(2,1)} custom-call(s32[2]{0:T(128)S(1)} %pad_add_fusion.pos, bf16[6,192,256]{2,1,0:T(8,128)(2,1)S(1)} %get-tuple-element.44.field, bf16[2,128,256]{2,1,0:T(8,128)(2,1)S(1)} %get-tuple-element.45.own, bf16[64,768]{1,0:T(8,128)(2,1)S(1)} %get-tuple-element.46.near.own_near, ...), custom_call_target="tpu_custom_call" | custom-call | flops 17179869184 | bytes 1048576 | tf_op jit(solution)/shard_map/pallas_call | solution.py:159
  55.3 3.8 %all-to-all-start.1 = ((bf16[8,288,128]{2,1,0:T(8,128)(2,1)}), bf16[8,288,128]{2,1,0:T(8,128)(2,1)S(1)}, u32[]{:S(2)}, u32[]{:S(2)}) async-start(bf16[8,288,128]{2,1,0:T(8,128)(2,1)} %shard_map.196), calls=%async_computation.1 | async-start | bytes 1179648 | tf_op jit(solution)/shard_map/all_to_all | solution.py:707
  59.1 2.7 %collective-permute-start.11 = (bf16[64,768]{1,0:T(8,128)(2,1)S(1)}, bf16[64,768]{1,0:T(8,128)(2,1)S(1)}, u32[]{:S(2)}, u32[]{:S(2)}) collective-permute-start(bf16[64,768]{1,0:T(8,128)(2,1)S(1)} %get-tuple-element.46.near.own_near), channel_id=1, source_target_pairs={{0,8},{8,0},{16,24},{24,16},{32,40},{40,32},{48,56},{56,48},{64,72... | collective-permute-start | bytes 294920 | tf_op jit(solution)/shard_map/ppermute | solution.py:544
  61.9 5.2 %collective-permute-start.12 = (bf16[64,768]{1,0:T(8,128)(2,1)S(1)}, bf16[64,768]{1,0:T(8,128)(2,1)S(1)}, u32[]{:S(2)}, u32[]{:S(2)}) collective-permute-start(bf16[64,768]{1,0:T(8,128)(2,1)S(1)} %get-tuple-element.47.far.own_far), channel_id=1, source_target_pairs={{8,16},{24,32},{40,48},{56,64},{72,80},{88,96},{104,112},{120,128}... | collective-permute-start | bytes 294920 | tf_op jit(solution)/shard_map/ppermute | solution.py:544
  67.1 2.6 %collective-permute-done.12.far = bf16[64,768]{1,0:T(8,128)(2,1)S(1)} collective-permute-done((bf16[64,768]{1,0:T(8,128)(2,1)S(1)}, bf16[64,768]{1,0:T(8,128)(2,1)S(1)}, u32[]{:S(2)}, u32[]{:S(2)}) %collective-permute-start.12) | collective-permute-done | bytes 98336 | tf_op jit(solution)/shard_map/ppermute | solution.py:544
  69.7 3.2 %shard_map.197 = f32[160,128]{1,0:T(8,128)S(1)} custom-call(s32[2]{0:T(128)S(1)} %pad_add_fusion.pos, bf16[64,768]{1,0:T(8,128)(2,1)S(1)} %get-tuple-element.46.near.own_near, bf16[64,768]{1,0:T(8,128)(2,1)S(1)} %get-tuple-element.47.far.own_far, bf16[64,768]{1,0:T(8,128)(2,1)S(1)} %collective-permute-done.11.near, ...), custom_call_target="tpu_custom_call" | custom-call | flops 4294967296 | bytes 1048576 | tf_op jit(solution)/shard_map/pallas_call | solution.py:159
  73.0 0.1 reduce_sum.30
  73.2 22.5 %all_to_all.25 = bf16[32,14,128]{2,1,0:T(8,128)(2,1)S(1)} all-to-all(bf16[32,14,128]{2,1,0:T(8,128)(2,1)S(1)} %pad_maximum_fusion.4), channel_id=1, replica_groups=mesh['gz'=32,'ch'=8] {'gz'}, dimensions={0} | all-to-all | bytes 229376 | tf_op jit(solution)/shard_map/all_to_all | solution.py:731
  95.7 10.8 %all_to_all.26 = bf16[8,5,128]{2,1,0:T(8,128)(2,1)S(1)} all-to-all(bf16[8,5,128]{2,1,0:T(8,128)(2,1)S(1)} %broadcast_in_dim.10), channel_id=1, replica_groups=mesh['gz'=32,'ch'=8] {'ch'}, dimensions={0} | all-to-all | bytes 20480 | tf_op jit(solution)/shard_map/all_to_all | solution.py:554
  106.6 0.7 broadcast_in_dim.11
  107.3 5.0 %all-to-all-start.4 = ((bf16[32,14,128]{2,1,0:T(8,128)(2,1)}), bf16[32,14,128]{2,1,0:T(8,128)(2,1)S(1)}, u32[]{:S(2)}, u32[]{:S(2)}) async-start(bf16[32,14,128]{2,1,0:T(8,128)(2,1)} %broadcast_in_dim.11), calls=%async_computation.4 | async-start | bytes 262144 | tf_op jit(solution)/shard_map/all_to_all | solution.py:554
  112.3 0.6 copy.98
  112.9 10.2 %all-to-all-done.4.whole = bf16[32,14,128]{2,1,0:T(8,128)(2,1)S(1)} async-done(((bf16[32,14,128]{2,1,0:T(8,128)(2,1)}), bf16[32,14,128]{2,1,0:T(8,128)(2,1)S(1)}, u32[]{:S(2)}, u32[]{:S(2)}) %all-to-all-start.4) | async-done | bytes 114720 | tf_op jit(solution)/shard_map/all_to_all | solution.py:554
  123.1 1.4 %shard_map.198 = (f32[216,128]{1,0:T(8,128)}, f32[27,4,64]{2,1,0:T(4,128)}, f32[3,144,32]{2,1,0:T(8,128)}) custom-call(s32[2]{0:T(128)S(1)} %pad_add_fusion.pos, bf16[32,14,128]{2,1,0:T(8,128)(2,1)S(1)} %all-to-all-done.4.whole), custom_call_target="tpu_custom_call" | custom-call | flops 1048576 | bytes 1048576 | tf_op jit(solution)/shard_map/pallas_call | solution.py:159
  (83 shorter events, 1.2 us)
Async XLA Ops:
  0.6 5.2 %copy-start = (bf16[128,8,3,3,3]{0,1,4,3,2:T(8,128)(2,1)S(1)}, bf16[128,8,3,3,3]{0,1,4,3,2:T(8,128)(2,1)}, u32[]{:S(2)}) copy-start(bf16[128,8,3,3,3]{0,1,4,3,2:T(8,128)(2,1)} %param.20) | copy-start | bytes 165892
  1.8 3.3 %copy-start.15 = (bf16[16,1,8,16]{3,2,1,0:T(8,128)(2,1)S(1)}, bf16[16,1,8,16]{3,2,1,0:T(8,128)(2,1)}, u32[]{:S(2)}) copy-start(bf16[16,1,8,16]{3,2,1,0:T(8,128)(2,1)} %param.21) | copy-start | bytes 12292
  1.8 12.0 %collective-permute-start = (bf16[8,3,16,128]{3,2,1,0:T(8,128)(2,1)S(1)}, bf16[8,3,16,128]{3,2,1,0:T(8,128)(2,1)S(1)}, u32[]{:S(2)}, u32[]{:S(2)}) collective-permute-start(bf16[8,3,16,128]{3,2,1,0:T(8,128)(2,1)S(1)} %get-tuple-element.82), channel_id=1, source_target_pairs={{0,1},{1,0},{2,3},{3,2},{4,5},{5,4},{6,7},{7,6},{8,9},{9,8},{10,11... | collective-permute-start | bytes 294920 | tf_op jit(solution)/shard_map/ppermute | solution.py:544
  4.4 9.4 %collective-permute-start.1 = (bf16[8,3,16,128]{3,2,1,0:T(8,128)(2,1)S(1)}, bf16[8,3,16,128]{3,2,1,0:T(8,128)(2,1)S(1)}, u32[]{:S(2)}, u32[]{:S(2)}) collective-permute-start(bf16[8,3,16,128]{3,2,1,0:T(8,128)(2,1)S(1)} %get-tuple-element.83), channel_id=1, source_target_pairs={{1,2},{3,4},{5,6},{2,1},{4,3},{6,5},{9,10},{11,12},{13,14},{10,9},... | collective-permute-start | bytes 294920 | tf_op jit(solution)/shard_map/ppermute | solution.py:544
  5.1 0.7 copy-start.16
  6.7 18.4 %all-to-all-start = ((bf16[8,178,128]{2,1,0:T(8,128)(2,1)}), bf16[8,178,128]{2,1,0:T(8,128)(2,1)S(1)}, u32[]{:S(2)}, u32[]{:S(2)}) async-start(bf16[8,178,128]{2,1,0:T(8,128)(2,1)} %broadcast_in_dim.8), calls=%async_computation | async-start | bytes 753664 | tf_op jit(solution)/shard_map/all_to_all | solution.py:603
  13.9 6.5 %copy-start.14 = (bf16[32,16,3,3,3]{0,1,4,3,2:T(8,128)(2,1)S(1)}, bf16[32,16,3,3,3]{0,1,4,3,2:T(8,128)(2,1)}, u32[]{:S(2)}) copy-start(bf16[32,16,3,3,3]{0,1,4,3,2:T(8,128)(2,1)} %param.18) | copy-start | bytes 82948
  14.0 6.5 %collective-permute-start.2 = (bf16[3,14,16,128]{3,2,1,0:T(8,128)(2,1)S(1)}, bf16[3,14,16,128]{3,2,1,0:T(8,128)(2,1)S(1)}, u32[]{:S(2)}, u32[]{:S(2)}) collective-permute-start(bf16[3,14,16,128]{3,2,1,0:T(8,128)(2,1)S(1)} %get-tuple-element.79), channel_id=1, source_target_pairs={{0,8},{8,0},{16,24},{24,16},{32,40},{40,32},{48,56},{56,48},{64,72... | collective-permute-start | bytes 516104 | tf_op jit(solution)/shard_map/ppermute | solution.py:544
  15.7 9.7 %collective-permute-start.3 = (bf16[3,14,16,128]{3,2,1,0:T(8,128)(2,1)S(1)}, bf16[3,14,16,128]{3,2,1,0:T(8,128)(2,1)S(1)}, u32[]{:S(2)}, u32[]{:S(2)}) collective-permute-start(bf16[3,14,16,128]{3,2,1,0:T(8,128)(2,1)S(1)} %get-tuple-element.78), channel_id=1, source_target_pairs={{8,16},{24,32},{40,48},{56,64},{72,80},{88,96},{104,112},{120,128}... | collective-permute-start | bytes 516104 | tf_op jit(solution)/shard_map/ppermute | solution.py:544
  21.4 0.8 copy-start.8
  25.2 0.8 copy-start.10
  25.2 0.9 copy-start.11
  25.3 0.9 copy-start.9
  25.3 3.3 %collective-permute-start.4 = (bf16[8,162,128]{2,0,1:T(8,128)(2,1)S(1)}, bf16[8,162,128]{2,0,1:T(8,128)(2,1)S(1)}, u32[]{:S(2)}, u32[]{:S(2)}) collective-permute-start(bf16[8,162,128]{2,0,1:T(8,128)(2,1)S(1)} %copy.101), channel_id=1, source_target_pairs={{0,8},{8,0},{16,24},{24,16},{32,40},{40,32},{48,56},{56,48},{64,72... | collective-permute-start | bytes 995336 | tf_op jit(solution)/shard_map/ppermute | solution.py:548
  30.2 7.6 %collective-permute-start.6 = (bf16[192,128]{1,0:T(8,128)(2,1)S(1)}, bf16[192,128]{1,0:T(8,128)(2,1)S(1)}, u32[]{:S(2)}, u32[]{:S(2)}) collective-permute-start(bf16[192,128]{1,0:T(8,128)(2,1)S(1)} %get-tuple-element.37.own3), channel_id=1, source_target_pairs={{8,16},{24,32},{40,48},{56,64},{72,80},{88,96},{104,112},{120,128}... | collective-permute-start | bytes 147464 | tf_op jit(solution)/shard_map/ppermute | solution.py:544
  35.1 2.7 %collective-permute-start.5 = (bf16[192,128]{1,0:T(8,128)(2,1)S(1)}, bf16[192,128]{1,0:T(8,128)(2,1)S(1)}, u32[]{:S(2)}, u32[]{:S(2)}) collective-permute-start(bf16[192,128]{1,0:T(8,128)(2,1)S(1)} %get-tuple-element.37.own3), channel_id=1, source_target_pairs={{0,8},{8,0},{16,24},{24,16},{32,40},{40,32},{48,56},{56,48},{64,72... | collective-permute-start | bytes 147464 | tf_op jit(solution)/shard_map/ppermute | solution.py:544
  37.8 11.0 %copy-start.2 = (bf16[640,512]{1,0:T(8,128)(2,1)S(1)}, bf16[640,512]{1,0:T(8,128)(2,1)}, u32[]{:S(2)}) copy-start(bf16[640,512]{1,0:T(8,128)(2,1)} %constant.70.clone.planes_of) | copy-start | bytes 1966084
  37.8 11.0 %collective-permute-start.8 = (bf16[320,128]{1,0:T(8,128)(2,1)S(1)}, bf16[320,128]{1,0:T(8,128)(2,1)S(1)}, u32[]{:S(2)}, u32[]{:S(2)}) collective-permute-start(bf16[320,128]{1,0:T(8,128)(2,1)S(1)} %get-tuple-element.92), channel_id=1, source_target_pairs={{1,2},{3,4},{5,6},{2,1},{4,3},{6,5},{9,10},{11,12},{13,14},{10,9},... | collective-permute-start | bytes 245768 | tf_op jit(solution)/shard_map/ppermute | solution.py:544
  38.6 10.2 %collective-permute-start.7 = (bf16[320,128]{1,0:T(8,128)(2,1)S(1)}, bf16[320,128]{1,0:T(8,128)(2,1)S(1)}, u32[]{:S(2)}, u32[]{:S(2)}) collective-permute-start(bf16[320,128]{1,0:T(8,128)(2,1)S(1)} %get-tuple-element.93), channel_id=1, source_target_pairs={{0,1},{1,0},{2,3},{3,2},{4,5},{5,4},{6,7},{7,6},{8,9},{9,8},{10,11... | collective-permute-start | bytes 245768 | tf_op jit(solution)/shard_map/ppermute | solution.py:544
  42.9 5.9 %copy-start.3 = (bf16[256,768]{1,0:T(8,128)(2,1)S(1)}, bf16[256,768]{1,0:T(8,128)(2,1)}, u32[]{:S(2)}) copy-start(bf16[256,768]{1,0:T(8,128)(2,1)} %constant.71.clone.shift4) | copy-start | bytes 1179652
  42.9 5.9 %copy-start.7 = (bf16[256,128]{1,0:T(8,128)(2,1)S(1)}, bf16[256,128]{1,0:T(8,128)(2,1)}, u32[]{:S(2)}) copy-start(bf16[256,128]{1,0:T(8,128)(2,1)} %constant.69.clone.pool4) | copy-start | bytes 196612
  42.9 5.7 %collective-permute-start.10 = (bf16[192,128]{1,0:T(8,128)(2,1)S(1)}, bf16[192,128]{1,0:T(8,128)(2,1)S(1)}, u32[]{:S(2)}, u32[]{:S(2)}) collective-permute-start(bf16[192,128]{1,0:T(8,128)(2,1)S(1)} %pad_maximum_fusion.8), channel_id=1, source_target_pairs={{2,4},{3,5},{4,2},{5,3},{10,12},{11,13},{12,10},{13,11},{18,20},{1... | collective-permute-start | bytes 147464 | tf_op jit(solution)/shard_map/ppermute | solution.py:544
  43.7 5.1 %collective-permute-start.9 = (bf16[192,128]{1,0:T(8,128)(2,1)S(1)}, bf16[192,128]{1,0:T(8,128)(2,1)S(1)}, u32[]{:S(2)}, u32[]{:S(2)}) collective-permute-start(bf16[192,128]{1,0:T(8,128)(2,1)S(1)} %pad_maximum_fusion.8), channel_id=1, source_target_pairs={{0,2},{1,3},{2,0},{3,1},{4,6},{5,7},{6,4},{7,5},{8,10},{9,11},{10,... | collective-permute-start | bytes 147464 | tf_op jit(solution)/shard_map/ppermute | solution.py:544
  55.3 14.4 %copy-start.1 = (bf16[96,576]{1,0:T(8,128)(2,1)S(1)}, bf16[96,576]{1,0:T(8,128)(2,1)}, u32[]{:S(2)}) copy-start(bf16[96,576]{1,0:T(8,128)(2,1)} %reshape.95.w3b) | copy-start | bytes 331780
  55.3 14.4 %copy-start.4 = (bf16[256,384]{1,0:T(8,128)(2,1)S(1)}, bf16[256,384]{1,0:T(8,128)(2,1)}, u32[]{:S(2)}) copy-start(bf16[256,384]{1,0:T(8,128)(2,1)} %constant.74.clone.cross) | copy-start | bytes 589828
  55.3 14.4 %copy-start.5 = (bf16[128,384]{1,0:T(8,128)(2,1)S(1)}, bf16[128,384]{1,0:T(8,128)(2,1)}, u32[]{:S(2)}) copy-start(bf16[128,384]{1,0:T(8,128)(2,1)} %constant.73.clone.straight) | copy-start | bytes 294916
  55.3 14.4 %copy-start.6 = (bf16[128,256]{1,0:T(8,128)(2,1)S(1)}, bf16[128,256]{1,0:T(8,128)(2,1)}, u32[]{:S(2)}) copy-start(bf16[128,256]{1,0:T(8,128)(2,1)} %constant.75.clone.spread2) | copy-start | bytes 196612
  55.3 14.4 %copy-start.12 = (bf16[2,128,512]{2,1,0:T(8,128)(2,1)S(1)}, bf16[2,128,512]{2,1,0:T(8,128)(2,1)}, u32[]{:S(2)}) copy-start(bf16[2,128,512]{2,1,0:T(8,128)(2,1)} %get-tuple-element.49.sl2_mid) | copy-start | bytes 786436
  55.3 14.4 %copy-start.13 = (bf16[2,128,512]{2,1,0:T(8,128)(2,1)S(1)}, bf16[2,128,512]{2,1,0:T(8,128)(2,1)}, u32[]{:S(2)}) copy-start(bf16[2,128,512]{2,1,0:T(8,128)(2,1)} %get-tuple-element.50.sl2_edge) | copy-start | bytes 786436
  55.3 17.7 %all-to-all-start.1 = ((bf16[8,288,128]{2,1,0:T(8,128)(2,1)}), bf16[8,288,128]{2,1,0:T(8,128)(2,1)S(1)}, u32[]{:S(2)}, u32[]{:S(2)}) async-start(bf16[8,288,128]{2,1,0:T(8,128)(2,1)} %shard_map.196), calls=%async_computation.1 | async-start | bytes 1179648 | tf_op jit(solution)/shard_map/all_to_all | solution.py:707
  59.1 8.0 %collective-permute-start.11 = (bf16[64,768]{1,0:T(8,128)(2,1)S(1)}, bf16[64,768]{1,0:T(8,128)(2,1)S(1)}, u32[]{:S(2)}, u32[]{:S(2)}) collective-permute-start(bf16[64,768]{1,0:T(8,128)(2,1)S(1)} %get-tuple-element.46.near.own_near), channel_id=1, source_target_pairs={{0,8},{8,0},{16,24},{24,16},{32,40},{40,32},{48,56},{56,48},{64,72... | collective-permute-start | bytes 294920 | tf_op jit(solution)/shard_map/ppermute | solution.py:544
  61.9 7.8 %collective-permute-start.12 = (bf16[64,768]{1,0:T(8,128)(2,1)S(1)}, bf16[64,768]{1,0:T(8,128)(2,1)S(1)}, u32[]{:S(2)}, u32[]{:S(2)}) collective-permute-start(bf16[64,768]{1,0:T(8,128)(2,1)S(1)} %get-tuple-element.47.far.own_far), channel_id=1, source_target_pairs={{8,16},{24,32},{40,48},{56,64},{72,80},{88,96},{104,112},{120,128}... | collective-permute-start | bytes 294920 | tf_op jit(solution)/shard_map/ppermute | solution.py:544
  107.3 15.8 %all-to-all-start.4 = ((bf16[32,14,128]{2,1,0:T(8,128)(2,1)}), bf16[32,14,128]{2,1,0:T(8,128)(2,1)S(1)}, u32[]{:S(2)}, u32[]{:S(2)}) async-start(bf16[32,14,128]{2,1,0:T(8,128)(2,1)} %broadcast_in_dim.11), calls=%async_computation.4 | async-start | bytes 262144 | tf_op jit(solution)/shard_map/all_to_all | solution.py:554
